TPU v7x, 32 devices: a whole 2x2x4 slice. The times are simulated.
32 devices in a mesh: groups: 2 (over y), frame: 4 (over z), tok: 2 (over x), head: 2 (over core).
Axes of the slice: x: 2, y: 2, z: 4, core: 2. Of those that a mesh axis runs over, the one named last changes fastest.
Arguments:
- frames: bfloat16 [8, 1024, 1152], P(('groups', 'frame'), 'tok'), parts along dimension 0, may hold values from -6 to 6
- modulation: float32 [3, 1152], replicated, may hold values from -4.1 to 6, as said below
- w_qkv: bfloat16 [1152, 16, 3, 72], P('frame', 'head'), may hold values from -0.1875 to 0.1875
- w_out: bfloat16 [1152, 1152], P('head', 'frame'), may hold values from -0.1875 to 0.1875
- anchor_offsets: int32 [2], P('groups'), parts along dimension 0, may hold values from 0 to 3
Outputs:
- updated: bfloat16 [8, 1024, 1152], P(('groups', 'frame'), 'tok', 'head'), parts along dimension 0
There are 2 independent parts, one for each index of `groups`. A program takes and returns all parts, laid end to end along the dimension named above; an argument that names none is the same for every part. Nothing has to cross between parts.
Inputs may be any that keep to these rules, and one draw needn't show every extreme that they name: anchor_offsets[c] is the offset, within span c of 4 frames, of the frame that all frames of the span attend to. `modulation`: row 0 is the shift, row 1 the scale, row 2 the gate.
All inputs are finite; a program needn't handle non-finite values.
Results may differ from a plain program's by a relative error of at most 0.0049.
The roundings to bfloat16 on the way count: a program that leaves them out, or rounds other values in their place, can miss the bound.
Values may be sent and summed in bfloat16 or wider, within the bound.
No kernel may reach another device: no remote copies, remote signals or barrier semaphores. Data moves between devices by JAX's collectives and lax.ppermute only.
A program may use at most 64 MiB of HBM per device.

v0:
```python
import math

import jax
import jax.numpy as jnp
from jax import lax
from jax.sharding import PartitionSpec as P


def shifted(block, axis, distance):
    devices = range(lax.axis_size(axis))
    route = [(i - distance, i) for i in devices if i - distance in devices]
    return lax.ppermute(block, axis, route)


def from_partner(block, axis, stride):
    count = lax.axis_size(axis)
    route = []
    for low in range(count):
        high = low | 1 << stride
        if high != low and high < count:
            route += [(low, high), (high, low)]
    return lax.ppermute(block, axis, route)


def attend(queries, kv_all, first_frame, anchor, head_dim):
    frame_count, query_rows, query_width = queries.shape
    key_count = kv_all.shape[1]
    head_count = query_width // head_dim
    block_rows = math.gcd(512, query_rows)
    kv_heads = kv_all.reshape(frame_count + 2, key_count, head_count, 2, head_dim)
    global_idx = first_frame + 0
    use_prev = global_idx > 0
    use_anchor = (anchor != global_idx) & (anchor != global_idx - 1)
    valid_keys = jnp.concatenate(
        [
            jnp.broadcast_to(use_anchor, (key_count,)),
            jnp.broadcast_to(use_prev, (key_count,)),
            jnp.ones((key_count,), bool),
        ]
    )
    frame_queries = queries[0]

    def one_head(head_idx):
        picked = lax.dynamic_index_in_dim(kv_heads, head_idx, 2, keepdims=False)
        key_rows = jnp.concatenate(
            [picked[frame_count + 1, :, 0], picked[frame_count, :, 0], picked[0, :, 0]], 0
        )
        val_rows = jnp.concatenate(
            [picked[frame_count + 1, :, 1], picked[frame_count, :, 1], picked[0, :, 1]], 0
        )
        query_head = lax.dynamic_slice_in_dim(frame_queries, head_idx * head_dim, head_dim, 1)
        query_blocks = query_head.reshape(query_rows // block_rows, block_rows, head_dim)

        def one_block(query_block):
            scores = lax.dot_general(
                query_block, key_rows, (((1,), (1,)), ((), ())), preferred_element_type=jnp.float32
            ) * head_dim ** (-0.5)
            scores = jnp.where(valid_keys[None, :], scores, -1e30)
            row_max = jnp.max(scores, axis=-1, keepdims=True)
            probs = jnp.exp(scores - row_max)
            denominator = jnp.sum(probs, axis=-1, keepdims=True)
            numerator = jnp.dot(
                probs.astype(jnp.bfloat16), val_rows, preferred_element_type=jnp.float32
            )
            return (numerator / denominator).astype(jnp.bfloat16)

        return lax.map(one_block, query_blocks).reshape(query_rows, head_dim)

    per_head = lax.map(one_head, jnp.arange(head_count, dtype=jnp.int32))
    frame_outputs = [jnp.transpose(per_head, (1, 0, 2)).reshape(query_rows, head_count * head_dim)]
    return jnp.stack(frame_outputs)


def on_device(frames, modulation, w_qkv, w_out, anchor_offsets):
    frame_count, row_count, model_width = frames.shape
    head_local = w_qkv.shape[1]
    head_dim = w_qkv.shape[3]
    my_index = lax.axis_index("frame")
    flat_rows = frames.reshape(frame_count * row_count, model_width).astype(jnp.float32)
    row_mean = jnp.mean(flat_rows, axis=-1, keepdims=True)
    centred = flat_rows - row_mean
    row_var = jnp.mean(centred * centred, axis=-1, keepdims=True)
    normed = centred * lax.rsqrt(row_var + 1e-06)
    hidden = (normed * (1.0 + modulation[1]) + modulation[0]).astype(jnp.bfloat16)
    full_weight = lax.all_gather(w_qkv, "frame", axis=0, tiled=True)
    mixed = jnp.dot(
        hidden,
        full_weight.reshape(model_width, head_local * 3 * head_dim),
        preferred_element_type=jnp.float32,
    )
    mixed = mixed.astype(jnp.bfloat16).reshape(frame_count, row_count, head_local, 3, head_dim)
    queries = mixed[:, :, :, 0, :].reshape(frame_count, row_count, head_local * head_dim)
    keyvals = mixed[:, :, :, 1:, :].reshape(frame_count, row_count, head_local * 2 * head_dim)
    span_count = anchor_offsets.shape[0]
    total_frames = frame_count * lax.axis_size("frame")
    span_len = total_frames // span_count
    first_frame = my_index * frame_count
    mine_span = first_frame // span_len
    anchor = mine_span * span_len + anchor_offsets[mine_span]
    prev_kv = shifted(keyvals[frame_count - 1], "frame", 1)
    holder = anchor // frame_count
    anchor_kv = lax.dynamic_index_in_dim(keyvals, anchor % frame_count, 0, keepdims=False)
    levels = (span_len // frame_count).bit_length() - 1
    for bit_index in range(levels):
        partner = from_partner(anchor_kv, "frame", bit_index)
        take_partner = my_index >> bit_index & 1 != holder >> bit_index & 1
        anchor_kv = jnp.where(take_partner, partner, anchor_kv)
    kv_all = jnp.concatenate([keyvals, prev_kv[None], anchor_kv[None]], 0)
    kv_whole = lax.all_gather(kv_all, "tok", axis=1, tiled=True)
    attended = attend(queries, kv_whole, first_frame, anchor, head_dim)
    flat_attended = attended.reshape(frame_count * row_count, head_local * head_dim)
    term_cols = jnp.dot(
        flat_attended,
        lax.all_gather(w_out, "frame", axis=1, tiled=True),
        preferred_element_type=jnp.float32,
    )
    summed = lax.psum_scatter(term_cols, "head", scatter_dimension=1, tiled=True)
    half_width = summed.shape[1]
    col_start = lax.axis_index("head") * half_width
    residual_in = lax.dynamic_slice_in_dim(flat_rows, col_start, half_width, 1)
    gate_part = lax.dynamic_slice_in_dim(modulation[2], col_start, half_width, 0)
    result = (residual_in + gate_part * summed).astype(jnp.bfloat16)
    return result.reshape(frame_count, row_count, half_width)


def solution(mesh):
    placed = (
        P(("groups", "frame"), "tok", None),
        P(),
        P("frame", "head", None, None),
        P("head", "frame"),
        P("groups"),
    )
    return jax.shard_map(
        on_device,
        mesh=mesh,
        in_specs=placed,
        out_specs=P(("groups", "frame"), "tok", "head"),
        check_vma=False,
    )
```

profile of v0, /device:TPU:0, one launch (start us, length us, event | category | flops | bytes accessed | tf_op | source)
XLA Modules:
  0.0 446.1 jit_solution(5562761133376638567)
XLA Ops:
  6.5 3.9 copy.20
  10.5 0.2 convert_reduce_fusion
  10.8 0.5 fusion.36
  11.3 130.3 %all-gather.4.cloned.1.call-done = bf16[1152,8,3,72]{3,1,2,0:T(8,128)(2,1)} async-done(((bf16[288,8,3,72]{3,1,2,0:T(8,128)(2,1)}), bf16[1152,8,3,72]{3,1,2,0:T(8,128)(2,1)}) %all-gather.4.cloned.1.call-update) | async-done | bytes 3981328 | tf_op jit(solution)/shard_map/all_gather | solution.py:85
  141.5 9.3 %copy.21 = bf16[1152,8,3,72]{0,3,2,1:T(8,128)(2,1)} copy(bf16[1152,8,3,72]{3,1,2,0:T(8,128)(2,1)} %all-gather.4.cloned.1.call-done) | data formatting | bytes 7962624 | tf_op jit(solution)/shard_map/all_gather | solution.py:85
  150.9 4.8 %convolution_convert_fusion = bf16[512,1728]{0,1:T(8,128)(2,1)S(1)} fusion(bf16[1152,1728]{0,1:T(8,128)(2,1)} %bitcast.65, bf16[1,512,1152]{2,1,0:T(8,128)(2,1)S(1)} %copy-done, f32[1152]{0:T(1024)S(1)} %get-tuple-element.75, f32[1152]{0:T(1024)S(1)} %get-tuple-element.74, f32[512]{0:T(512)S(1)} %add_rsqrt_fusion, f32[512]{0:T(512)S(1)} %broadcast_multiply_fusion), kind=kOutput, calls=%fused_computation.36 | convolution fusion | flops 2042855424 | bytes 6943744 | tf_op jit(solution)/shard_map/dot_general | solution.py:86
  155.8 1.1 copy-done.1
  157.6 27.4 %collective-permute-done.1 = bf16[512,1152]{0,1:T(8,128)(2,1)} collective-permute-done((bf16[512,1152]{0,1:T(8,128)(2,1)S(1)}, bf16[512,1152]{0,1:T(8,128)(2,1)}, u32[]{:S(2)}, u32[]{:S(2)}) %collective-permute-start.1) | collective-permute-done | bytes 1179680 | tf_op jit(solution)/shard_map/ppermute | solution.py:22
  184.9 0.2 broadcast_select_fusion
  185.1 0.5 collective-permute-start.2
  185.6 4.6 %collective-permute-start = (bf16[512,1152]{0,1:T(8,128)(2,1)S(1)}, bf16[512,1152]{0,1:T(8,128)(2,1)}, u32[]{:S(2)}, u32[]{:S(2)}) collective-permute-start(bf16[512,1152]{0,1:T(8,128)(2,1)S(1)} %bitcast.63), channel_id=1, source_target_pairs={{0,4},{4,8},{8,12},{1,5},{5,9},{9,13},{2,6},{6,10},{10,14},{3,7},{... | collective-permute-start | bytes 3538952 | tf_op jit(solution)/shard_map/ppermute | solution.py:12
  190.2 48.4 %collective-permute-done.2 = bf16[512,1152]{0,1:T(8,128)(2,1)} collective-permute-done((bf16[512,1152]{0,1:T(8,128)(2,1)S(1)}, bf16[512,1152]{0,1:T(8,128)(2,1)}, u32[]{:S(2)}, u32[]{:S(2)}) %collective-permute-start.2) | collective-permute-done | bytes 1179680 | tf_op jit(solution)/shard_map/ppermute | solution.py:22
  238.6 1.4 select_bitcast_fusion
  240.0 3.0 pad_maximum_fusion
  243.1 0.7 all-gather.8.cloned.1.call-update
  243.9 1.1 slice.44
  245.0 109.2 %all-gather.6.cloned.1.call-done = bf16[3,1024,1152]{1,2,0:T(8,128)(2,1)} async-done(((bf16[3,512,1152]{1,2,0:T(8,128)(2,1)}), bf16[3,1024,1152]{1,2,0:T(8,128)(2,1)}) %all-gather.6.cloned.1.call-update) | async-done | bytes 7077904 | tf_op jit(solution)/shard_map/all_gather | solution.py:109
  354.2 69.1 %while.10 = (s32[]{:T(128)}, bf16[8,512,72]{1,2,0:T(8,128)(2,1)S(1)}, pred[3072]{0:T(1024)(128)(4,1)S(1)}, s32[8]{0:T(128)S(1)}, bf16[512,576]{0,1:T(8,128)(2,1)...) while((s32[]{:T(128)}, ...), condition=%wide.region_5.6_spmd, body=%wide.region_2.5_spmd.sunk | while | flops 473013248 | bytes 23465172 | solution.py:69
  354.2 0.6 dynamic_slice.40
  356.7 1.2 dynamic-slice_bitcast_fusion.2
  358.7 1.3 fusion.56
  359.9 1.4 fusion.57
  361.4 1.5 fusion.58
  362.9 0.6 dynamic_slice.40
  365.4 1.2 dynamic-slice_bitcast_fusion.2
  367.3 1.2 fusion.56
  368.6 1.4 fusion.57
  370.0 1.5 fusion.58
  371.5 0.6 dynamic_slice.40
  374.0 1.3 dynamic-slice_bitcast_fusion.2
  376.0 1.2 fusion.56
  377.2 1.4 fusion.57
  378.7 1.5 fusion.58
  380.1 0.6 dynamic_slice.40
  382.7 1.2 dynamic-slice_bitcast_fusion.2
  384.6 1.2 fusion.56
  385.9 1.4 fusion.57
  387.3 1.5 fusion.58
  388.8 0.6 dynamic_slice.40
  391.3 1.2 dynamic-slice_bitcast_fusion.2
  393.3 1.2 fusion.56
  394.5 1.4 fusion.57
  395.9 1.5 fusion.58
  397.4 0.6 dynamic_slice.40
  399.9 1.2 dynamic-slice_bitcast_fusion.2
  401.9 1.2 fusion.56
  403.2 1.4 fusion.57
  404.6 1.5 fusion.58
  406.1 0.6 dynamic_slice.40
  408.6 1.2 dynamic-slice_bitcast_fusion.2
  410.5 1.2 fusion.56
  411.8 1.4 fusion.57
  413.2 1.5 fusion.58
  414.7 0.6 dynamic_slice.40
  417.2 1.2 dynamic-slice_bitcast_fusion.2
  419.2 1.2 fusion.56
  420.4 1.4 fusion.57
  421.9 1.5 fusion.58
  423.4 3.9 fusion.45
  427.3 0.2 convert_element_type.27
  427.4 1.5 constant_dynamic-slice_fusion
  428.9 1.7 copy.19
  430.7 6.6 %reduce-scatter.2.cloned.1.call-done = f32[512,576]{0,1:T(8,128)} async-done(((f32[512,1152]{0,1:T(8,128)}), f32[512,576]{0,1:T(8,128)}) %reduce-scatter.2.cloned.1.call-update) | async-done | bytes 1179664 | tf_op jit(solution)/shard_map/reduce_scatter | solution.py:117
  437.3 2.3 fusion.44
  (34 shorter events, 1.0 us)
Async XLA Ops:
  6.5 135.0 %all-gather.4.cloned.1.call-start = ((), (), s32[]{:S(2)}) async-start(), calls=%async_computation.1 | async-start | bytes 8847360 | tf_op jit(solution)/shard_map/all_gather | solution.py:85
  6.5 4.0 copy-start
  10.5 0.8 copy-start.2
  10.5 343.7 %all-gather.6.cloned.1.call-start = ((), (), s32[]{:S(2)}) async-start(), calls=%async_computation.2 | async-start | bytes 10616832 | tf_op jit(solution)/shard_map/all_gather | solution.py:109
  155.7 1.2 copy-start.1
  156.9 28.0 %collective-permute-start.1 = (bf16[512,1152]{0,1:T(8,128)(2,1)S(1)}, bf16[512,1152]{0,1:T(8,128)(2,1)}, u32[]{:S(2)}, u32[]{:S(2)}) collective-permute-start(bf16[512,1152]{0,1:T(8,128)(2,1)S(1)} %bitcast.62), channel_id=1, source_target_pairs={{0,4},{4,0},{8,12},{12,8},{1,5},{5,1},{9,13},{13,9},{2,6},{6,2},{1... | collective-permute-start | bytes 3538952 | tf_op jit(solution)/shard_map/ppermute | solution.py:22
  185.1 53.4 %collective-permute-start.2 = (bf16[512,1152]{0,1:T(8,128)(2,1)S(1)}, bf16[512,1152]{0,1:T(8,128)(2,1)}, u32[]{:S(2)}, u32[]{:S(2)}) collective-permute-start(bf16[512,1152]{0,1:T(8,128)(2,1)S(1)} %broadcast_select_fusion), channel_id=1, source_target_pairs={{0,8},{8,0},{4,12},{12,4},{1,9},{9,1},{5,13},{13,5},{2,10},{10,2},... | collective-permute-start | bytes 3538952 | tf_op jit(solution)/shard_map/ppermute | solution.py:22
  185.6 54.4 %collective-permute-start = (bf16[512,1152]{0,1:T(8,128)(2,1)S(1)}, bf16[512,1152]{0,1:T(8,128)(2,1)}, u32[]{:S(2)}, u32[]{:S(2)}) collective-permute-start(bf16[512,1152]{0,1:T(8,128)(2,1)S(1)} %bitcast.63), channel_id=1, source_target_pairs={{0,4},{4,8},{8,12},{1,5},{5,9},{9,13},{2,6},{6,10},{10,14},{3,7},{... | collective-permute-start | bytes 3538952 | tf_op jit(solution)/shard_map/ppermute | solution.py:12
  243.0 180.3 %all-gather.8.cloned.1.call-start = ((), (), s32[]{:S(2)}) async-start(), calls=%async_computation.3 | async-start | bytes 1843200 | tf_op jit(solution)/shard_map/all_gather | solution.py:114
  243.8 193.6 %reduce-scatter.2.cloned.1.call-start = ((), (), s32[]{:S(2)}) async-start(), calls=%async_computation.4 | async-start | bytes 3538944 | tf_op jit(solution)/shard_map/reduce_scatter | solution.py:117
Sparse Core Ops, SparseCore 0:
  10.6 130.8 all-gather.3
  243.2 111.0 all-gather.5
  355.8 35.4 all-gather.7
  427.4 9.8 reduce-scatter.1
where the time goes:
time: 447 us; the launch traced here: 446 us
  waiting for transfers between devices  323 us (72%)
  local copies, waits for them, and re-layouts  34.2 us (8%)
  matrix products  30.4 us (7%)
  loops' own time  20.6 us (5%)
  other arithmetic  19.2 us (4%)
  between operations  14 us (3%)
  starting transfers between devices  5.15 us (1%)
    all_gather x1, waiting for transfers between devices, on_device(): full_weight = lax.all_gather(w_qkv, 'frame', axis=0, tiled=True)  130 us
    all_gather x1, waiting for transfers between devices, on_device(): kv_whole = lax.all_gather(kv_all, 'tok', axis=1, tiled=True)  109 us
    ppermute x2, waiting for transfers between devices, from_partner(): return lax.ppermute(block, axis, route)  75.8 us
    another operation x1, loops' own time, attend(): per_head = lax.map(one_head, jnp.arange(head_count, dtype=jnp.int32))  20.6 us
    dot_general x8, matrix products, one_block(): jnp.dot(probs.astype(jnp.bfloat16), val_rows, preferred_element_type=jnp....  11.8 us
    reduce_sum x8, other arithmetic, one_block(): denominator = jnp.sum(probs, axis=-1, keepdims=True)  11.4 us
    dot_general x8, matrix products, one_block(): lax.dot_general(query_block, key_rows, (((1,), (1,)), ((), ())), preferre...  10 us
    squeeze x8, local copies, waits for them, and re-layouts, one_head(): picked = lax.dynamic_index_in_dim(kv_heads, head_idx, 2, keepdims=False)  9.88 us
  transfers between devices with their start and end apart: 7, of which 5 were waited for; matrix products, arithmetic and copies ran while one was open for 12% of the time, Pallas kernels for 0%

commit v1 on v0

--- a/solution.py
+++ b/solution.py
@@ -1,9 +1,200 @@
+import functools
 import math
 
 import jax
 import jax.numpy as jnp
 from jax import lax
+from jax.experimental import pallas as pl
+from jax.experimental.pallas import tpu as pltpu
 from jax.sharding import PartitionSpec as P
+
+VMEM_LIMIT = 56 * 2**20
+
+
+def dot_nn(a, b):
+    return lax.dot_general(a, b, (((1,), (0,)), ((), ())), preferred_element_type=jnp.float32)
+
+
+def dot_nt(a, b):
+    return lax.dot_general(a, b, (((1,), (1,)), ((), ())), preferred_element_type=jnp.float32)
+
+
+def call(kernel, out_shape, operands, scratch=(), flops=0, moved=0):
+    smem = pl.BlockSpec(memory_space=pltpu.SMEM)
+    vmem = pl.BlockSpec(memory_space=pltpu.VMEM)
+    many = isinstance(out_shape, (list, tuple))
+    return pl.pallas_call(
+        kernel,
+        out_shape=out_shape,
+        in_specs=[smem if x.dtype == jnp.int32 else vmem for x in operands],
+        out_specs=[vmem] * len(out_shape) if many else vmem,
+        scratch_shapes=list(scratch),
+        compiler_params=pltpu.CompilerParams(vmem_limit_bytes=VMEM_LIMIT),
+        cost_estimate=pl.CostEstimate(flops=flops, bytes_accessed=moved, transcendentals=0),
+    )(*operands)
+
+
+def project_kernel(kv_width, place_ref, mine_ref, other_ref, mod_ref, weight_ref, kv_ref, q_ref, hidden):
+    half = mine_ref.shape[0]
+    for part, ref in ((place_ref[0], mine_ref), (1 - place_ref[0], other_ref)):
+        values = ref[...].astype(jnp.float32)
+        row_mean = jnp.mean(values, axis=-1, keepdims=True)
+        centred = values - row_mean
+        row_var = jnp.mean(centred * centred, axis=-1, keepdims=True)
+        normed = centred * lax.rsqrt(row_var + 1e-06)
+        normed = normed * (1.0 + mod_ref[1:2, :]) + mod_ref[0:1, :]
+        hidden[pl.ds(pl.multiple_of(part * half, half), half), :] = normed.astype(jnp.bfloat16)
+    mixed = dot_nt(weight_ref[...], hidden[...]).astype(jnp.bfloat16)
+    kv_ref[...] = mixed[:kv_width]
+    q_ref[...] = mixed[kv_width:]
+
+
+def project(place, mine, other, modulation, weight, kv_width):
+    half, width = mine.shape
+    rows = 2 * half
+    out_width = weight.shape[0]
+    return call(
+        functools.partial(project_kernel, kv_width),
+        (
+            jax.ShapeDtypeStruct((kv_width, rows), jnp.bfloat16),
+            jax.ShapeDtypeStruct((out_width - kv_width, rows), jnp.bfloat16),
+        ),
+        (place, mine, other, modulation, weight),
+        [pltpu.VMEM((rows, width), jnp.bfloat16)],
+        flops=2 * rows * width * out_width,
+        moved=2 * (rows * width + width * out_width + rows * out_width),
+    )
+
+
+def attend_kernel(count, heads, head_dim, *refs):
+    ids_ref = refs[0]
+    q_refs = refs[1 : 1 + count]
+    near_refs = refs[1 + count : 1 + 2 * count]
+    far_refs = refs[1 + 2 * count : 1 + 3 * count]
+    out_ref = refs[1 + 3 * count]
+    (q_all, k_all, v_all, even_scores, odd_scores, high, block_high, scale_old, total, q_list, k_list) = refs[2 + 3 * count :]
+    rows = q_refs[0].shape[1]
+    factor = math.log2(math.e) / math.sqrt(head_dim)
+    value_rows = v_all.shape[1]
+    ones = jnp.ones((value_rows - head_dim, rows), jnp.float32)
+    for slot in range(count):
+        frame = ids_ref[slot]
+        queries = q_refs[slot][...].astype(jnp.float32)
+        for head in range(heads):
+            q_all[frame * heads + head] = queries[head * head_dim : (head + 1) * head_dim].astype(jnp.bfloat16)
+        for side, ref in ((0, near_refs[slot]), (1, far_refs[slot])):
+            keyvals = ref[...].astype(jnp.float32)
+            span = pl.ds(side * rows, rows)
+            for head in range(heads):
+                keys = keyvals[head * head_dim : (head + 1) * head_dim]
+                k_all[frame * heads + head, span, :] = keys.T.astype(jnp.bfloat16)
+                first = (heads + head) * head_dim
+                values = jnp.concatenate([keyvals[first : first + head_dim], ones], 0)
+                v_all[frame * heads + head, :, span] = values.astype(jnp.bfloat16)
+    anchor = ids_ref[count]
+    items = jnp.int32(0)
+    for frame in range(count):
+        q_list[items] = frame
+        k_list[items] = frame
+        items += 1
+        if frame > 0:
+            q_list[items] = frame
+            k_list[items] = frame - 1
+            items += 1
+        q_list[items] = frame
+        k_list[items] = anchor
+        items += jnp.where((anchor != frame) & (anchor != frame - 1), 1, 0)
+    high[...] = jnp.full_like(high, -1e30)
+    total[...] = jnp.zeros_like(total)
+    scores_of = (even_scores, odd_scores)
+    spare = count * heads
+    key_rows = 2 * rows
+    step = math.gcd(key_rows, 256)
+
+    def stage(head_a, item_a, live_a, head_b, item_b, live_b):
+        slot_a = q_list[item_a] * heads + head_a
+        state_a = jnp.where(live_a, slot_a, spare)
+        key_a = k_list[item_a] * heads + head_a
+        state_b = jnp.where(live_b, q_list[item_b] * heads + head_b, spare)
+        key_b = k_list[item_b] * heads + head_b
+        queries = q_all[slot_a]
+        top_b = block_high[head_b]
+        running = total[state_b] * scale_old[head_b]
+        old = high[state_a]
+        top = old
+        for start in range(0, key_rows, step):
+            part = pl.ds(start, step)
+            scores = dot_nn(k_all[key_a, part, :], queries)
+            scores_of[head_a][part, :] = scores
+            top = jnp.maximum(top, jnp.max(scores, axis=0, keepdims=True))
+            probs = jnp.exp2((scores_of[head_b][part, :] - top_b) * factor).astype(jnp.bfloat16)
+            running = running + dot_nn(v_all[key_b, :, part], probs)
+        total[state_b] = running
+        scale_old[head_a] = jnp.exp2((old - top) * factor)
+        block_high[head_a] = top
+        high[state_a] = top
+
+    def body(index, carry):
+        now = jnp.minimum(index, items - 1)
+        before = jnp.maximum(index - 1, 0)
+        stage(0, now, index < items, 1, before, index > 0)
+        stage(1, now, index < items, 0, now, index < items)
+        return carry
+
+    lax.fori_loop(0, items + 1, body, 0)
+    for frame in range(count):
+        parts = []
+        for head in range(heads):
+            sums = total[frame * heads + head]
+            parts.append(sums[:head_dim] / sums[head_dim : head_dim + 1])
+        out_ref[frame] = jnp.concatenate(parts, 0).astype(jnp.bfloat16)
+
+
+def attend_all(ids, queries, near, far, heads, head_dim):
+    count = len(queries)
+    rows = queries[0].shape[1]
+    value_rows = head_dim + 8
+    states = count * heads + 1
+    return call(
+        functools.partial(attend_kernel, count, heads, head_dim),
+        jax.ShapeDtypeStruct((count, heads * head_dim, rows), jnp.bfloat16),
+        (ids, *queries, *near, *far),
+        [
+            pltpu.VMEM((count * heads, head_dim, rows), jnp.bfloat16),
+            pltpu.VMEM((count * heads, 2 * rows, head_dim), jnp.bfloat16),
+            pltpu.VMEM((count * heads, value_rows, 2 * rows), jnp.bfloat16),
+            pltpu.VMEM((2 * rows, rows), jnp.float32),
+            pltpu.VMEM((2 * rows, rows), jnp.float32),
+            pltpu.VMEM((states, 1, rows), jnp.float32),
+            pltpu.VMEM((heads, 1, rows), jnp.float32),
+            pltpu.VMEM((heads, 1, rows), jnp.float32),
+            pltpu.VMEM((states, value_rows, rows), jnp.float32),
+            pltpu.SMEM((3 * count + 1,), jnp.int32),
+            pltpu.SMEM((3 * count + 1,), jnp.int32),
+        ],
+        flops=3 * count * heads * rows * 2 * rows * head_dim * 4,
+        moved=2 * count * heads * head_dim * rows * 6,
+    )
+
+
+def finish_kernel(near_w, far_w, near_ref, far_ref, frame_ref, gate_ref, out_ref):
+    projected = dot_nn(near_w[...], near_ref[...]) + dot_nn(far_w[...], far_ref[...])
+    updated = frame_ref[...].astype(jnp.float32) + gate_ref[...] * projected
+    out_ref[...] = updated.astype(jnp.bfloat16)
+
+
+def finish(near_w, far_w, near, far, frame_part, gate_part):
+    return call(
+        finish_kernel,
+        jax.ShapeDtypeStruct(frame_part.shape, jnp.bfloat16),
+        (near_w, far_w, near, far, frame_part, gate_part),
+        flops=4 * near_w.shape[0] * near_w.shape[1] * near.shape[1],
+        moved=4 * (near_w.size + near.size + frame_part.size),
+    )
+
+
+def swapped(block, axis):
+    return lax.ppermute(block, axis, [(0, 1), (1, 0)])
 
 
 def shifted(block, axis, distance):
@@ -71,7 +262,7 @@
     return jnp.stack(frame_outputs)
 
 
-def on_device(frames, modulation, w_qkv, w_out, anchor_offsets):
+def by_frames(frames, modulation, w_qkv, w_out, anchor_offsets):
     frame_count, row_count, model_width = frames.shape
     head_local = w_qkv.shape[1]
     head_dim = w_qkv.shape[3]
@@ -123,6 +314,102 @@
     return result.reshape(frame_count, row_count, half_width)
 
 
+def line_gather(block, axis):
+    count = lax.axis_size(axis)
+    me = lax.axis_index(axis)
+    middle = count // 2
+    right, left, both = {}, {}, {}
+    for d in range(1, middle):
+        right[d] = lax.ppermute(block, axis, [(i, i + d) for i in range(count - d)])
+        left[d] = lax.ppermute(block, axis, [(i + d, i) for i in range(count - d)])
+    both[middle] = lax.ppermute(block, axis, [(i, i ^ middle) for i in range(count)])
+    for d in range(middle + 1, count):
+        route = [(i + d - 1, i + d) for i in range(count - d)] + [(i - d + 1, i - d) for i in range(d, count)]
+        both[d] = lax.ppermute(both[d - 1], axis, route)
+    found = []
+    for d in range(1, middle):
+        found.append((jnp.where(me >= d, me - d, me + d), jnp.where(me >= d, right[d], left[d])))
+    found.append((me ^ middle, both[middle]))
+    for d in range(1, middle):
+        e = count - d
+        inner = (me >= d) & (me < e)
+        index = jnp.where(me < d, me + e, jnp.where(me >= e, me - e, me + d))
+        found.append((index, jnp.where(inner, left[d], both[e])))
+    return found
+
+
+def by_heads(frames, modulation, w_qkv, w_out, anchor_offsets):
+    _, rows, width = frames.shape
+    share, head_local, _, head_dim = w_qkv.shape
+    count = lax.axis_size("frame")
+    heads = head_local // count
+    core = lax.axis_index("head")
+    me = lax.axis_index("frame")
+    frame = frames[0]
+    half = rows // 2
+    mine = lax.dynamic_slice_in_dim(frame, core * half, half, 0)
+    found = line_gather(mine, "frame")
+
+    blocks = jnp.transpose(w_qkv, (1, 2, 3, 0)).reshape(count, heads, 3 * head_dim, share)
+    group_count = lax.axis_size("groups")
+    if group_count == 2 and heads == 2:
+        group = lax.axis_index("groups")
+        part = lax.dynamic_index_in_dim(blocks, group, 1, keepdims=False)
+        part = lax.all_to_all(part, "frame", 0, 0)
+        partner = swapped(part, "groups")
+        per_head = [jnp.where(group == 0, part, partner), jnp.where(group == 0, partner, part)]
+    else:
+        whole = lax.all_to_all(blocks, "frame", 0, 0)
+        per_head = [whole[:, h] for h in range(heads)]
+    per_head = [jnp.transpose(w, (1, 0, 2)).reshape(3, head_dim, width) for w in per_head]
+    weight = jnp.concatenate([w[kind] for kind in (1, 2, 0) for w in per_head], 0)
+    kv_width = 2 * heads * head_dim
+
+    queries, near, far, ids = [], [], [], []
+    zero = jnp.zeros((1,), jnp.int32)
+    place = core.reshape(1).astype(jnp.int32)
+    for index, block in [(me, None)] + found:
+        if block is None:
+            kv, q = project(zero, frame[:half], frame[half:], modulation, weight, kv_width)
+        else:
+            kv, q = project(place, block, swapped(block, "head"), modulation, weight, kv_width)
+        ids.append(index)
+        queries.append(q)
+        near.append(kv)
+        far.append(swapped(kv, "tok"))
+    ids = jnp.stack(ids + [anchor_offsets[0]]).astype(jnp.int32)
+    attended = attend_all(ids, queries, near, far, heads, head_dim)
+    arrived = lax.all_to_all(attended, "frame", 0, 0).reshape(count * heads * head_dim, rows)
+    arrived_far = swapped(arrived, "head")
+
+    out_half = width // 2
+    w_cols = lax.all_gather(w_out.T, "frame", axis=0, tiled=True)
+    near_w = lax.dynamic_slice_in_dim(w_cols, core * out_half, out_half, 0)
+    far_w = swapped(lax.dynamic_slice_in_dim(w_cols, (1 - core) * out_half, out_half, 0), "head")
+    frame_part = lax.dynamic_slice_in_dim(frame, core * out_half, out_half, 1).T
+    gate_part = lax.dynamic_slice_in_dim(modulation[2], core * out_half, out_half, 0)[:, None]
+    updated = finish(near_w, far_w, arrived, arrived_far, frame_part, gate_part)
+    return updated.T[None]
+
+
+def on_device(frames, modulation, w_qkv, w_out, anchor_offsets):
+    count = lax.axis_size("frame")
+    fits = (
+        frames.shape[0] == 1
+        and anchor_offsets.shape[0] == 1
+        and count >= 2
+        and count & (count - 1) == 0
+        and lax.axis_size("head") == 2
+        and lax.axis_size("tok") == 2
+        and w_qkv.shape[1] % count == 0
+        and w_qkv.shape[3] % 8 == 0
+        and frames.shape[1] % 256 == 0
+        and frames.shape[2] % 32 == 0
+    )
+    step = by_heads if fits else by_frames
+    return step(frames, modulation, w_qkv, w_out, anchor_offsets)
+
+
 def solution(mesh):
     placed = (
         P(("groups", "frame"), "tok", None),

time: 447 us -> 196 us (0.44)
  waiting for transfers between devices: 323 us -> 86 us
  Pallas kernels: 0 us -> 39.1 us
  matrix products: 30.4 us -> 0 us
  loops' own time: 20.6 us -> 0 us
  starting transfers between devices: 5.15 us -> 24.7 us
  other arithmetic: 19.2 us -> 1.5 us
    all_gather x3 -> x1, waiting for transfers between devices: 239 us -> 0.02 us  [by_heads(): w_cols = lax.all_gather(w_out.T, 'frame', axis=0, tiled=True)]
    pallas_call x0 -> x6, Pallas kernels: none -> 39.1 us  [call(): pl.pallas_call(kernel, out_shape=out_shape, in_specs=[smem if x.dtype ==...]
    dot_general x18 -> x0, matrix products: 30.4 us -> none  [the longest x8 11.8 us: one_block(): jnp.dot(probs.astype(jnp.bfloat16), val_rows, preferred_element_type=jnp....]
    another operation x1 -> x0, loops' own time: 20.6 us -> none  [attend(): per_head = lax.map(one_head, jnp.arange(head_count, dtype=jnp.int32))]
    all_to_all x0 -> x2, waiting for transfers between devices: none -> 17.8 us  [the longest x1 13 us: by_heads(): lax.all_to_all(attended, 'frame', 0, 0)]
    reduce_sum x10 -> x0, other arithmetic: 12.1 us -> none  [the longest x8 11.4 us: one_block(): denominator = jnp.sum(probs, axis=-1, keepdims=True)]
    ppermute x3 -> x14, starting transfers between devices: 5.03 us -> 17 us  [the longest x10 6.52 us: swapped(): return lax.ppermute(block, axis, [(0, 1), (1, 0)])]
    all_gather x1 -> x0, local copies, waits for them, and re-layouts: 9.34 us -> none  [on_device(): full_weight = lax.all_gather(w_qkv, 'frame', axis=0, tiled=True)]
  transfers between devices with their start and end apart: 7 -> 17, of which waited for: 5 -> 7; matrix products, arithmetic and copies ran while one was open for 12% -> 13% of each run, Pallas kernels for 0% -> 18%
where the time goes in v1:
time: 196 us; the launch traced here: 195 us
  waiting for transfers between devices  86 us (44%)
  Pallas kernels  39.1 us (20%)
  local copies, waits for them, and re-layouts  29.8 us (15%)
  starting transfers between devices  24.7 us (13%)
  between operations  14.3 us (7%)
    pallas_call x6, Pallas kernels, call(): pl.pallas_call(kernel, out_shape=out_shape, in_specs=[smem if x.dtype ==...  39.1 us
    ppermute x1, waiting for transfers between devices, line_gather(): both[d] = lax.ppermute(both[d - 1], axis, route)  31.3 us
    ppermute x1, waiting for transfers between devices, line_gather(): lax.ppermute(block, axis, [(i, i ^ middle) for i in range(count)])  23.6 us
    all_to_all x1, waiting for transfers between devices, by_heads(): lax.all_to_all(attended, 'frame', 0, 0)  13 us
    ppermute x10, waiting for transfers between devices, swapped(): return lax.ppermute(block, axis, [(0, 1), (1, 0)])  10.4 us
    squeeze x6, local copies, waits for them, and re-layouts, by_heads(): w[kind]  9.74 us
    unnamed x28, local copies, waits for them, and re-layouts  8.27 us
    ppermute x10, starting transfers between devices, swapped(): return lax.ppermute(block, axis, [(0, 1), (1, 0)])  6.52 us
  transfers between devices with their start and end apart: 17, of which 7 were waited for; matrix products, arithmetic and copies ran while one was open for 13% of the time, Pallas kernels for 18%

profile of v1, /device:TPU:0, one launch (start us, length us, event | category | flops | bytes accessed | tf_op | source)
XLA Modules:
  0.0 195.3 jit_solution(14868074792682495437)
XLA Ops:
  6.5 2.8 %dynamic-slice_bitcast_fusion = (bf16[256,1152]{1,0:T(8,128)(2,1)}, bf16[256,1152]{1,0:T(8,128)(2,1)}, bf16[256,1152]{1,0:T(8,128)(2,1)}) fusion(bf16[1,512,1152]{2,1,0:T(8,128)(2,1)} %param.5, s32[]{:T(128)S(6)} %select_n.61), kind=kLoop, calls=%fused_computation | loop fusion | bytes 3538948 | tf_op jit(solution)/shard_map/dynamic_slice | solution.py:350
  9.3 4.0 %collective-permute-start.5 = (bf16[256,1152]{1,0:T(8,128)(2,1)}, bf16[256,1152]{1,0:T(8,128)(2,1)}, u32[]{:S(2)}, u32[]{:S(2)}) collective-permute-start(bf16[256,1152]{1,0:T(8,128)(2,1)} %get-tuple-element.23), channel_id=1, source_target_pairs={{0,8},{4,12},{8,0},{12,4},{1,9},{5,13},{9,1},{13,5},{2,10},{6,14},... | collective-permute-start | bytes 1769480 | tf_op jit(solution)/shard_map/ppermute | solution.py:325
  13.4 0.1 constant_dynamic-slice_fusion.1
  13.4 1.1 copy.26
  14.5 3.5 %all-to-all-start = ((bf16[4,216,288]{1,2,0:T(8,128)(2,1)}), bf16[4,216,288]{1,2,0:T(8,128)(2,1)S(1)}, u32[]{:S(2)}, u32[]{:S(2)}) async-start(bf16[4,216,288]{1,2,0:T(8,128)(2,1)} %bitcast.9), calls=%async_computation | async-start | bytes 1179648 | tf_op jit(solution)/shard_map/all_to_all | solution.py:358
  18.0 0.0 all-gather.2.cloned.1.call-start
  18.1 3.9 %collective-permute-start.2 = (bf16[256,1152]{1,0:T(8,128)(2,1)}, bf16[256,1152]{1,0:T(8,128)(2,1)S(1)}, u32[]{:S(2)}, u32[]{:S(2)}) collective-permute-start(bf16[256,1152]{1,0:T(8,128)(2,1)} %get-tuple-element.23), channel_id=1, source_target_pairs={{0,4},{4,8},{8,12},{1,5},{5,9},{9,13},{2,6},{6,10},{10,14},{3,7},{... | collective-permute-start | bytes 1769480 | tf_op jit(solution)/shard_map/ppermute | solution.py:323
  21.9 1.3 collective-permute-start.3
  23.2 23.6 %collective-permute-done.5.mine_ref = bf16[256,1152]{1,0:T(8,128)(2,1)} collective-permute-done((bf16[256,1152]{1,0:T(8,128)(2,1)}, bf16[256,1152]{1,0:T(8,128)(2,1)}, u32[]{:S(2)}, u32[]{:S(2)}) %collective-permute-start.5) | collective-permute-done | bytes 589856 | tf_op jit(solution)/shard_map/ppermute | solution.py:325
  46.9 1.3 collective-permute-start.7
  48.2 0.0 all-gather.2.cloned.1.call-update
  48.2 0.1 collective-permute-start.6
  48.3 4.8 %all-to-all-done = bf16[4,216,288]{1,2,0:T(8,128)(2,1)S(1)} async-done(((bf16[4,216,288]{1,2,0:T(8,128)(2,1)}), bf16[4,216,288]{1,2,0:T(8,128)(2,1)S(1)}, u32[]{:S(2)}, u32[]{:S(2)}) %all-to-all-start) | async-done | bytes 497696 | tf_op jit(solution)/shard_map/all_to_all | solution.py:358
  53.1 1.8 collective-permute-start.1
  55.0 2.8 %collective-permute-done.3 = bf16[256,1152]{1,0:T(8,128)(2,1)S(1)} collective-permute-done((bf16[256,1152]{1,0:T(8,128)(2,1)}, bf16[256,1152]{1,0:T(8,128)(2,1)S(1)}, u32[]{:S(2)}, u32[]{:S(2)}) %collective-permute-start.3) | collective-permute-done | bytes 589856 | tf_op jit(solution)/shard_map/ppermute | solution.py:324
  57.8 0.8 copy-done.6
  58.6 31.3 %collective-permute-done.7 = bf16[256,1152]{1,0:T(8,128)(2,1)} collective-permute-done((bf16[256,1152]{1,0:T(8,128)(2,1)}, bf16[256,1152]{1,0:T(8,128)(2,1)}, u32[]{:S(2)}, u32[]{:S(2)}) %collective-permute-start.7) | collective-permute-done | bytes 589856 | tf_op jit(solution)/shard_map/ppermute | solution.py:328
  89.9 1.4 broadcast_select_fusion
  91.2 0.0 copy-start.3
  91.2 0.1 collective-permute-start.8
  91.3 0.5 collective-permute-start.4
  91.8 0.0 collective-permute-done.1
  91.8 0.1 select_bitcast_fusion
  92.0 1.6 fusion
  93.5 0.8 copy.20
  94.4 0.9 constant_dynamic-update-slice_fusion.5
  95.3 1.8 copy.21
  97.1 1.8 copy.22
  98.8 1.8 copy.23
  100.6 0.9 constant_dynamic-update-slice_fusion.4
  101.6 0.9 constant_dynamic-update-slice_fusion.3
  102.5 0.9 constant_dynamic-update-slice_fusion.2
  103.5 1.8 copy.24
  105.2 1.8 copy.25
  107.0 0.9 constant_dynamic-update-slice_fusion.1
  108.0 0.9 constant_dynamic-update-slice_fusion.weight_ref
  108.9 0.9 copy-done.1
  109.9 4.1 %shard_map.57 = (bf16[288,512]{1,0:T(8,128)(2,1)}, bf16[144,512]{1,0:T(8,128)(2,1)}) custom-call(s32[1]{0:T(128)} %bitcast.18.place_ref, bf16[256,1152]{1,0:T(8,128)(2,1)} %collective-permute-done.5.mine_ref, bf16[256,1152]{1,0:T(8,128)(2,1)} %collective-permute-done.6.other_ref, f32[3,1152]{1,0:T(4,128)} %mod_ref.7, bf16[432,1152]{1,0:T(8,128)(2,1)} %copy-done.1), custom_call_target="tpu_custom_call" | custom-call | flops 509607936 | bytes 2617344 | tf_op jit(solution)/shard_map/pallas_call | solution.py:26
  114.0 1.6 collective-permute-start.11
  115.6 4.1 %shard_map.55 = (bf16[288,512]{1,0:T(8,128)(2,1)}, bf16[144,512]{1,0:T(8,128)(2,1)}) custom-call(s32[1]{0:T(128)} %constant.38.clone.1.place_ref, bf16[256,1152]{1,0:T(8,128)(2,1)} %get-tuple-element.25.mine_ref, bf16[256,1152]{1,0:T(8,128)(2,1)} %get-tuple-element.24.other_ref, f32[3,1152]{1,0:T(4,128)} %mod_ref.7, bf16[432,1152]{1,0:T(8,128)(2,1)} %copy-done.1), custom_call_target="tpu_custom_call" | custom-call | flops 509607936 | bytes 2617344 | tf_op jit(solution)/shard_map/pallas_call | solution.py:26
  119.7 0.4 collective-permute-start.9
  120.1 4.1 %shard_map.58 = (bf16[288,512]{1,0:T(8,128)(2,1)}, bf16[144,512]{1,0:T(8,128)(2,1)}) custom-call(s32[1]{0:T(128)} %bitcast.18.place_ref, bf16[256,1152]{1,0:T(8,128)(2,1)} %copy-done.4, bf16[256,1152]{1,0:T(8,128)(2,1)} %collective-permute-done.8.other_ref, f32[3,1152]{1,0:T(4,128)} %mod_ref.7, bf16[432,1152]{1,0:T(8,128)(2,1)} %copy-done.1), custom_call_target="tpu_custom_call" | custom-call | flops 509607936 | bytes 2617344 | tf_op jit(solution)/shard_map/pallas_call | solution.py:26
  124.2 1.6 collective-permute-start.12
  125.9 4.1 %shard_map.56 = (bf16[288,512]{1,0:T(8,128)(2,1)}, bf16[144,512]{1,0:T(8,128)(2,1)}) custom-call(s32[1]{0:T(128)} %bitcast.18.place_ref, bf16[256,1152]{1,0:T(8,128)(2,1)} %copy-done.3, bf16[256,1152]{1,0:T(8,128)(2,1)} %collective-permute-done.4.other_ref, f32[3,1152]{1,0:T(4,128)} %mod_ref.7, bf16[432,1152]{1,0:T(8,128)(2,1)} %copy-done.1), custom_call_target="tpu_custom_call" | custom-call | flops 509607936 | bytes 2617344 | tf_op jit(solution)/shard_map/pallas_call | solution.py:26
  130.0 0.4 collective-permute-start.10
  131.1 0.6 stack.19.refs_0_
  131.7 4.9 %collective-permute-done.12.refs_12_ = bf16[288,512]{1,0:T(8,128)(2,1)S(1)} collective-permute-done((bf16[288,512]{1,0:T(8,128)(2,1)}, bf16[288,512]{1,0:T(8,128)(2,1)S(1)}, u32[]{:S(2)}, u32[]{:S(2)}) %collective-permute-start.12) | collective-permute-done | bytes 294944 | tf_op jit(solution)/shard_map/ppermute | solution.py:197
  136.6 5.5 %collective-permute-done.10.refs_10_ = bf16[288,512]{1,0:T(8,128)(2,1)S(1)} collective-permute-done((bf16[288,512]{1,0:T(8,128)(2,1)}, bf16[288,512]{1,0:T(8,128)(2,1)S(1)}, u32[]{:S(2)}, u32[]{:S(2)}) %collective-permute-start.10) | collective-permute-done | bytes 294944 | tf_op jit(solution)/shard_map/ppermute | solution.py:197
  142.1 0.7 copy-done.10
  142.8 18.7 %shard_map.59 = bf16[4,144,512]{2,1,0:T(8,128)(2,1)} custom-call(s32[5]{0:T(128)} %stack.19.refs_0_, bf16[144,512]{1,0:T(8,128)(2,1)} %get-tuple-element.13.refs_1_, bf16[144,512]{1,0:T(8,128)(2,1)} %get-tuple-element.14.refs_2_, bf16[144,512]{1,0:T(8,128)(2,1)} %get-tuple-element.15.refs_3_, bf16[144,512]{1,0:T(8,128)(2,1)} %get-tuple-element.16.refs_4_, ...), custom_call_target="tpu_custom_call" | custom-call | flops 3623878656 | bytes 3538944 | tf_op jit(solution)/shard_map/pallas_call | solution.py:26
  161.6 4.2 %all-to-all-start.1 = ((bf16[4,144,512]{2,1,0:T(8,128)(2,1)}), bf16[4,144,512]{2,1,0:T(8,128)(2,1)}, u32[]{:S(2)}, u32[]{:S(2)}) async-start(bf16[4,144,512]{2,1,0:T(8,128)(2,1)} %shard_map.59), calls=%async_computation.1 | async-start | bytes 1179648 | tf_op jit(solution)/shard_map/all_to_all | solution.py:382
  165.8 0.0 copy-start.2
  165.8 0.0 all-gather.2.cloned.1.call-done
  165.8 2.6 %constant_dynamic-slice_fusion.2 = (bf16[576,576]{1,0:T(8,128)(2,1)}, bf16[576,576]{1,0:T(8,128)(2,1)}) fusion(bf16[1152,576]{1,0:T(8,128)(2,1)} %all-gather.2.cloned.1.call-done, s32[]{:T(128)S(6)} %select_n.52, s32[]{:T(128)S(6)} %select_n.51), kind=kLoop, calls=%fused_computation.16 | loop fusion | bytes 2654216 | tf_op jit(solution)/shard_map/dynamic_slice | solution.py:388
  168.5 0.0 collective-permute-start
  168.5 13.0 %all-to-all-done.1 = bf16[4,144,512]{2,1,0:T(8,128)(2,1)} async-done(((bf16[4,144,512]{2,1,0:T(8,128)(2,1)}), bf16[4,144,512]{2,1,0:T(8,128)(2,1)}, u32[]{:S(2)}, u32[]{:S(2)}) %all-to-all-start.1) | async-done | bytes 589856 | tf_op jit(solution)/shard_map/all_to_all | solution.py:382
  181.5 0.0 collective-permute-start.13
  181.5 0.7 slice.49
  182.2 0.4 constant_dynamic-slice_fusion
  182.6 1.1 copy.18
  183.7 0.1 dynamic-slice_bitcast_fusion.1
  183.7 0.9 copy.19.gate_ref
  184.6 0.0 collective-permute-done.far_w
  184.6 3.8 %shard_map.60 = bf16[576,512]{1,0:T(8,128)(2,1)} custom-call(bf16[576,576]{1,0:T(8,128)(2,1)} %get-tuple-element.22.near_w, bf16[576,576]{1,0:T(8,128)(2,1)} %collective-permute-done.far_w, bf16[576,512]{1,0:T(8,128)(2,1)} %bitcast.20.near_ref, bf16[576,512]{1,0:T(8,128)(2,1)} %collective-permute-done.13.far_ref, bf16[576,512]{1,0:T(8,128)(2,1)} %bitcast.36, ...), custom_call_target="tpu_custom_call" | custom-call | flops 679477248 | bytes 3686400 | tf_op jit(solution)/shard_map/pallas_call | solution.py:26
  (24 shorter events, 0.1 us)
Async XLA Ops:
  6.5 6.8 %copy-start = (bf16[288,8,3,72]{0,3,2,1:T(8,128)(2,1)S(1)}, bf16[288,8,3,72]{0,3,2,1:T(8,128)(2,1)}, u32[]{:S(2)}) copy-start(bf16[288,8,3,72]{0,3,2,1:T(8,128)(2,1)} %param.7) | copy-start | bytes 2985988
  9.3 37.6 %collective-permute-start.5 = (bf16[256,1152]{1,0:T(8,128)(2,1)}, bf16[256,1152]{1,0:T(8,128)(2,1)}, u32[]{:S(2)}, u32[]{:S(2)}) collective-permute-start(bf16[256,1152]{1,0:T(8,128)(2,1)} %get-tuple-element.23), channel_id=1, source_target_pairs={{0,8},{4,12},{8,0},{12,4},{1,9},{5,13},{9,1},{13,5},{2,10},{6,14},... | collective-permute-start | bytes 1769480 | tf_op jit(solution)/shard_map/ppermute | solution.py:325
  14.5 38.6 %all-to-all-start = ((bf16[4,216,288]{1,2,0:T(8,128)(2,1)}), bf16[4,216,288]{1,2,0:T(8,128)(2,1)S(1)}, u32[]{:S(2)}, u32[]{:S(2)}) async-start(bf16[4,216,288]{1,2,0:T(8,128)(2,1)} %bitcast.9), calls=%async_computation | async-start | bytes 1179648 | tf_op jit(solution)/shard_map/all_to_all | solution.py:358
  18.0 147.8 %all-gather.2.cloned.1.call-start = ((), (), s32[]{:S(2)}) async-start(), calls=%async_computation.2 | async-start | bytes 1843200 | tf_op jit(solution)/shard_map/all_gather | solution.py:386
  18.1 36.9 %collective-permute-start.2 = (bf16[256,1152]{1,0:T(8,128)(2,1)}, bf16[256,1152]{1,0:T(8,128)(2,1)S(1)}, u32[]{:S(2)}, u32[]{:S(2)}) collective-permute-start(bf16[256,1152]{1,0:T(8,128)(2,1)} %get-tuple-element.23), channel_id=1, source_target_pairs={{0,4},{4,8},{8,12},{1,5},{5,9},{9,13},{2,6},{6,10},{10,14},{3,7},{... | collective-permute-start | bytes 1769480 | tf_op jit(solution)/shard_map/ppermute | solution.py:323
  21.9 35.8 %collective-permute-start.3 = (bf16[256,1152]{1,0:T(8,128)(2,1)}, bf16[256,1152]{1,0:T(8,128)(2,1)S(1)}, u32[]{:S(2)}, u32[]{:S(2)}) collective-permute-start(bf16[256,1152]{1,0:T(8,128)(2,1)} %get-tuple-element.23), channel_id=1, source_target_pairs={{4,0},{8,4},{12,8},{5,1},{9,5},{13,9},{6,2},{10,6},{14,10},{7,3},{... | collective-permute-start | bytes 1769480 | tf_op jit(solution)/shard_map/ppermute | solution.py:324
  46.9 43.0 %collective-permute-start.7 = (bf16[256,1152]{1,0:T(8,128)(2,1)}, bf16[256,1152]{1,0:T(8,128)(2,1)}, u32[]{:S(2)}, u32[]{:S(2)}) collective-permute-start(bf16[256,1152]{1,0:T(8,128)(2,1)} %collective-permute-done.5.mine_ref), channel_id=1, source_target_pairs={{8,12},{4,0},{9,13},{5,1},{10,14},{6,2},{11,15},{7,3},{24,28},{20,... | collective-permute-start | bytes 1769480 | tf_op jit(solution)/shard_map/ppermute | solution.py:328
  48.2 60.7 %collective-permute-start.6 = (bf16[256,1152]{1,0:T(8,128)(2,1)}, bf16[256,1152]{1,0:T(8,128)(2,1)}, u32[]{:S(2)}, u32[]{:S(2)}) collective-permute-start(bf16[256,1152]{1,0:T(8,128)(2,1)} %collective-permute-done.5.mine_ref), channel_id=1, source_target_pairs={{0,1},{1,0},{2,3},{3,2},{4,5},{5,4},{6,7},{7,6},{8,9},{9,8},{10,11... | collective-permute-start | bytes 1769480 | tf_op jit(solution)/shard_map/ppermute | solution.py:197
  53.1 38.7 %collective-permute-start.1 = (bf16[4,216,288]{1,2,0:T(8,128)(2,1)S(1)}, bf16[4,216,288]{1,2,0:T(8,128)(2,1)S(1)}, u32[]{:S(2)}, u32[]{:S(2)}) collective-permute-start(bf16[4,216,288]{1,2,0:T(8,128)(2,1)S(1)} %all-to-all-done), channel_id=1, source_target_pairs={{0,16},{16,0},{1,17},{17,1},{2,18},{18,2},{3,19},{19,3},{4,20},{20... | collective-permute-start | bytes 1493000 | tf_op jit(solution)/shard_map/ppermute | solution.py:197
  55.0 2.8 %copy-start.5 = (bf16[256,1152]{1,0:T(8,128)(2,1)}, bf16[256,1152]{1,0:T(8,128)(2,1)S(1)}, u32[]{:S(2)}) copy-start(bf16[256,1152]{1,0:T(8,128)(2,1)S(1)} %collective-permute-done.2) | copy-start | bytes 1769476
  57.8 0.8 copy-start.6
  91.2 2.3 %copy-start.3 = (bf16[256,1152]{1,0:T(8,128)(2,1)}, bf16[256,1152]{1,0:T(8,128)(2,1)S(1)}, u32[]{:S(2)}) copy-start(bf16[256,1152]{1,0:T(8,128)(2,1)S(1)} %get-tuple-element.29.mine_ref) | copy-start | bytes 1769476
  91.2 2.3 %copy-start.4 = (bf16[256,1152]{1,0:T(8,128)(2,1)}, bf16[256,1152]{1,0:T(8,128)(2,1)S(1)}, u32[]{:S(2)}) copy-start(bf16[256,1152]{1,0:T(8,128)(2,1)S(1)} %get-tuple-element.28.mine_ref) | copy-start | bytes 1769476
  91.2 28.8 %collective-permute-start.8 = (bf16[256,1152]{1,0:T(8,128)(2,1)S(1)}, bf16[256,1152]{1,0:T(8,128)(2,1)}, u32[]{:S(2)}, u32[]{:S(2)}) collective-permute-start(bf16[256,1152]{1,0:T(8,128)(2,1)S(1)} %get-tuple-element.28.mine_ref), channel_id=1, source_target_pairs={{0,1},{1,0},{2,3},{3,2},{4,5},{5,4},{6,7},{7,6},{8,9},{9,8},{10,11... | collective-permute-start | bytes 1769480 | tf_op jit(solution)/shard_map/ppermute | solution.py:197
  91.3 34.5 %collective-permute-start.4 = (bf16[256,1152]{1,0:T(8,128)(2,1)S(1)}, bf16[256,1152]{1,0:T(8,128)(2,1)}, u32[]{:S(2)}, u32[]{:S(2)}) collective-permute-start(bf16[256,1152]{1,0:T(8,128)(2,1)S(1)} %get-tuple-element.29.mine_ref), channel_id=1, source_target_pairs={{0,1},{1,0},{2,3},{3,2},{4,5},{5,4},{6,7},{7,6},{8,9},{9,8},{10,11... | collective-permute-start | bytes 1769480 | tf_op jit(solution)/shard_map/ppermute | solution.py:197
  108.9 1.0 copy-start.1
  114.0 17.7 %collective-permute-start.11 = (bf16[288,512]{1,0:T(8,128)(2,1)}, bf16[288,512]{1,0:T(8,128)(2,1)S(1)}, u32[]{:S(2)}, u32[]{:S(2)}) collective-permute-start(bf16[288,512]{1,0:T(8,128)(2,1)} %get-tuple-element.19.refs_7_), channel_id=1, source_target_pairs={{0,2},{2,0},{1,3},{3,1},{4,6},{6,4},{5,7},{7,5},{8,10},{10,8},{9,1... | collective-permute-start | bytes 884744 | tf_op jit(solution)/shard_map/ppermute | solution.py:197
  119.7 12.0 %collective-permute-start.9 = (bf16[288,512]{1,0:T(8,128)(2,1)}, bf16[288,512]{1,0:T(8,128)(2,1)S(1)}, u32[]{:S(2)}, u32[]{:S(2)}) collective-permute-start(bf16[288,512]{1,0:T(8,128)(2,1)} %get-tuple-element.17.refs_5_), channel_id=1, source_target_pairs={{0,2},{2,0},{1,3},{3,1},{4,6},{6,4},{5,7},{7,5},{8,10},{10,8},{9,1... | collective-permute-start | bytes 884744 | tf_op jit(solution)/shard_map/ppermute | solution.py:197
  124.2 12.4 %collective-permute-start.12 = (bf16[288,512]{1,0:T(8,128)(2,1)}, bf16[288,512]{1,0:T(8,128)(2,1)S(1)}, u32[]{:S(2)}, u32[]{:S(2)}) collective-permute-start(bf16[288,512]{1,0:T(8,128)(2,1)} %get-tuple-element.20.refs_8_), channel_id=1, source_target_pairs={{0,2},{2,0},{1,3},{3,1},{4,6},{6,4},{5,7},{7,5},{8,10},{10,8},{9,1... | collective-permute-start | bytes 884744 | tf_op jit(solution)/shard_map/ppermute | solution.py:197
  130.0 12.1 %collective-permute-start.10 = (bf16[288,512]{1,0:T(8,128)(2,1)}, bf16[288,512]{1,0:T(8,128)(2,1)S(1)}, u32[]{:S(2)}, u32[]{:S(2)}) collective-permute-start(bf16[288,512]{1,0:T(8,128)(2,1)} %get-tuple-element.18.refs_6_), channel_id=1, source_target_pairs={{0,2},{2,0},{1,3},{3,1},{4,6},{6,4},{5,7},{7,5},{8,10},{10,8},{9,1... | collective-permute-start | bytes 884744 | tf_op jit(solution)/shard_map/ppermute | solution.py:197
  131.7 10.4 %copy-start.7 = (bf16[288,512]{1,0:T(8,128)(2,1)}, bf16[288,512]{1,0:T(8,128)(2,1)S(1)}, u32[]{:S(2)}) copy-start(bf16[288,512]{1,0:T(8,128)(2,1)S(1)} %collective-permute-done.11.refs_11_) | copy-start | bytes 884740
  131.7 10.4 %copy-start.8 = (bf16[288,512]{1,0:T(8,128)(2,1)}, bf16[288,512]{1,0:T(8,128)(2,1)S(1)}, u32[]{:S(2)}) copy-start(bf16[288,512]{1,0:T(8,128)(2,1)S(1)} %collective-permute-done.9.refs_9_) | copy-start | bytes 884740
  136.6 5.5 %copy-start.9 = (bf16[288,512]{1,0:T(8,128)(2,1)}, bf16[288,512]{1,0:T(8,128)(2,1)S(1)}, u32[]{:S(2)}) copy-start(bf16[288,512]{1,0:T(8,128)(2,1)S(1)} %collective-permute-done.12.refs_12_) | copy-start | bytes 884740
  142.1 0.7 copy-start.10
  161.6 19.9 %all-to-all-start.1 = ((bf16[4,144,512]{2,1,0:T(8,128)(2,1)}), bf16[4,144,512]{2,1,0:T(8,128)(2,1)}, u32[]{:S(2)}, u32[]{:S(2)}) async-start(bf16[4,144,512]{2,1,0:T(8,128)(2,1)} %shard_map.59), calls=%async_computation.1 | async-start | bytes 1179648 | tf_op jit(solution)/shard_map/all_to_all | solution.py:382
  165.8 16.4 %copy-start.2 = (bf16[1,512,1152]{2,1,0:T(8,128)(2,1)S(1)}, bf16[1,512,1152]{2,1,0:T(8,128)(2,1)}, u32[]{:S(2)}) copy-start(bf16[1,512,1152]{2,1,0:T(8,128)(2,1)} %param.5) | copy-start | bytes 3538948
  168.5 16.2 %collective-permute-start = (bf16[576,576]{1,0:T(8,128)(2,1)}, bf16[576,576]{1,0:T(8,128)(2,1)}, u32[]{:S(2)}, u32[]{:S(2)}) collective-permute-start(bf16[576,576]{1,0:T(8,128)(2,1)} %get-tuple-element.21), channel_id=1, source_target_pairs={{0,1},{1,0},{2,3},{3,2},{4,5},{5,4},{6,7},{7,6},{8,9},{9,8},{10,11... | collective-permute-start | bytes 1990664 | tf_op jit(solution)/shard_map/ppermute | solution.py:197
  181.5 3.2 %collective-permute-start.13 = (bf16[576,512]{1,0:T(8,128)(2,1)}, bf16[576,512]{1,0:T(8,128)(2,1)}, u32[]{:S(2)}, u32[]{:S(2)}) collective-permute-start(bf16[576,512]{1,0:T(8,128)(2,1)} %bitcast.20.near_ref), channel_id=1, source_target_pairs={{0,1},{1,0},{2,3},{3,2},{4,5},{5,4},{6,7},{7,6},{8,9},{9,8},{10,11... | collective-permute-start | bytes 1769480 | tf_op jit(solution)/shard_map/ppermute | solution.py:197
Sparse Core Ops, SparseCore 0:
  48.3 44.4 all-gather.1

commit v2 on v0

--- a/solution.py
+++ b/solution.py
@@ -1,9 +1,333 @@
+import functools
 import math
 
 import jax
 import jax.numpy as jnp
 from jax import lax
+from jax.experimental import pallas as pl
+from jax.experimental.pallas import tpu as pltpu
 from jax.sharding import PartitionSpec as P
+
+VMEM_LIMIT = 56 * 2**20
+
+
+def dot_nn(a, b):
+    return lax.dot_general(a, b, (((1,), (0,)), ((), ())), preferred_element_type=jnp.float32)
+
+
+def dot_nt(a, b):
+    return lax.dot_general(a, b, (((1,), (1,)), ((), ())), preferred_element_type=jnp.float32)
+
+
+def call(kernel, out_shape, operands, scratch=(), flops=0, moved=0, left=()):
+    smem = pl.BlockSpec(memory_space=pltpu.SMEM)
+    vmem = pl.BlockSpec(memory_space=pltpu.VMEM)
+    where = pl.BlockSpec(memory_space=pl.ANY)
+    many = isinstance(out_shape, (list, tuple))
+    return pl.pallas_call(
+        kernel,
+        out_shape=out_shape,
+        in_specs=[where if i in left else smem if x.dtype == jnp.int32 else vmem for i, x in enumerate(operands)],
+        out_specs=[vmem] * len(out_shape) if many else vmem,
+        scratch_shapes=list(scratch),
+        compiler_params=pltpu.CompilerParams(vmem_limit_bytes=VMEM_LIMIT),
+        cost_estimate=pl.CostEstimate(flops=flops, bytes_accessed=moved, transcendentals=0),
+    )(*operands)
+
+
+def norm_kernel(place_ref, frame_ref, mod_ref, out_ref, rows, arrived):
+    half = out_ref.shape[0]
+    start = pl.multiple_of(place_ref[0] * half, half)
+    copy = pltpu.make_async_copy(frame_ref.at[pl.ds(start, half), :], rows, arrived)
+    copy.start()
+    copy.wait()
+    values = rows[...].astype(jnp.float32)
+    row_mean = jnp.mean(values, axis=-1, keepdims=True)
+    centred = values - row_mean
+    row_var = jnp.mean(centred * centred, axis=-1, keepdims=True)
+    normed = centred * lax.rsqrt(row_var + 1e-06)
+    out_ref[...] = (normed * (1.0 + mod_ref[1:2, :]) + mod_ref[0:1, :]).astype(jnp.bfloat16)
+
+
+def norm_half(place, frame, modulation):
+    half, width = frame.shape[0] // 2, frame.shape[1]
+    return call(
+        norm_kernel,
+        jax.ShapeDtypeStruct((half, width), jnp.bfloat16),
+        (place, frame, modulation),
+        [pltpu.VMEM((half, width), jnp.bfloat16), pltpu.SemaphoreType.DMA],
+        flops=20 * half * width,
+        moved=4 * half * width,
+        left=(1,),
+    )
+
+
+def weight_kernel(heads, head_dim, group_ref, mine_ref, partner_ref, out_ref):
+    parts = []
+    for ref in (mine_ref, partner_ref):
+        pieces = [ref[source].astype(jnp.float32) for source in range(ref.shape[0])]
+        parts.append(jnp.concatenate(pieces, 1))
+    swap = group_ref[0] == 1
+    per_head = (jnp.where(swap, parts[1], parts[0]), jnp.where(swap, parts[0], parts[1]))
+    rows = [w[kind * head_dim : (kind + 1) * head_dim] for kind in (1, 2, 0) for w in per_head]
+    out_ref[...] = jnp.concatenate(rows, 0).astype(jnp.bfloat16)
+
+
+def join_weight(group, mine, partner, heads, head_dim):
+    count, part_rows, share = mine.shape
+    out = (2 * part_rows, count * share)
+    return call(
+        functools.partial(weight_kernel, heads, head_dim),
+        jax.ShapeDtypeStruct(out, jnp.bfloat16),
+        (group, mine, partner),
+        flops=4 * out[0] * out[1],
+        moved=4 * out[0] * out[1],
+    )
+
+
+def project_kernel(kv_width, sources, *refs):
+    pick_ref, weight_ref = refs[0], refs[1]
+    pairs = [refs[2 + 2 * i : 4 + 2 * i] for i in range(sources)]
+    kv_ref, q_ref, hidden, arrived = refs[2 + 2 * sources :]
+    half = pairs[0][0].shape[0]
+    starts = (pl.multiple_of(pick_ref[0] * half, half), pl.multiple_of((1 - pick_ref[0]) * half, half))
+
+    def copies(pair):
+        return [
+            pltpu.make_async_copy(ref, hidden.at[pl.ds(start, half), :], arrived.at[i])
+            for i, (ref, start) in enumerate(zip(pair, starts))
+        ]
+
+    for i, pair in enumerate(pairs):
+        def fetch(pair=pair):
+            for copy in copies(pair):
+                copy.start()
+        if sources == 1:
+            fetch()
+        else:
+            pl.when(pick_ref[1] == i)(fetch)
+    for copy in copies(pairs[0]):
+        copy.wait()
+    mixed = dot_nt(weight_ref[...], hidden[...]).astype(jnp.bfloat16)
+    kv_ref[...] = mixed[:kv_width]
+    q_ref[...] = mixed[kv_width:]
+
+
+def project(pick, sources, weight, kv_width):
+    half, width = sources[0][0].shape
+    rows = 2 * half
+    out_width = weight.shape[0]
+    flat = [block for pair in sources for block in pair]
+    return call(
+        functools.partial(project_kernel, kv_width, len(sources)),
+        (
+            jax.ShapeDtypeStruct((kv_width, rows), jnp.bfloat16),
+            jax.ShapeDtypeStruct((out_width - kv_width, rows), jnp.bfloat16),
+        ),
+        (pick, weight, *flat),
+        [pltpu.VMEM((rows, width), jnp.bfloat16), pltpu.SemaphoreType.DMA((2,))],
+        flops=2 * rows * width * out_width,
+        moved=2 * (rows * width + width * out_width + rows * out_width),
+        left=range(2, 2 + len(flat)),
+    )
+
+
+def unpack_queries(ref, frame, heads, head_dim, q_all):
+    queries = ref[...].astype(jnp.float32)
+    for head in range(heads):
+        q_all[frame * heads + head] = queries[head * head_dim : (head + 1) * head_dim].astype(jnp.bfloat16)
+
+
+def unpack_keyvals(ref, base, side, heads, head_dim, k_all, v_all):
+    rows = ref.shape[1]
+    ones = jnp.ones((v_all.shape[1] - head_dim, rows), jnp.float32)
+    keyvals = ref[...].astype(jnp.float32)
+    span = pl.ds(side * rows, rows)
+    for head in range(heads):
+        keys = keyvals[head * head_dim : (head + 1) * head_dim]
+        k_all[base + head, span, :] = keys.T.astype(jnp.bfloat16)
+        first = (heads + head) * head_dim
+        values = jnp.concatenate([keyvals[first : first + head_dim], ones], 0)
+        v_all[base + head, :, span] = values.astype(jnp.bfloat16)
+
+
+def run_items(items, q_list, k_list, key_rows, heads, head_dim, q_all, k_all, v_all, scores_of, block_high, scale_old, high, total):
+    factor = math.log2(math.e) / math.sqrt(head_dim)
+    step = math.gcd(key_rows, 256)
+
+    def stage(now, before):
+        if now is not None:
+            head_a, item_a = now
+            state_a = q_list[item_a] * heads + head_a
+            key_a = k_list[item_a] * heads + head_a
+            queries = q_all[state_a]
+            old = high[state_a]
+            top = old
+        if before is not None:
+            head_b, item_b = before
+            state_b = q_list[item_b] * heads + head_b
+            key_b = k_list[item_b] * heads + head_b
+            top_b = block_high[head_b]
+            running = total[state_b] * scale_old[head_b]
+        for start in range(0, key_rows, step):
+            part = pl.ds(start, step)
+            if now is not None:
+                scores = dot_nn(k_all[key_a, part, :], queries)
+                scores_of[head_a][part, :] = scores
+                top = jnp.maximum(top, jnp.max(scores, axis=0, keepdims=True))
+            if before is not None:
+                probs = jnp.exp2((scores_of[head_b][part, :] - top_b) * factor).astype(jnp.bfloat16)
+                running = running + dot_nn(v_all[key_b, :, part], probs)
+        if before is not None:
+            total[state_b] = running
+        if now is not None:
+            scale_old[head_a] = jnp.exp2((old - top) * factor)
+            block_high[head_a] = top
+            high[state_a] = top
+
+    def body(index, carry):
+        stage((1, index), (0, index))
+        stage((0, index + 1), (1, index))
+        return carry
+
+    stage((0, 0), None)
+    lax.fori_loop(0, items - 1, body, 0)
+    stage((1, items - 1), (0, items - 1))
+    stage(None, (1, items - 1))
+
+
+def list_items(count, anchor, keep, q_list, k_list):
+    items = jnp.int32(0)
+    for frame in range(count):
+        pairs = [(jnp.int32(frame), None)]
+        if frame > 0:
+            pairs.append((jnp.int32(frame - 1), None))
+        pairs.append((anchor, (anchor != frame) & (anchor != frame - 1)))
+        for key, valid in pairs:
+            q_list[items] = frame
+            k_list[items] = key
+            kept = keep(frame, key)
+            items += jnp.where(kept if valid is None else kept & valid, 1, 0)
+    return items
+
+
+def first_kernel(count, heads, head_dim, *refs):
+    ids_ref = refs[0]
+    q_refs = refs[1 : 1 + count]
+    near_refs = refs[1 + count : 1 + 2 * count]
+    far_refs = refs[1 + 2 * count : 3 * count]
+    high, total = refs[3 * count : 3 * count + 2]
+    q_all, k_all, v_all, even, odd, block_high, scale_old, q_list, k_list = refs[3 * count + 2 :]
+    rows = q_refs[0].shape[1]
+    for slot in range(count):
+        frame = ids_ref[slot]
+        unpack_queries(q_refs[slot], frame, heads, head_dim, q_all)
+        unpack_keyvals(near_refs[slot], frame * heads, 0, heads, head_dim, k_all, v_all)
+        if slot < count - 1:
+            unpack_keyvals(far_refs[slot], frame * heads, 1, heads, head_dim, k_all, v_all)
+    anchor = ids_ref[count]
+    late = ids_ref[count - 1]
+    high[...] = jnp.full_like(high, -1e30)
+    total[...] = jnp.zeros_like(total)
+    rest = (heads, head_dim, q_all, k_all, v_all, (even, odd), block_high, scale_old, high, total)
+    items = list_items(count, anchor, lambda q, k: k != late, q_list, k_list)
+    run_items(items, q_list, k_list, 2 * rows, *rest)
+    items = list_items(count, anchor, lambda q, k: k == late, q_list, k_list)
+    run_items(items, q_list, k_list, rows, *rest)
+
+
+def second_kernel(count, heads, head_dim, *refs):
+    ids_ref = refs[0]
+    q_refs = refs[1 : 1 + count]
+    far_ref, high_in, total_in, out_ref = refs[1 + count : 5 + count]
+    high, total, q_all, k_late, v_late, even, odd, block_high, scale_old, q_list, k_list = refs[5 + count :]
+    rows = q_refs[0].shape[1]
+    for slot in range(count):
+        unpack_queries(q_refs[slot], ids_ref[slot], heads, head_dim, q_all)
+    unpack_keyvals(far_ref, 0, 0, heads, head_dim, k_late, v_late)
+    high[...] = high_in[...]
+    total[...] = total_in[...]
+    late = ids_ref[count - 1]
+    items = list_items(count, ids_ref[count], lambda q, k: k == late, q_list, k_list)
+    for item in range(count):
+        k_list[item] = 0
+    run_items(
+        items, q_list, k_list, rows, heads, head_dim, q_all, k_late, v_late, (even, odd), block_high, scale_old, high, total
+    )
+    for frame in range(count):
+        parts = []
+        for head in range(heads):
+            sums = total[frame * heads + head]
+            parts.append(sums[:head_dim] / sums[head_dim : head_dim + 1])
+        out_ref[frame] = jnp.concatenate(parts, 0).astype(jnp.bfloat16)
+
+
+def attend_all(ids, queries, near, far, heads, head_dim):
+    count = len(queries)
+    rows = queries[0].shape[1]
+    value_rows = head_dim + 8
+    states = count * heads
+    f32 = jnp.float32
+    lists = [pltpu.SMEM((3 * count + 1,), jnp.int32)] * 2
+    tops = [pltpu.VMEM((heads, 1, rows), f32)] * 2
+    state = (
+        jax.ShapeDtypeStruct((states, 1, rows), f32),
+        jax.ShapeDtypeStruct((states, value_rows, rows), f32),
+    )
+    high, total = call(
+        functools.partial(first_kernel, count, heads, head_dim),
+        state,
+        (ids, *queries, *near, *far[:-1]),
+        [
+            pltpu.VMEM((states, head_dim, rows), jnp.bfloat16),
+            pltpu.VMEM((states, 2 * rows, head_dim), jnp.bfloat16),
+            pltpu.VMEM((states, value_rows, 2 * rows), jnp.bfloat16),
+            pltpu.VMEM((2 * rows, rows), f32),
+            pltpu.VMEM((2 * rows, rows), f32),
+            *tops,
+            *lists,
+        ],
+        flops=3 * count * heads * rows * 2 * rows * head_dim * 16,
+        moved=2 * count * heads * head_dim * rows * 6,
+    )
+    return call(
+        functools.partial(second_kernel, count, heads, head_dim),
+        jax.ShapeDtypeStruct((count, heads * head_dim, rows), jnp.bfloat16),
+        (ids, *queries, far[-1], high, total),
+        [
+            pltpu.VMEM(state[0].shape, f32),
+            pltpu.VMEM(state[1].shape, f32),
+            pltpu.VMEM((states, head_dim, rows), jnp.bfloat16),
+            pltpu.VMEM((heads, rows, head_dim), jnp.bfloat16),
+            pltpu.VMEM((heads, value_rows, rows), jnp.bfloat16),
+            pltpu.VMEM((rows, rows), f32),
+            pltpu.VMEM((rows, rows), f32),
+            *tops,
+            *lists,
+        ],
+        flops=heads * rows * rows * head_dim * 16,
+        moved=2 * count * heads * head_dim * rows * 6,
+    )
+
+
+def finish_kernel(near_w, far_w, near_ref, far_ref, frame_ref, gate_ref, out_ref):
+    projected = dot_nn(near_w[...], near_ref[...]) + dot_nn(far_w[...], far_ref[...])
+    updated = frame_ref[...].astype(jnp.float32) + gate_ref[...] * projected
+    out_ref[...] = updated.astype(jnp.bfloat16)
+
+
+def finish(near_w, far_w, near, far, frame_part, gate_part):
+    return call(
+        finish_kernel,
+        jax.ShapeDtypeStruct(frame_part.shape, jnp.bfloat16),
+        (near_w, far_w, near, far, frame_part, gate_part),
+        flops=4 * near_w.shape[0] * near_w.shape[1] * near.shape[1],
+        moved=4 * (near_w.size + near.size + frame_part.size),
+    )
+
+
+def swapped(block, axis):
+    return lax.ppermute(block, axis, [(0, 1), (1, 0)])
 
 
 def shifted(block, axis, distance):
@@ -71,7 +395,7 @@
     return jnp.stack(frame_outputs)
 
 
-def on_device(frames, modulation, w_qkv, w_out, anchor_offsets):
+def by_frames(frames, modulation, w_qkv, w_out, anchor_offsets):
     frame_count, row_count, model_width = frames.shape
     head_local = w_qkv.shape[1]
     head_dim = w_qkv.shape[3]
@@ -123,6 +447,89 @@
     return result.reshape(frame_count, row_count, half_width)
 
 
+def after(block, other):
+    return lax.optimization_barrier((block, other))[0]
+
+
+def by_heads(frames, modulation, w_qkv, w_out, anchor_offsets):
+    _, rows, width = frames.shape
+    share, head_local, _, head_dim = w_qkv.shape
+    count = lax.axis_size("frame")
+    heads = head_local // count
+    core = lax.axis_index("head")
+    me = lax.axis_index("frame")
+    group = lax.axis_index("groups")
+    frame = frames[0]
+    place = core.reshape(1).astype(jnp.int32)
+    middle = count // 2
+
+    blocks = jnp.transpose(w_qkv, (1, 2, 3, 0)).reshape(count, heads, 3 * head_dim, share)
+    part = lax.dynamic_index_in_dim(blocks, group, 1, keepdims=False)
+    part = lax.all_to_all(part, "frame", 0, 0)
+    weight = join_weight(group.reshape(1).astype(jnp.int32), part, swapped(part, "groups"), heads, head_dim)
+    kv_width = 2 * heads * head_dim
+
+    mine = norm_half(place, frame, modulation)
+    across = lax.ppermute(mine, "frame", [(i, i ^ middle) for i in range(count)])
+    right = lax.ppermute(mine, "frame", [(i, i + 1) for i in range(count - 1)])
+    left = lax.ppermute(mine, "frame", [(i + 1, i) for i in range(count - 1)])
+    ends = lax.ppermute(across, "frame", [(count - 2, count - 1), (1, 0)])
+    pairs = {name: (block, swapped(block, "head")) for name, block in (("own", mine), ("right", right), ("left", left), ("across", across), ("ends", ends))}
+
+    at_end = (me == 0) | (me == count - 1)
+    slots = (
+        (me, 0, ("own",)),
+        (jnp.where(me == 0, 1, me - 1), jnp.where(me == 0, 1, 0), ("right", "left")),
+        (me ^ middle, 0, ("across",)),
+        (jnp.where(at_end, count - 1 - me, me + 1), jnp.where(at_end, 1, 0), ("left", "ends")),
+    )
+    queries, near, far = [], [], []
+    for _, pick, names in slots:
+        picked = jnp.stack([core, pick]).astype(jnp.int32)
+        kv, q = project(picked, [pairs[name] for name in names], weight, kv_width)
+        queries.append(q)
+        near.append(kv)
+        far.append(swapped(kv, "tok"))
+    ids = jnp.stack([index for index, _, _ in slots] + [anchor_offsets[0]]).astype(jnp.int32)
+    attended = attend_all(ids, queries, near, far, heads, head_dim)
+    arrived = lax.all_to_all(attended, "frame", 0, 0).reshape(count * heads * head_dim, rows)
+    arrived_far = swapped(arrived, "head")
+
+    out_half = width // 2
+    columns = w_out.shape[1] // 2
+    w_part = lax.dynamic_slice_in_dim(w_out.T, group * columns, columns, 0)
+    w_part = after(w_part, ends)
+    w_part = lax.all_to_all(jnp.broadcast_to(w_part[None], (count, *w_part.shape)), "frame", 0, 0)
+    w_other = swapped(w_part, "groups")
+    w_first = jnp.where(group == 0, w_part, w_other)
+    w_second = jnp.where(group == 0, w_other, w_part)
+    w_cols = jnp.concatenate([w_first, w_second], 1).reshape(width, w_out.shape[0])
+    near_w = lax.dynamic_slice_in_dim(w_cols, core * out_half, out_half, 0)
+    far_w = swapped(lax.dynamic_slice_in_dim(w_cols, (1 - core) * out_half, out_half, 0), "head")
+    frame_part = lax.dynamic_slice_in_dim(frame, core * out_half, out_half, 1).T
+    gate_part = lax.dynamic_slice_in_dim(modulation[2], core * out_half, out_half, 0)[:, None]
+    updated = finish(near_w, far_w, arrived, arrived_far, frame_part, gate_part)
+    return updated.T[None]
+
+
+def on_device(frames, modulation, w_qkv, w_out, anchor_offsets):
+    count = lax.axis_size("frame")
+    fits = (
+        frames.shape[0] == 1
+        and anchor_offsets.shape[0] == 1
+        and count == 4
+        and lax.axis_size("groups") == 2
+        and lax.axis_size("head") == 2
+        and lax.axis_size("tok") == 2
+        and w_qkv.shape[1] == 2 * count
+        and w_qkv.shape[3] % 8 == 0
+        and frames.shape[1] % 256 == 0
+        and frames.shape[2] % 32 == 0
+    )
+    step = by_heads if fits else by_frames
+    return step(frames, modulation, w_qkv, w_out, anchor_offsets)
+
+
 def solution(mesh):
     placed = (
         P(("groups", "frame"), "tok", None),

time: 447 us -> 151 us (0.34)
  waiting for transfers between devices: 323 us -> 54.6 us
  Pallas kernels: 0 us -> 44.5 us
  starting transfers between devices: 5.15 us -> 36.1 us
  matrix products: 30.4 us -> 0 us
  local copies, waits for them, and re-layouts: 34.2 us -> 12 us
  loops' own time: 20.6 us -> 0 us
  other arithmetic: 19.2 us -> 1.58 us
  between operations: 14 us -> 0.81 us
    all_gather x3 -> x0, waiting for transfers between devices: 239 us -> none  [the longest x1 130 us: on_device(): full_weight = lax.all_gather(w_qkv, 'frame', axis=0, tiled=True)]
    pallas_call x0 -> x9, Pallas kernels: none -> 44.5 us  [call(): pl.pallas_call(kernel, out_shape=out_shape, in_specs=[where if i in left...]
    ppermute x3 -> x17, waiting for transfers between devices: 75.8 us -> 35.6 us  [the longest x1 22.2 us: by_heads(): lax.ppermute(mine, 'frame', [(i, i ^ middle) for i in range(count)])]
    dot_general x18 -> x0, matrix products: 30.4 us -> none  [the longest x8 11.8 us: one_block(): jnp.dot(probs.astype(jnp.bfloat16), val_rows, preferred_element_type=jnp....]
    another operation x1 -> x0, loops' own time: 20.6 us -> none  [attend(): per_head = lax.map(one_head, jnp.arange(head_count, dtype=jnp.int32))]
    all_to_all x0 -> x3, waiting for transfers between devices: none -> 19 us  [the longest x1 14.1 us: by_heads(): lax.all_to_all(attended, 'frame', 0, 0)]
    ppermute x3 -> x17, starting transfers between devices: 5.03 us -> 20.7 us  [the longest x13 8.68 us: swapped(): return lax.ppermute(block, axis, [(0, 1), (1, 0)])]
    all_to_all x0 -> x3, starting transfers between devices: none -> 15.4 us  [the longest x1 7.4 us: by_heads(): lax.all_to_all(jnp.broadcast_to(w_part[None], (count, *w_part.shape)), 'f...]
  transfers between devices with their start and end apart: 7 -> 20, of which waited for: 5 -> 6; matrix products, arithmetic and copies ran while one was open for 12% -> 9% of each run, Pallas kernels for 0% -> 25%
where the time goes in v2:
time: 151 us; the launch traced here: 150 us
  waiting for transfers between devices  54.6 us (36%)
  Pallas kernels  44.5 us (29%)
  starting transfers between devices  36.1 us (24%)
  local copies, waits for them, and re-layouts  12 us (8%)
  other arithmetic  1.58 us (1%)
    pallas_call x9, Pallas kernels, call(): pl.pallas_call(kernel, out_shape=out_shape, in_specs=[where if i in left...  44.5 us
    ppermute x1, waiting for transfers between devices, by_heads(): lax.ppermute(mine, 'frame', [(i, i ^ middle) for i in range(count)])  22.2 us
    all_to_all x1, waiting for transfers between devices, by_heads(): lax.all_to_all(attended, 'frame', 0, 0)  14.1 us
    ppermute x1, waiting for transfers between devices, by_heads(): ends = lax.ppermute(across, 'frame', [(count - 2, count - 1), (1, 0)])  9.76 us
    ppermute x13, starting transfers between devices, swapped(): return lax.ppermute(block, axis, [(0, 1), (1, 0)])  8.68 us
    all_to_all x1, starting transfers between devices, by_heads(): lax.all_to_all(jnp.broadcast_to(w_part[None], (count, *w_part.shape)), 'f...  7.4 us
    ppermute x1, starting transfers between devices, by_heads(): right = lax.ppermute(mine, 'frame', [(i, i + 1) for i in range(count - 1)])  5.39 us
    all_to_all x1, waiting for transfers between devices, by_heads(): part = lax.all_to_all(part, 'frame', 0, 0)  4.97 us
  transfers between devices with their start and end apart: 20, of which 6 were waited for; matrix products, arithmetic and copies ran while one was open for 9% of the time, Pallas kernels for 25%

profile of v2, /device:TPU:0, one launch (start us, length us, event | category | flops | bytes accessed | tf_op | source)
XLA Modules:
  0.0 149.8 jit_solution(7211960185029899773)
XLA Ops:
  0.0 3.1 %shard_map.55.refs_2_ = bf16[256,1152]{1,0:T(8,128)(2,1)} custom-call(s32[1]{0:T(128)} %bitcast.1.place_ref, bf16[512,1152]{1,0:T(8,128)(2,1)} %bitcast.27, f32[3,1152]{1,0:T(4,128)} %mod_ref.1), custom_call_target="tpu_custom_call" | custom-call | flops 5898240 | bytes 1179648 | tf_op jit(solution)/shard_map/pallas_call | solution.py:27
  3.1 4.1 %collective-permute-start = (bf16[256,1152]{1,0:T(8,128)(2,1)}, bf16[256,1152]{1,0:T(8,128)(2,1)}, u32[]{:S(2)}, u32[]{:S(2)}) collective-permute-start(bf16[256,1152]{1,0:T(8,128)(2,1)} %shard_map.55.refs_2_), channel_id=1, source_target_pairs={{0,8},{4,12},{8,0},{12,4},{1,9},{5,13},{9,1},{13,5},{2,10},{6,14},... | collective-permute-start | bytes 1769480 | tf_op jit(solution)/shard_map/ppermute | solution.py:473
  7.2 0.1 constant_dynamic-slice_fusion.1
  7.3 1.1 copy.16
  8.4 3.5 %all-to-all-start.1 = ((bf16[4,216,288]{1,2,0:T(8,128)(2,1)}), bf16[4,216,288]{1,2,0:T(8,128)(2,1)S(1)}, u32[]{:S(2)}, u32[]{:S(2)}) async-start(bf16[4,216,288]{1,2,0:T(8,128)(2,1)} %bitcast.28), calls=%async_computation.1 | async-start | bytes 1179648 | tf_op jit(solution)/shard_map/all_to_all | solution.py:468
  11.9 1.3 collective-permute-start.8
  13.2 5.4 %collective-permute-start.6 = (bf16[256,1152]{1,0:T(8,128)(2,1)S(1)}, bf16[256,1152]{1,0:T(8,128)(2,1)}, u32[]{:S(2)}, u32[]{:S(2)}) collective-permute-start(bf16[256,1152]{1,0:T(8,128)(2,1)S(1)} %copy-done.2), channel_id=1, source_target_pairs={{0,4},{4,8},{8,12},{1,5},{5,9},{9,13},{2,6},{6,10},{10,14},{3,7},{... | collective-permute-start | bytes 1769480 | tf_op jit(solution)/shard_map/ppermute | solution.py:474
  18.6 22.2 %collective-permute-done.refs_2_ = bf16[256,1152]{1,0:T(8,128)(2,1)} collective-permute-done((bf16[256,1152]{1,0:T(8,128)(2,1)}, bf16[256,1152]{1,0:T(8,128)(2,1)}, u32[]{:S(2)}, u32[]{:S(2)}) %collective-permute-start) | collective-permute-done | bytes 589856 | tf_op jit(solution)/shard_map/ppermute | solution.py:473
  40.8 1.3 collective-permute-start.1
  42.0 5.0 %all-to-all-done.1 = bf16[4,216,288]{1,2,0:T(8,128)(2,1)S(1)} async-done(((bf16[4,216,288]{1,2,0:T(8,128)(2,1)}), bf16[4,216,288]{1,2,0:T(8,128)(2,1)S(1)}, u32[]{:S(2)}, u32[]{:S(2)}) %all-to-all-start.1) | async-done | bytes 497696 | tf_op jit(solution)/shard_map/all_to_all | solution.py:468
  47.0 1.8 %collective-permute-start.4 = (bf16[4,216,288]{1,2,0:T(8,128)(2,1)S(1)}, bf16[4,216,288]{1,2,0:T(8,128)(2,1)}, u32[]{:S(2)}, u32[]{:S(2)}) collective-permute-start(bf16[4,216,288]{1,2,0:T(8,128)(2,1)S(1)} %all-to-all-done.1), channel_id=1, source_target_pairs={{0,16},{16,0},{1,17},{17,1},{2,18},{18,2},{3,19},{19,3},{4,20},{20... | collective-permute-start | bytes 1493000 | tf_op jit(solution)/shard_map/ppermute | solution.py:330
  48.8 0.5 collective-permute-done.8.refs_4_.refs_2_
  49.3 0.0 collective-permute-start.9
  49.3 0.0 collective-permute-done.6.refs_2_
  49.3 0.5 collective-permute-start.7
  49.8 0.9 dynamic-slice_bitcast_fusion
  50.8 9.8 %collective-permute-done.1.refs_4_ = bf16[256,1152]{1,0:T(8,128)(2,1)} collective-permute-done((bf16[256,1152]{1,0:T(8,128)(2,1)}, bf16[256,1152]{1,0:T(8,128)(2,1)}, u32[]{:S(2)}, u32[]{:S(2)}) %collective-permute-start.1) | collective-permute-done | bytes 589856 | tf_op jit(solution)/shard_map/ppermute | solution.py:476
  60.6 0.9 broadcast_in_dim.12
  61.5 7.4 %all-to-all-start = ((bf16[4,144,576]{2,1,0:T(8,128)(2,1)}), bf16[4,144,576]{2,1,0:T(8,128)(2,1)S(1)}, u32[]{:S(2)}, u32[]{:S(2)}) async-start(bf16[4,144,576]{2,1,0:T(8,128)(2,1)} %broadcast_in_dim.12), calls=%async_computation | async-start | bytes 1474560 | tf_op jit(solution)/shard_map/all_to_all | solution.py:502
  68.9 0.0 collective-permute-start.10
  68.9 0.5 collective-permute-start.5
  69.4 0.0 collective-permute-done.4
  69.4 0.0 collective-permute-start.11
  69.4 0.7 pad_add_fusion
  70.1 1.1 copy.12.mine_ref
  71.2 2.2 %copy.13.partner_ref = bf16[4,216,288]{2,1,0:T(8,128)(2,1)} copy(bf16[4,216,288]{1,2,0:T(8,128)(2,1)} %collective-permute-done.4) | data formatting | bytes 995328 | tf_op jit(solution)/shard_map/ppermute | solution.py:330
  73.3 2.7 %shard_map.56.refs_1_ = bf16[432,1152]{1,0:T(8,128)(2,1)} custom-call(s32[1]{0:T(128)} %bitcast.8.group_ref, bf16[4,216,288]{2,1,0:T(8,128)(2,1)} %copy.12.mine_ref, bf16[4,216,288]{2,1,0:T(8,128)(2,1)} %copy.13.partner_ref), custom_call_target="tpu_custom_call" | custom-call | flops 1990656 | bytes 1990656 | tf_op jit(solution)/shard_map/pallas_call | solution.py:27
  76.0 0.0 collective-permute-done.9.refs_5_.refs_3_
  76.0 0.0 collective-permute-done.7.refs_3_
  76.0 4.0 %shard_map.58 = (bf16[288,512]{1,0:T(8,128)(2,1)}, bf16[144,512]{1,0:T(8,128)(2,1)}) custom-call(s32[2]{0:T(128)} %get-tuple-element.32.refs_0_, bf16[432,1152]{1,0:T(8,128)(2,1)} %shard_map.56.refs_1_, bf16[256,1152]{1,0:T(8,128)(2,1)} %collective-permute-done.6.refs_2_, bf16[256,1152]{1,0:T(8,128)(2,1)} %collective-permute-done.7.refs_3_, ...), custom_call_target="tpu_custom_call" | custom-call | flops 509607936 | bytes 2617344 | tf_op jit(solution)/shard_map/pallas_call | solution.py:27
  80.0 1.6 %collective-permute-start.14 = (bf16[288,512]{1,0:T(8,128)(2,1)}, bf16[288,512]{1,0:T(8,128)(2,1)S(1)}, u32[]{:S(2)}, u32[]{:S(2)}) collective-permute-start(bf16[288,512]{1,0:T(8,128)(2,1)} %get-tuple-element.23.refs_6_), channel_id=1, source_target_pairs={{0,2},{2,0},{1,3},{3,1},{4,6},{6,4},{5,7},{7,5},{8,10},{10,8},{9,1... | collective-permute-start | bytes 884744 | tf_op jit(solution)/shard_map/ppermute | solution.py:330
  81.6 0.0 collective-permute-done.10.refs_3_
  81.6 4.0 %shard_map.59 = (bf16[288,512]{1,0:T(8,128)(2,1)}, bf16[144,512]{1,0:T(8,128)(2,1)}) custom-call(s32[2]{0:T(128)} %get-tuple-element.31.refs_0_, bf16[432,1152]{1,0:T(8,128)(2,1)} %shard_map.56.refs_1_, bf16[256,1152]{1,0:T(8,128)(2,1)} %collective-permute-done.refs_2_, bf16[256,1152]{1,0:T(8,128)(2,1)} %collective-permute-done.10.refs_3_), custom_call_target="tpu_custom_call" | custom-call | flops 509607936 | bytes 2617344 | tf_op jit(solution)/shard_map/pallas_call | solution.py:27
  85.5 0.6 collective-permute-start.15
  86.1 0.0 collective-permute-done.5.refs_3_
  86.1 4.0 %shard_map.57 = (bf16[288,512]{1,0:T(8,128)(2,1)}, bf16[144,512]{1,0:T(8,128)(2,1)}) custom-call(s32[2]{0:T(128)} %get-tuple-element.31.refs_0_, bf16[432,1152]{1,0:T(8,128)(2,1)} %shard_map.56.refs_1_, bf16[256,1152]{1,0:T(8,128)(2,1)} %shard_map.55.refs_2_, bf16[256,1152]{1,0:T(8,128)(2,1)} %collective-permute-done.5.refs_3_), custom_call_target="tpu_custom_call" | custom-call | flops 509607936 | bytes 2617344 | tf_op jit(solution)/shard_map/pallas_call | solution.py:27
  90.1 1.6 %collective-permute-start.13 = (bf16[288,512]{1,0:T(8,128)(2,1)}, bf16[288,512]{1,0:T(8,128)(2,1)}, u32[]{:S(2)}, u32[]{:S(2)}) collective-permute-start(bf16[288,512]{1,0:T(8,128)(2,1)} %get-tuple-element.22.refs_5_), channel_id=1, source_target_pairs={{0,2},{2,0},{1,3},{3,1},{4,6},{6,4},{5,7},{7,5},{8,10},{10,8},{9,1... | collective-permute-start | bytes 884744 | tf_op jit(solution)/shard_map/ppermute | solution.py:330
  92.3 0.6 stack.39.refs_0_
  92.9 0.6 pad_add_fusion.2.refs_0_
  93.5 0.0 collective-permute-done.11.refs_5_
  93.6 4.0 %shard_map.60 = (bf16[288,512]{1,0:T(8,128)(2,1)}, bf16[144,512]{1,0:T(8,128)(2,1)}) custom-call(s32[2]{0:T(128)} %pad_add_fusion.2.refs_0_, bf16[432,1152]{1,0:T(8,128)(2,1)} %shard_map.56.refs_1_, bf16[256,1152]{1,0:T(8,128)(2,1)} %collective-permute-done.8.refs_4_.refs_2_, bf16[256,1152]{1,0:T(8,128)(2,1)} %collective-permute-done.9.refs_5_.refs_3_, ...), custom_call_target="tpu_custom_call" | custom-call | flops 509607936 | bytes 2617344 | tf_op jit(solution)/shard_map/pallas_call | solution.py:27
  97.5 0.6 collective-permute-start.12
  98.2 0.0 all-to-all-done
  98.2 1.5 %collective-permute-start.2 = (bf16[4,144,576]{2,1,0:T(8,128)(2,1)S(1)}, bf16[4,144,576]{2,1,0:T(8,128)(2,1)S(1)}, u32[]{:S(2)}, u32[]{:S(2)}) collective-permute-start(bf16[4,144,576]{2,1,0:T(8,128)(2,1)S(1)} %all-to-all-done), channel_id=1, source_target_pairs={{0,16},{16,0},{1,17},{17,1},{2,18},{18,2},{3,19},{19,3},{4,20},{20... | collective-permute-start | bytes 1990664 | tf_op jit(solution)/shard_map/ppermute | solution.py:330
  99.7 0.0 collective-permute-done.14.refs_10_
  99.7 0.0 collective-permute-done.15.refs_11_
  99.7 3.1 %collective-permute-done.13.refs_9_ = bf16[288,512]{1,0:T(8,128)(2,1)} collective-permute-done((bf16[288,512]{1,0:T(8,128)(2,1)}, bf16[288,512]{1,0:T(8,128)(2,1)}, u32[]{:S(2)}, u32[]{:S(2)}) %collective-permute-start.13) | collective-permute-done | bytes 294944 | tf_op jit(solution)/shard_map/ppermute | solution.py:330
  102.8 13.2 %shard_map.61 = (f32[8,1,512]{2,1,0:T(1,128)}, f32[8,80,512]{2,1,0:T(8,128)}) custom-call(s32[5]{0:T(128)} %stack.39.refs_0_, bf16[144,512]{1,0:T(8,128)(2,1)} %get-tuple-element.17.refs_1_, bf16[144,512]{1,0:T(8,128)(2,1)} %get-tuple-element.18.refs_2_, bf16[144,512]{1,0:T(8,128)(2,1)} %get-tuple-element.19.refs_3_, ...), custom_call_target="tpu_custom_call" | custom-call | flops 14495514624 | bytes 3538944 | tf_op jit(solution)/shard_map/pallas_call | solution.py:27
  116.0 0.7 copy-done.3
  116.7 5.8 %shard_map.62 = bf16[4,144,512]{2,1,0:T(8,128)(2,1)} custom-call(s32[5]{0:T(128)} %stack.39.refs_0_, bf16[144,512]{1,0:T(8,128)(2,1)} %get-tuple-element.17.refs_1_, bf16[144,512]{1,0:T(8,128)(2,1)} %get-tuple-element.18.refs_2_, bf16[144,512]{1,0:T(8,128)(2,1)} %get-tuple-element.19.refs_3_, bf16[144,512]{1,0:T(8,128)(2,1)} %get-tuple-element.20.refs_4_, ...), custom_call_target="tpu_custom_call" | custom-call | flops 603979776 | bytes 3538944 | tf_op jit(solution)/shard_map/pallas_call | solution.py:27
  122.6 4.5 %all-to-all-start.2 = ((bf16[4,144,512]{2,1,0:T(8,128)(2,1)}), bf16[4,144,512]{2,1,0:T(8,128)(2,1)}, u32[]{:S(2)}, u32[]{:S(2)}) async-start(bf16[4,144,512]{2,1,0:T(8,128)(2,1)} %shard_map.62), calls=%async_computation.2 | async-start | bytes 1179648 | tf_op jit(solution)/shard_map/all_to_all | solution.py:495
  127.1 0.1 broadcast_select_fusion.1
  127.2 0.1 pad_maximum_fusion
  127.4 0.0 copy-start.1
  127.4 1.3 constant_dynamic-slice_fusion.2
  128.7 0.0 collective-permute-start.3
  128.7 14.1 %all-to-all-done.2 = bf16[4,144,512]{2,1,0:T(8,128)(2,1)} async-done(((bf16[4,144,512]{2,1,0:T(8,128)(2,1)}), bf16[4,144,512]{2,1,0:T(8,128)(2,1)}, u32[]{:S(2)}, u32[]{:S(2)}) %all-to-all-start.2) | async-done | bytes 589856 | tf_op jit(solution)/shard_map/all_to_all | solution.py:495
  142.8 0.0 collective-permute-start.16
  142.8 0.7 slice.3
  143.5 0.4 constant_dynamic-slice_fusion
  143.9 1.1 copy.14
  144.9 0.1 dynamic-slice_bitcast_fusion.1
  145.0 0.9 copy.15.gate_ref
  145.9 3.8 %shard_map.63 = bf16[576,512]{1,0:T(8,128)(2,1)} custom-call(bf16[576,576]{1,0:T(8,128)(2,1)} %get-tuple-element.28.near_w, bf16[576,576]{1,0:T(8,128)(2,1)} %collective-permute-done.3.far_w, bf16[576,512]{1,0:T(8,128)(2,1)} %bitcast.14.near_ref, bf16[576,512]{1,0:T(8,128)(2,1)} %collective-permute-done.16.far_ref, bf16[576,512]{1,0:T(8,128)(2,1)} %bitcast.29, ...), custom_call_target="tpu_custom_call" | custom-call | flops 679477248 | bytes 3686400 | tf_op jit(solution)/shard_map/pallas_call | solution.py:27
  (12 shorter events, 0.0 us)
Async XLA Ops:
  0.0 7.2 %copy-start = (bf16[288,8,3,72]{0,3,2,1:T(8,128)(2,1)S(1)}, bf16[288,8,3,72]{0,3,2,1:T(8,128)(2,1)}, u32[]{:S(2)}) copy-start(bf16[288,8,3,72]{0,3,2,1:T(8,128)(2,1)} %param.7) | copy-start | bytes 2985988
  3.1 37.6 %collective-permute-start = (bf16[256,1152]{1,0:T(8,128)(2,1)}, bf16[256,1152]{1,0:T(8,128)(2,1)}, u32[]{:S(2)}, u32[]{:S(2)}) collective-permute-start(bf16[256,1152]{1,0:T(8,128)(2,1)} %shard_map.55.refs_2_), channel_id=1, source_target_pairs={{0,8},{4,12},{8,0},{12,4},{1,9},{5,13},{9,1},{13,5},{2,10},{6,14},... | collective-permute-start | bytes 1769480 | tf_op jit(solution)/shard_map/ppermute | solution.py:473
  7.3 4.6 %copy-start.2 = (bf16[256,1152]{1,0:T(8,128)(2,1)S(1)}, bf16[256,1152]{1,0:T(8,128)(2,1)}, u32[]{:S(2)}) copy-start(bf16[256,1152]{1,0:T(8,128)(2,1)} %shard_map.55.refs_2_) | copy-start | bytes 1769476
  8.4 38.6 %all-to-all-start.1 = ((bf16[4,216,288]{1,2,0:T(8,128)(2,1)}), bf16[4,216,288]{1,2,0:T(8,128)(2,1)S(1)}, u32[]{:S(2)}, u32[]{:S(2)}) async-start(bf16[4,216,288]{1,2,0:T(8,128)(2,1)} %bitcast.28), calls=%async_computation.1 | async-start | bytes 1179648 | tf_op jit(solution)/shard_map/all_to_all | solution.py:468
  11.9 37.4 %collective-permute-start.8 = (bf16[256,1152]{1,0:T(8,128)(2,1)S(1)}, bf16[256,1152]{1,0:T(8,128)(2,1)}, u32[]{:S(2)}, u32[]{:S(2)}) collective-permute-start(bf16[256,1152]{1,0:T(8,128)(2,1)S(1)} %copy-done.2), channel_id=1, source_target_pairs={{4,0},{8,4},{12,8},{5,1},{9,5},{13,9},{6,2},{10,6},{14,10},{7,3},{... | collective-permute-start | bytes 1769480 | tf_op jit(solution)/shard_map/ppermute | solution.py:475
  13.2 36.1 %collective-permute-start.6 = (bf16[256,1152]{1,0:T(8,128)(2,1)S(1)}, bf16[256,1152]{1,0:T(8,128)(2,1)}, u32[]{:S(2)}, u32[]{:S(2)}) collective-permute-start(bf16[256,1152]{1,0:T(8,128)(2,1)S(1)} %copy-done.2), channel_id=1, source_target_pairs={{0,4},{4,8},{8,12},{1,5},{5,9},{9,13},{2,6},{6,10},{10,14},{3,7},{... | collective-permute-start | bytes 1769480 | tf_op jit(solution)/shard_map/ppermute | solution.py:474
  40.8 19.8 %collective-permute-start.1 = (bf16[256,1152]{1,0:T(8,128)(2,1)}, bf16[256,1152]{1,0:T(8,128)(2,1)}, u32[]{:S(2)}, u32[]{:S(2)}) collective-permute-start(bf16[256,1152]{1,0:T(8,128)(2,1)} %collective-permute-done.refs_2_), channel_id=1, source_target_pairs={{8,12},{4,0},{9,13},{5,1},{10,14},{6,2},{11,15},{7,3},{24,28},{20,... | collective-permute-start | bytes 1769480 | tf_op jit(solution)/shard_map/ppermute | solution.py:476
  47.0 22.4 %collective-permute-start.4 = (bf16[4,216,288]{1,2,0:T(8,128)(2,1)S(1)}, bf16[4,216,288]{1,2,0:T(8,128)(2,1)}, u32[]{:S(2)}, u32[]{:S(2)}) collective-permute-start(bf16[4,216,288]{1,2,0:T(8,128)(2,1)S(1)} %all-to-all-done.1), channel_id=1, source_target_pairs={{0,16},{16,0},{1,17},{17,1},{2,18},{18,2},{3,19},{19,3},{4,20},{20... | collective-permute-start | bytes 1493000 | tf_op jit(solution)/shard_map/ppermute | solution.py:330
  49.3 26.7 %collective-permute-start.9 = (bf16[256,1152]{1,0:T(8,128)(2,1)}, bf16[256,1152]{1,0:T(8,128)(2,1)}, u32[]{:S(2)}, u32[]{:S(2)}) collective-permute-start(bf16[256,1152]{1,0:T(8,128)(2,1)} %collective-permute-done.8.refs_4_.refs_2_), channel_id=1, source_target_pairs={{0,1},{1,0},{2,3},{3,2},{4,5},{5,4},{6,7},{7,6},{8,9},{9,8},{10,11... | collective-permute-start | bytes 1769480 | tf_op jit(solution)/shard_map/ppermute | solution.py:330
  49.3 26.7 %collective-permute-start.7 = (bf16[256,1152]{1,0:T(8,128)(2,1)}, bf16[256,1152]{1,0:T(8,128)(2,1)}, u32[]{:S(2)}, u32[]{:S(2)}) collective-permute-start(bf16[256,1152]{1,0:T(8,128)(2,1)} %collective-permute-done.6.refs_2_), channel_id=1, source_target_pairs={{0,1},{1,0},{2,3},{3,2},{4,5},{5,4},{6,7},{7,6},{8,9},{9,8},{10,11... | collective-permute-start | bytes 1769480 | tf_op jit(solution)/shard_map/ppermute | solution.py:330
  61.5 36.7 %all-to-all-start = ((bf16[4,144,576]{2,1,0:T(8,128)(2,1)}), bf16[4,144,576]{2,1,0:T(8,128)(2,1)S(1)}, u32[]{:S(2)}, u32[]{:S(2)}) async-start(bf16[4,144,576]{2,1,0:T(8,128)(2,1)} %broadcast_in_dim.12), calls=%async_computation | async-start | bytes 1474560 | tf_op jit(solution)/shard_map/all_to_all | solution.py:502
  68.9 12.7 %collective-permute-start.10 = (bf16[256,1152]{1,0:T(8,128)(2,1)}, bf16[256,1152]{1,0:T(8,128)(2,1)}, u32[]{:S(2)}, u32[]{:S(2)}) collective-permute-start(bf16[256,1152]{1,0:T(8,128)(2,1)} %collective-permute-done.refs_2_), channel_id=1, source_target_pairs={{0,1},{1,0},{2,3},{3,2},{4,5},{5,4},{6,7},{7,6},{8,9},{9,8},{10,11... | collective-permute-start | bytes 1769480 | tf_op jit(solution)/shard_map/ppermute | solution.py:330
  68.9 17.3 %collective-permute-start.5 = (bf16[256,1152]{1,0:T(8,128)(2,1)S(1)}, bf16[256,1152]{1,0:T(8,128)(2,1)}, u32[]{:S(2)}, u32[]{:S(2)}) collective-permute-start(bf16[256,1152]{1,0:T(8,128)(2,1)S(1)} %copy-done.2), channel_id=1, source_target_pairs={{0,1},{1,0},{2,3},{3,2},{4,5},{5,4},{6,7},{7,6},{8,9},{9,8},{10,11... | collective-permute-start | bytes 1769480 | tf_op jit(solution)/shard_map/ppermute | solution.py:330
  69.4 24.2 %collective-permute-start.11 = (bf16[256,1152]{1,0:T(8,128)(2,1)}, bf16[256,1152]{1,0:T(8,128)(2,1)}, u32[]{:S(2)}, u32[]{:S(2)}) collective-permute-start(bf16[256,1152]{1,0:T(8,128)(2,1)} %collective-permute-done.1.refs_4_), channel_id=1, source_target_pairs={{0,1},{1,0},{2,3},{3,2},{4,5},{5,4},{6,7},{7,6},{8,9},{9,8},{10,11... | collective-permute-start | bytes 1769480 | tf_op jit(solution)/shard_map/ppermute | solution.py:330
  80.0 19.7 %collective-permute-start.14 = (bf16[288,512]{1,0:T(8,128)(2,1)}, bf16[288,512]{1,0:T(8,128)(2,1)S(1)}, u32[]{:S(2)}, u32[]{:S(2)}) collective-permute-start(bf16[288,512]{1,0:T(8,128)(2,1)} %get-tuple-element.23.refs_6_), channel_id=1, source_target_pairs={{0,2},{2,0},{1,3},{3,1},{4,6},{6,4},{5,7},{7,5},{8,10},{10,8},{9,1... | collective-permute-start | bytes 884744 | tf_op jit(solution)/shard_map/ppermute | solution.py:330
  85.5 14.1 %collective-permute-start.15 = (bf16[288,512]{1,0:T(8,128)(2,1)}, bf16[288,512]{1,0:T(8,128)(2,1)}, u32[]{:S(2)}, u32[]{:S(2)}) collective-permute-start(bf16[288,512]{1,0:T(8,128)(2,1)} %get-tuple-element.24.refs_7_), channel_id=1, source_target_pairs={{0,2},{2,0},{1,3},{3,1},{4,6},{6,4},{5,7},{7,5},{8,10},{10,8},{9,1... | collective-permute-start | bytes 884744 | tf_op jit(solution)/shard_map/ppermute | solution.py:330
  90.1 12.7 %collective-permute-start.13 = (bf16[288,512]{1,0:T(8,128)(2,1)}, bf16[288,512]{1,0:T(8,128)(2,1)}, u32[]{:S(2)}, u32[]{:S(2)}) collective-permute-start(bf16[288,512]{1,0:T(8,128)(2,1)} %get-tuple-element.22.refs_5_), channel_id=1, source_target_pairs={{0,2},{2,0},{1,3},{3,1},{4,6},{6,4},{5,7},{7,5},{8,10},{10,8},{9,1... | collective-permute-start | bytes 884744 | tf_op jit(solution)/shard_map/ppermute | solution.py:330
  97.5 18.5 %collective-permute-start.12 = (bf16[288,512]{1,0:T(8,128)(2,1)}, bf16[288,512]{1,0:T(8,128)(2,1)S(1)}, u32[]{:S(2)}, u32[]{:S(2)}) collective-permute-start(bf16[288,512]{1,0:T(8,128)(2,1)} %get-tuple-element.21.refs_8_), channel_id=1, source_target_pairs={{0,2},{2,0},{1,3},{3,1},{4,6},{6,4},{5,7},{7,5},{8,10},{10,8},{9,1... | collective-permute-start | bytes 884744 | tf_op jit(solution)/shard_map/ppermute | solution.py:330
  98.2 28.9 %collective-permute-start.2 = (bf16[4,144,576]{2,1,0:T(8,128)(2,1)S(1)}, bf16[4,144,576]{2,1,0:T(8,128)(2,1)S(1)}, u32[]{:S(2)}, u32[]{:S(2)}) collective-permute-start(bf16[4,144,576]{2,1,0:T(8,128)(2,1)S(1)} %all-to-all-done), channel_id=1, source_target_pairs={{0,16},{16,0},{1,17},{17,1},{2,18},{18,2},{3,19},{19,3},{4,20},{20... | collective-permute-start | bytes 1990664 | tf_op jit(solution)/shard_map/ppermute | solution.py:330
  99.7 3.2 %copy-start.4 = (bf16[288,512]{1,0:T(8,128)(2,1)}, bf16[288,512]{1,0:T(8,128)(2,1)S(1)}, u32[]{:S(2)}) copy-start(bf16[288,512]{1,0:T(8,128)(2,1)S(1)} %collective-permute-done.14.refs_10_) | copy-start | bytes 884740
  116.0 0.7 copy-start.3
  122.6 20.2 %all-to-all-start.2 = ((bf16[4,144,512]{2,1,0:T(8,128)(2,1)}), bf16[4,144,512]{2,1,0:T(8,128)(2,1)}, u32[]{:S(2)}, u32[]{:S(2)}) async-start(bf16[4,144,512]{2,1,0:T(8,128)(2,1)} %shard_map.62), calls=%async_computation.2 | async-start | bytes 1179648 | tf_op jit(solution)/shard_map/all_to_all | solution.py:495
  127.4 16.1 %copy-start.1 = (bf16[1,512,1152]{2,1,0:T(8,128)(2,1)S(1)}, bf16[1,512,1152]{2,1,0:T(8,128)(2,1)}, u32[]{:S(2)}) copy-start(bf16[1,512,1152]{2,1,0:T(8,128)(2,1)} %param.5) | copy-start | bytes 3538948
  128.7 17.2 %collective-permute-start.3 = (bf16[576,576]{1,0:T(8,128)(2,1)}, bf16[576,576]{1,0:T(8,128)(2,1)}, u32[]{:S(2)}, u32[]{:S(2)}) collective-permute-start(bf16[576,576]{1,0:T(8,128)(2,1)} %get-tuple-element.27), channel_id=1, source_target_pairs={{0,1},{1,0},{2,3},{3,2},{4,5},{5,4},{6,7},{7,6},{8,9},{9,8},{10,11... | collective-permute-start | bytes 1990664 | tf_op jit(solution)/shard_map/ppermute | solution.py:330
  142.8 3.2 %collective-permute-start.16 = (bf16[576,512]{1,0:T(8,128)(2,1)}, bf16[576,512]{1,0:T(8,128)(2,1)}, u32[]{:S(2)}, u32[]{:S(2)}) collective-permute-start(bf16[576,512]{1,0:T(8,128)(2,1)} %bitcast.14.near_ref), channel_id=1, source_target_pairs={{0,1},{1,0},{2,3},{3,2},{4,5},{5,4},{6,7},{7,6},{8,9},{9,8},{10,11... | collective-permute-start | bytes 1769480 | tf_op jit(solution)/shard_map/ppermute | solution.py:330

commit v3 on v2

--- a/solution.py
+++ b/solution.py
@@ -8,7 +8,7 @@
 from jax.experimental.pallas import tpu as pltpu
 from jax.sharding import PartitionSpec as P
 
-VMEM_LIMIT = 56 * 2**20
+MIB = 2**20
 
 
 def dot_nn(a, b):
@@ -19,7 +19,7 @@
     return lax.dot_general(a, b, (((1,), (1,)), ((), ())), preferred_element_type=jnp.float32)
 
 
-def call(kernel, out_shape, operands, scratch=(), flops=0, moved=0, left=()):
+def call(kernel, out_shape, operands, scratch=(), flops=0, moved=0, left=(), grant=8):
     smem = pl.BlockSpec(memory_space=pltpu.SMEM)
     vmem = pl.BlockSpec(memory_space=pltpu.VMEM)
     where = pl.BlockSpec(memory_space=pl.ANY)
@@ -30,7 +30,7 @@
         in_specs=[where if i in left else smem if x.dtype == jnp.int32 else vmem for i, x in enumerate(operands)],
         out_specs=[vmem] * len(out_shape) if many else vmem,
         scratch_shapes=list(scratch),
-        compiler_params=pltpu.CompilerParams(vmem_limit_bytes=VMEM_LIMIT),
+        compiler_params=pltpu.CompilerParams(vmem_limit_bytes=grant * MIB),
         cost_estimate=pl.CostEstimate(flops=flops, bytes_accessed=moved, transcendentals=0),
     )(*operands)
 
@@ -62,73 +62,55 @@
     )
 
 
-def weight_kernel(heads, head_dim, group_ref, mine_ref, partner_ref, out_ref):
-    parts = []
-    for ref in (mine_ref, partner_ref):
-        pieces = [ref[source].astype(jnp.float32) for source in range(ref.shape[0])]
-        parts.append(jnp.concatenate(pieces, 1))
-    swap = group_ref[0] == 1
-    per_head = (jnp.where(swap, parts[1], parts[0]), jnp.where(swap, parts[0], parts[1]))
+def weight_kernel(heads, head_dim, parts_ref, out_ref):
+    _, count, part_rows, share = parts_ref.shape
+    head_rows = 3 * head_dim
+    per_head = []
+    for head in range(heads):
+        low, high = [
+            jnp.concatenate([parts_ref[head * 2 + i, source].astype(jnp.float32) for source in range(count)], 1)
+            for i in range(2)
+        ]
+        per_head.append(jnp.concatenate([low, high[2 * part_rows - head_rows :]], 0))
     rows = [w[kind * head_dim : (kind + 1) * head_dim] for kind in (1, 2, 0) for w in per_head]
     out_ref[...] = jnp.concatenate(rows, 0).astype(jnp.bfloat16)
 
 
-def join_weight(group, mine, partner, heads, head_dim):
-    count, part_rows, share = mine.shape
-    out = (2 * part_rows, count * share)
+def join_weight(parts, heads, head_dim):
+    _, count, _, share = parts.shape
+    out = (heads * 3 * head_dim, count * share)
     return call(
         functools.partial(weight_kernel, heads, head_dim),
         jax.ShapeDtypeStruct(out, jnp.bfloat16),
-        (group, mine, partner),
+        (parts,),
         flops=4 * out[0] * out[1],
         moved=4 * out[0] * out[1],
-    )
-
-
-def project_kernel(kv_width, sources, *refs):
-    pick_ref, weight_ref = refs[0], refs[1]
-    pairs = [refs[2 + 2 * i : 4 + 2 * i] for i in range(sources)]
-    kv_ref, q_ref, hidden, arrived = refs[2 + 2 * sources :]
-    half = pairs[0][0].shape[0]
-    starts = (pl.multiple_of(pick_ref[0] * half, half), pl.multiple_of((1 - pick_ref[0]) * half, half))
-
-    def copies(pair):
-        return [
-            pltpu.make_async_copy(ref, hidden.at[pl.ds(start, half), :], arrived.at[i])
-            for i, (ref, start) in enumerate(zip(pair, starts))
-        ]
-
-    for i, pair in enumerate(pairs):
-        def fetch(pair=pair):
-            for copy in copies(pair):
-                copy.start()
-        if sources == 1:
-            fetch()
-        else:
-            pl.when(pick_ref[1] == i)(fetch)
-    for copy in copies(pairs[0]):
-        copy.wait()
-    mixed = dot_nt(weight_ref[...], hidden[...]).astype(jnp.bfloat16)
-    kv_ref[...] = mixed[:kv_width]
-    q_ref[...] = mixed[kv_width:]
-
-
-def project(pick, sources, weight, kv_width):
-    half, width = sources[0][0].shape
+        grant=16,
+    )
+
+
+def project_kernel(kv_width, place_ref, weight_ref, mine_ref, other_ref, kv_ref, q_ref):
+    half = mine_ref.shape[0]
+    for part, ref in ((place_ref[0], mine_ref), (1 - place_ref[0], other_ref)):
+        span = pl.ds(pl.multiple_of(part * half, half), half)
+        mixed = dot_nt(weight_ref[...], ref[...]).astype(jnp.bfloat16)
+        kv_ref[:, span] = mixed[:kv_width]
+        q_ref[:, span] = mixed[kv_width:]
+
+
+def project(place, weight, mine, other, kv_width):
+    half, width = mine.shape
     rows = 2 * half
     out_width = weight.shape[0]
-    flat = [block for pair in sources for block in pair]
     return call(
-        functools.partial(project_kernel, kv_width, len(sources)),
+        functools.partial(project_kernel, kv_width),
         (
             jax.ShapeDtypeStruct((kv_width, rows), jnp.bfloat16),
             jax.ShapeDtypeStruct((out_width - kv_width, rows), jnp.bfloat16),
         ),
-        (pick, weight, *flat),
-        [pltpu.VMEM((rows, width), jnp.bfloat16), pltpu.SemaphoreType.DMA((2,))],
+        (place, weight, mine, other),
         flops=2 * rows * width * out_width,
         moved=2 * (rows * width + width * out_width + rows * out_width),
-        left=range(2, 2 + len(flat)),
     )
 
 
@@ -289,6 +271,7 @@
         ],
         flops=3 * count * heads * rows * 2 * rows * head_dim * 16,
         moved=2 * count * heads * head_dim * rows * 6,
+        grant=24,
     )
     return call(
         functools.partial(second_kernel, count, heads, head_dim),
@@ -307,12 +290,53 @@
         ],
         flops=heads * rows * rows * head_dim * 16,
         moved=2 * count * heads * head_dim * rows * 6,
-    )
+        grant=16,
+    )
+
+
+def residual_kernel(core_ref, frame_ref, mod_ref, out_ref, gate_ref):
+    width = out_ref.shape[0]
+    frame = frame_ref[...].astype(jnp.float32)
+    mine = jnp.where(core_ref[0] == 0, frame[:, :width], frame[:, width:])
+    out_ref[...] = mine.T.astype(jnp.bfloat16)
+    gate = jnp.broadcast_to(mod_ref[2:3, :], (8, 2 * width))
+    gate = jnp.where(core_ref[0] == 0, gate[:, :width], gate[:, width:])
+    gate_ref[...] = gate.T
+
+
+def residual(core, frame, modulation):
+    rows, width = frame.shape
+    return call(
+        residual_kernel,
+        (jax.ShapeDtypeStruct((width // 2, rows), jnp.bfloat16), jax.ShapeDtypeStruct((width // 2, 8), jnp.float32)),
+        (core, frame, modulation),
+        flops=4 * rows * width,
+        moved=3 * rows * width,
+        grant=16,
+    )
+
+
+def order_kernel(where_ref, mine_ref, other_ref, near_ref, send_ref):
+    group, core = where_ref[1], where_ref[3]
+    block = mine_ref.shape[1]
+    per_core = mine_ref.shape[0] // 2
+    for same, ref in ((True, mine_ref), (False, other_ref)):
+        half = group if same else 1 - group
+        for index in range(per_core):
+            start = pl.multiple_of((index * 2 + half) * block, block)
+            near_ref[pl.ds(start, block), :] = ref[core * per_core + index]
+            send_ref[pl.ds(start, block), :] = ref[(1 - core) * per_core + index]
+
+
+def order_columns(where, mine, other):
+    count, block, depth = mine.shape
+    out = jax.ShapeDtypeStruct((count * block, depth), mine.dtype)
+    return call(order_kernel, (out, out), (where, mine, other), moved=8 * mine.size, grant=8)
 
 
 def finish_kernel(near_w, far_w, near_ref, far_ref, frame_ref, gate_ref, out_ref):
     projected = dot_nn(near_w[...], near_ref[...]) + dot_nn(far_w[...], far_ref[...])
-    updated = frame_ref[...].astype(jnp.float32) + gate_ref[...] * projected
+    updated = frame_ref[...].astype(jnp.float32) + gate_ref[:, 0:1] * projected
     out_ref[...] = updated.astype(jnp.bfloat16)
 
 
@@ -323,6 +347,7 @@
         (near_w, far_w, near, far, frame_part, gate_part),
         flops=4 * near_w.shape[0] * near_w.shape[1] * near.shape[1],
         moved=4 * (near_w.size + near.size + frame_part.size),
+        grant=16,
     )
 
 
@@ -447,6 +472,10 @@
     return result.reshape(frame_count, row_count, half_width)
 
 
+def flipped(block, axis, distance):
+    return lax.ppermute(block, axis, [(i, i ^ distance) for i in range(lax.axis_size(axis))])
+
+
 def after(block, other):
     return lax.optimization_barrier((block, other))[0]
 
@@ -461,53 +490,43 @@
     group = lax.axis_index("groups")
     frame = frames[0]
     place = core.reshape(1).astype(jnp.int32)
-    middle = count // 2
+
+    tok = lax.axis_index("tok")
+    where = jnp.stack([me, group, tok, core]).astype(jnp.int32)
 
     blocks = jnp.transpose(w_qkv, (1, 2, 3, 0)).reshape(count, heads, 3 * head_dim, share)
-    part = lax.dynamic_index_in_dim(blocks, group, 1, keepdims=False)
+    part_rows = -(-3 * head_dim // 32) * 16
+    start = tok * (3 * head_dim - part_rows)
+    part = lax.dynamic_slice(blocks, (0, group, start, 0), (count, 1, part_rows, share))[:, 0]
     part = lax.all_to_all(part, "frame", 0, 0)
-    weight = join_weight(group.reshape(1).astype(jnp.int32), part, swapped(part, "groups"), heads, head_dim)
+    plane = lax.all_to_all(jnp.broadcast_to(part[None], (4, *part.shape)), ("groups", "tok"), 0, 0)
+    weight = join_weight(plane, heads, head_dim)
     kv_width = 2 * heads * head_dim
 
     mine = norm_half(place, frame, modulation)
-    across = lax.ppermute(mine, "frame", [(i, i ^ middle) for i in range(count)])
-    right = lax.ppermute(mine, "frame", [(i, i + 1) for i in range(count - 1)])
-    left = lax.ppermute(mine, "frame", [(i + 1, i) for i in range(count - 1)])
-    ends = lax.ppermute(across, "frame", [(count - 2, count - 1), (1, 0)])
-    pairs = {name: (block, swapped(block, "head")) for name, block in (("own", mine), ("right", right), ("left", left), ("across", across), ("ends", ends))}
-
-    at_end = (me == 0) | (me == count - 1)
-    slots = (
-        (me, 0, ("own",)),
-        (jnp.where(me == 0, 1, me - 1), jnp.where(me == 0, 1, 0), ("right", "left")),
-        (me ^ middle, 0, ("across",)),
-        (jnp.where(at_end, count - 1 - me, me + 1), jnp.where(at_end, 1, 0), ("left", "ends")),
-    )
+    arrivals = [mine, flipped(mine, "frame", 1), flipped(mine, "frame", 2)]
+    arrivals.append(flipped(arrivals[2], "frame", 1))
+    frame_part, gate_part = residual(place, after(frame, arrivals[1]), modulation)
+
     queries, near, far = [], [], []
-    for _, pick, names in slots:
-        picked = jnp.stack([core, pick]).astype(jnp.int32)
-        kv, q = project(picked, [pairs[name] for name in names], weight, kv_width)
+    for distance, block in enumerate(arrivals):
+        if distance == 3:
+            block = after(block, (frame_part, near[0], near[1]))
+        kv, q = project(place, weight, block, swapped(block, "head"), kv_width)
         queries.append(q)
         near.append(kv)
         far.append(swapped(kv, "tok"))
-    ids = jnp.stack([index for index, _, _ in slots] + [anchor_offsets[0]]).astype(jnp.int32)
+    ids = jnp.stack([me ^ distance for distance in range(count)] + [anchor_offsets[0]]).astype(jnp.int32)
     attended = attend_all(ids, queries, near, far, heads, head_dim)
     arrived = lax.all_to_all(attended, "frame", 0, 0).reshape(count * heads * head_dim, rows)
     arrived_far = swapped(arrived, "head")
 
-    out_half = width // 2
     columns = w_out.shape[1] // 2
     w_part = lax.dynamic_slice_in_dim(w_out.T, group * columns, columns, 0)
-    w_part = after(w_part, ends)
+    w_part = after(w_part, near[-1])
     w_part = lax.all_to_all(jnp.broadcast_to(w_part[None], (count, *w_part.shape)), "frame", 0, 0)
-    w_other = swapped(w_part, "groups")
-    w_first = jnp.where(group == 0, w_part, w_other)
-    w_second = jnp.where(group == 0, w_other, w_part)
-    w_cols = jnp.concatenate([w_first, w_second], 1).reshape(width, w_out.shape[0])
-    near_w = lax.dynamic_slice_in_dim(w_cols, core * out_half, out_half, 0)
-    far_w = swapped(lax.dynamic_slice_in_dim(w_cols, (1 - core) * out_half, out_half, 0), "head")
-    frame_part = lax.dynamic_slice_in_dim(frame, core * out_half, out_half, 1).T
-    gate_part = lax.dynamic_slice_in_dim(modulation[2], core * out_half, out_half, 0)[:, None]
+    near_w, send_w = order_columns(where, w_part, swapped(w_part, "groups"))
+    far_w = swapped(send_w, "head")
     updated = finish(near_w, far_w, arrived, arrived_far, frame_part, gate_part)
     return updated.T[None]
 

time: 151 us -> 126 us (0.83)
  Pallas kernels: 44.5 us -> 31.8 us
  starting transfers between devices: 36.1 us -> 28.7 us
  waiting for transfers between devices: 54.6 us -> 51.9 us
    ppermute x13 -> x11, waiting for transfers between devices: 3.18 us -> 26 us  [swapped(): return lax.ppermute(block, axis, [(0, 1), (1, 0)])]
    all_to_all x1, waiting for transfers between devices: 14.1 us -> 0.01 us  [by_heads(): lax.all_to_all(attended, 'frame', 0, 0)]
    pallas_call x9 -> x11, Pallas kernels: 44.5 us -> 31.8 us  [call(): pl.pallas_call(kernel, out_shape=out_shape, in_specs=[where if i in left...]
    ppermute x4 -> x3, waiting for transfers between devices: 32.4 us -> 20.2 us  [flipped(): lax.ppermute(block, axis, [(i, i ^ distance) for i in range(lax.axis_size...]
    ppermute x4 -> x3, starting transfers between devices: 12.1 us -> 4.45 us  [flipped(): lax.ppermute(block, axis, [(i, i ^ distance) for i in range(lax.axis_size...]
    unnamed x11 -> x17, local copies, waits for them, and re-layouts: 1.82 us -> 7.12 us
    all_to_all x0 -> x1, starting transfers between devices: none -> 4.29 us  [by_heads(): lax.all_to_all(jnp.broadcast_to(part[None], (4, *part.shape)), ('groups',...]
    ppermute x13 -> x11, starting transfers between devices: 8.68 us -> 5.1 us  [swapped(): return lax.ppermute(block, axis, [(0, 1), (1, 0)])]
  transfers between devices with their start and end apart: 20 -> 18, of which waited for: 6 -> 8; matrix products, arithmetic and copies ran while one was open for 9% -> 5% of each run, Pallas kernels for 25% -> 24%
where the time goes in v3:
time: 126 us
  waiting for transfers between devices  51.9 us (41%)
  Pallas kernels  31.8 us (25%)
  starting transfers between devices  28.7 us (23%)
  local copies, waits for them, and re-layouts  12.8 us (10%)
    pallas_call x11, Pallas kernels, call(): pl.pallas_call(kernel, out_shape=out_shape, in_specs=[where if i in left...  31.8 us
    ppermute x11, waiting for transfers between devices, swapped(): return lax.ppermute(block, axis, [(0, 1), (1, 0)])  26 us
    ppermute x3, waiting for transfers between devices, flipped(): lax.ppermute(block, axis, [(i, i ^ distance) for i in range(lax.axis_size...  20.2 us
    unnamed x17, local copies, waits for them, and re-layouts  7.12 us
    all_to_all x1, starting transfers between devices, by_heads(): part = lax.all_to_all(part, 'frame', 0, 0)  6.32 us
    all_to_all x1, waiting for transfers between devices, by_heads(): part = lax.all_to_all(part, 'frame', 0, 0)  5.71 us
    ppermute x11, starting transfers between devices, swapped(): return lax.ppermute(block, axis, [(0, 1), (1, 0)])  5.1 us
    all_to_all x1, starting transfers between devices, by_heads(): lax.all_to_all(jnp.broadcast_to(w_part[None], (count, *w_part.shape)), 'f...  4.55 us
  transfers between devices with their start and end apart: 18, of which 8 were waited for; matrix products, arithmetic and copies ran while one was open for 5% of the time, Pallas kernels for 24%

profile of v3, /device:TPU:0, one launch (start us, length us, event | category | flops | bytes accessed | tf_op | source)
XLA Modules:
  0.0 126.0 jit_solution(8505055600030847485)
XLA Ops:
  0.0 0.0 copy-start
  0.0 1.3 %copy-done = bf16[288,8,3,72]{0,3,2,1:T(8,128)(2,1)S(1)} copy-done((bf16[288,8,3,72]{0,3,2,1:T(8,128)(2,1)S(1)}, bf16[288,8,3,72]{0,3,2,1:T(8,128)(2,1)}, u32[]{:S(2)}) %copy-start) | copy-done | bytes 995352
  1.4 0.9 copy.8
  2.3 6.3 %all-to-all-start = ((bf16[4,112,288]{1,2,0:T(8,128)(2,1)}), bf16[4,112,288]{1,2,0:T(8,128)(2,1)S(1)}, u32[]{:S(2)}, u32[]{:S(2)}) async-start(bf16[4,112,288]{1,2,0:T(8,128)(2,1)} %bitcast.7), calls=%async_computation | async-start | bytes 589824 | tf_op jit(solution)/shard_map/all_to_all | solution.py:501
  8.6 0.0 copy-done.2
  8.6 0.0 copy-done.7
  8.6 0.5 shard_map.56.mine_ref
  9.1 2.1 %collective-permute-start.2 = (bf16[256,1152]{1,0:T(8,128)(2,1)S(1)}, bf16[256,1152]{1,0:T(8,128)(2,1)}, u32[]{:S(2)}, u32[]{:S(2)}) collective-permute-start(bf16[256,1152]{1,0:T(8,128)(2,1)S(1)} %shard_map.56.mine_ref), channel_id=1, source_target_pairs={{0,4},{4,0},{8,12},{12,8},{1,5},{5,1},{9,13},{13,9},{2,6},{6,2},{1... | collective-permute-start | bytes 1769480 | tf_op jit(solution)/shard_map/ppermute | solution.py:476
  11.2 2.4 %collective-permute-start = (bf16[256,1152]{1,0:T(8,128)(2,1)S(1)}, bf16[256,1152]{1,0:T(8,128)(2,1)}, u32[]{:S(2)}, u32[]{:S(2)}) collective-permute-start(bf16[256,1152]{1,0:T(8,128)(2,1)S(1)} %shard_map.56.mine_ref), channel_id=1, source_target_pairs={{0,8},{4,12},{8,0},{12,4},{1,9},{5,13},{9,1},{13,5},{2,10},{6,14},... | collective-permute-start | bytes 1769480 | tf_op jit(solution)/shard_map/ppermute | solution.py:476
  13.6 5.7 %all-to-all-done = bf16[4,112,288]{1,2,0:T(8,128)(2,1)S(1)} async-done(((bf16[4,112,288]{1,2,0:T(8,128)(2,1)}), bf16[4,112,288]{1,2,0:T(8,128)(2,1)S(1)}, u32[]{:S(2)}, u32[]{:S(2)}) %all-to-all-start) | async-done | bytes 258080 | tf_op jit(solution)/shard_map/all_to_all | solution.py:501
  19.3 1.2 broadcast_in_dim.6
  20.4 4.3 %all-to-all-start.1 = ((bf16[4,4,112,288]{2,3,1,0:T(8,128)(2,1)}), bf16[4,4,112,288]{2,3,1,0:T(8,128)(2,1)}, u32[]{:S(2)}, u32[]{:S(2)}) async-start(bf16[4,4,112,288]{2,3,1,0:T(8,128)(2,1)} %broadcast_in_dim.6), calls=%async_computation.1 | async-start | bytes 2359296 | tf_op jit(solution)/shard_map/all_to_all | solution.py:502
  24.7 0.1 collective-permute-start.3
  24.8 15.7 %collective-permute-done.2.mine_ref = bf16[256,1152]{1,0:T(8,128)(2,1)} collective-permute-done((bf16[256,1152]{1,0:T(8,128)(2,1)S(1)}, bf16[256,1152]{1,0:T(8,128)(2,1)}, u32[]{:S(2)}, u32[]{:S(2)}) %collective-permute-start.2) | collective-permute-done | bytes 589856 | tf_op jit(solution)/shard_map/ppermute | solution.py:476
  40.5 0.0 collective-permute-start.4
  40.5 3.1 %collective-permute-done.mine_ref = bf16[256,1152]{1,0:T(8,128)(2,1)} collective-permute-done((bf16[256,1152]{1,0:T(8,128)(2,1)S(1)}, bf16[256,1152]{1,0:T(8,128)(2,1)}, u32[]{:S(2)}, u32[]{:S(2)}) %collective-permute-start) | collective-permute-done | bytes 589856 | tf_op jit(solution)/shard_map/ppermute | solution.py:476
  43.6 0.0 collective-permute-start.1
  43.6 0.0 collective-permute-start.8
  43.6 0.5 shard_map.57
  44.1 0.0 copy-start.3
  44.1 0.8 copy-done.3
  44.9 0.7 copy-done.5
  45.7 0.0 all-to-all-done.1
  45.7 2.5 %copy.7.parts_ref = bf16[4,4,112,288]{3,2,1,0:T(8,128)(2,1)} copy(bf16[4,4,112,288]{2,3,1,0:T(8,128)(2,1)} %all-to-all-done.1) | data formatting | bytes 2064384 | tf_op jit(solution)/shard_map/all_to_all | solution.py:502
  48.2 1.3 %copy-done.1 = bf16[4,4,112,288]{3,2,1,0:T(8,128)(2,1)S(1)} copy-done((bf16[4,4,112,288]{3,2,1,0:T(8,128)(2,1)S(1)}, bf16[4,4,112,288]{3,2,1,0:T(8,128)(2,1)}, u32[]{:S(2)}) %copy-start.1) | copy-done | bytes 1032216
  49.5 0.3 shard_map.55.weight_ref
  49.8 0.0 collective-permute-done.3.other_ref
  49.9 2.5 %shard_map.58 = (bf16[288,512]{1,0:T(8,128)(2,1)}, bf16[144,512]{1,0:T(8,128)(2,1)S(1)}) custom-call(s32[1]{0:T(128)} %bitcast.3.place_ref.core_ref, bf16[432,1152]{1,0:T(8,128)(2,1)S(1)} %shard_map.55.weight_ref, bf16[256,1152]{1,0:T(8,128)(2,1)S(1)} %shard_map.56.mine_ref, bf16[256,1152]{1,0:T(8,128)(2,1)} %collective-permute-done.3.other_ref), custom_call_target="tpu_custom_call" | custom-call | flops 509607936 | bytes 2617344 | tf_op jit(solution)/shard_map/pallas_call | solution.py:27
  52.4 0.0 collective-permute-done.4.other_ref
  52.4 2.7 %shard_map.59 = (bf16[288,512]{1,0:T(8,128)(2,1)}, bf16[144,512]{1,0:T(8,128)(2,1)S(1)}) custom-call(s32[1]{0:T(128)} %bitcast.3.place_ref.core_ref, bf16[432,1152]{1,0:T(8,128)(2,1)S(1)} %shard_map.55.weight_ref, bf16[256,1152]{1,0:T(8,128)(2,1)} %collective-permute-done.2.mine_ref, bf16[256,1152]{1,0:T(8,128)(2,1)} %collective-permute-done.4.other_ref), custom_call_target="tpu_custom_call" | custom-call | flops 509607936 | bytes 2617344 | tf_op jit(solution)/shard_map/pallas_call | solution.py:27
  55.1 1.5 %collective-permute-done.1.mine_ref = bf16[256,1152]{1,0:T(8,128)(2,1)} collective-permute-done((bf16[256,1152]{1,0:T(8,128)(2,1)}, bf16[256,1152]{1,0:T(8,128)(2,1)}, u32[]{:S(2)}, u32[]{:S(2)}) %collective-permute-start.1) | collective-permute-done | bytes 589856 | tf_op jit(solution)/shard_map/ppermute | solution.py:476
  56.5 0.0 collective-permute-start.5
  56.5 1.5 %collective-permute-start.10 = (bf16[288,512]{1,0:T(8,128)(2,1)}, bf16[288,512]{1,0:T(8,128)(2,1)}, u32[]{:S(2)}, u32[]{:S(2)}) collective-permute-start(bf16[288,512]{1,0:T(8,128)(2,1)} %get-tuple-element.24.refs_5_), channel_id=1, source_target_pairs={{0,2},{2,0},{1,3},{3,1},{4,6},{6,4},{5,7},{7,5},{8,10},{10,8},{9,1... | collective-permute-start | bytes 884744 | tf_op jit(solution)/shard_map/ppermute | solution.py:355
  58.0 0.5 collective-permute-start.11
  58.6 0.0 collective-permute-done.8.other_ref
  58.6 2.7 %shard_map.62 = (bf16[288,512]{1,0:T(8,128)(2,1)}, bf16[144,512]{1,0:T(8,128)(2,1)S(1)}) custom-call(s32[1]{0:T(128)} %bitcast.3.place_ref.core_ref, bf16[432,1152]{1,0:T(8,128)(2,1)S(1)} %shard_map.55.weight_ref, bf16[256,1152]{1,0:T(8,128)(2,1)} %collective-permute-done.mine_ref, bf16[256,1152]{1,0:T(8,128)(2,1)} %collective-permute-done.8.other_ref), custom_call_target="tpu_custom_call" | custom-call | flops 509607936 | bytes 2617344 | tf_op jit(solution)/shard_map/pallas_call | solution.py:27
  61.3 1.5 %collective-permute-start.12 = (bf16[288,512]{1,0:T(8,128)(2,1)}, bf16[288,512]{1,0:T(8,128)(2,1)}, u32[]{:S(2)}, u32[]{:S(2)}) collective-permute-start(bf16[288,512]{1,0:T(8,128)(2,1)} %get-tuple-element.35.refs_7_), channel_id=1, source_target_pairs={{0,2},{2,0},{1,3},{3,1},{4,6},{6,4},{5,7},{7,5},{8,10},{10,8},{9,1... | collective-permute-start | bytes 884744 | tf_op jit(solution)/shard_map/ppermute | solution.py:355
  63.4 0.1 stack.36.refs_0_
  63.5 0.9 dynamic-slice_bitcast_fusion
  64.5 0.0 collective-permute-done.5.other_ref
  64.5 2.5 %shard_map.60 = (bf16[288,512]{1,0:T(8,128)(2,1)}, bf16[144,512]{1,0:T(8,128)(2,1)S(1)}) custom-call(s32[1]{0:T(128)} %bitcast.3.place_ref.core_ref, bf16[432,1152]{1,0:T(8,128)(2,1)S(1)} %shard_map.55.weight_ref, bf16[256,1152]{1,0:T(8,128)(2,1)} %collective-permute-done.1.mine_ref, bf16[256,1152]{1,0:T(8,128)(2,1)S(1)} %collective-permute-done.5.other_ref), custom_call_target="tpu_custom_call" | custom-call | flops 509607936 | bytes 2617344 | tf_op jit(solution)/shard_map/pallas_call | solution.py:27
  67.0 0.5 collective-permute-start.9
  67.5 0.9 broadcast_in_dim.7
  68.5 4.6 %all-to-all-start.2 = ((bf16[4,144,576]{2,1,0:T(8,128)(2,1)}), bf16[4,144,576]{2,1,0:T(8,128)(2,1)S(1)}, u32[]{:S(2)}, u32[]{:S(2)}) async-start(bf16[4,144,576]{2,1,0:T(8,128)(2,1)} %broadcast_in_dim.7), calls=%async_computation.2 | async-start | bytes 1474560 | tf_op jit(solution)/shard_map/all_to_all | solution.py:527
  73.0 0.0 collective-permute-done.10.refs_9_
  73.0 0.0 collective-permute-done.11.refs_10_
  73.0 6.3 %collective-permute-done.12.refs_11_ = bf16[288,512]{1,0:T(8,128)(2,1)} collective-permute-done((bf16[288,512]{1,0:T(8,128)(2,1)}, bf16[288,512]{1,0:T(8,128)(2,1)}, u32[]{:S(2)}, u32[]{:S(2)}) %collective-permute-start.12) | collective-permute-done | bytes 294944 | tf_op jit(solution)/shard_map/ppermute | solution.py:355
  79.3 11.8 %shard_map.63 = (f32[8,1,512]{2,1,0:T(1,128)S(1)}, f32[8,80,512]{2,1,0:T(8,128)S(1)}) custom-call(s32[5]{0:T(128)S(1)} %stack.36.refs_0_, bf16[144,512]{1,0:T(8,128)(2,1)S(1)} %get-tuple-element.31.refs_1_, bf16[144,512]{1,0:T(8,128)(2,1)S(1)} %get-tuple-element.32.refs_2_, bf16[144,512]{1,0:T(8,128)(2,1)S(1)} %get-tuple-element.33.refs_3_, ...), custom_call_target="tpu_custom_call" | custom-call | flops 14495514624 | bytes 3538944 | tf_op jit(solution)/shard_map/pallas_call | solution.py:27
  91.1 0.0 collective-permute-done.9.refs_5_
  91.1 4.7 %shard_map.64 = bf16[4,144,512]{2,1,0:T(8,128)(2,1)} custom-call(s32[5]{0:T(128)S(1)} %stack.36.refs_0_, bf16[144,512]{1,0:T(8,128)(2,1)S(1)} %get-tuple-element.31.refs_1_, bf16[144,512]{1,0:T(8,128)(2,1)S(1)} %get-tuple-element.32.refs_2_, bf16[144,512]{1,0:T(8,128)(2,1)S(1)} %get-tuple-element.33.refs_3_, bf16[144,512]{1,0:T(8,128)(2,1)S(1)} %get-tuple-element.34.refs_4_, ...), custom_call_target="tpu_custom_call" | custom-call | flops 603979776 | bytes 3538944 | tf_op jit(solution)/shard_map/pallas_call | solution.py:27
  95.8 0.0 all-to-all-done.2.mine_ref
  95.8 3.9 %all-to-all-start.3 = ((bf16[4,144,512]{2,1,0:T(8,128)(2,1)}), bf16[4,144,512]{2,1,0:T(8,128)(2,1)S(1)}, u32[]{:S(2)}, u32[]{:S(2)}) async-start(bf16[4,144,512]{2,1,0:T(8,128)(2,1)} %shard_map.64), calls=%async_computation.3 | async-start | bytes 1179648 | tf_op jit(solution)/shard_map/all_to_all | solution.py:521
  99.8 0.4 collective-permute-start.6
  100.2 0.1 pad_add_fusion.where_ref
  100.3 16.9 %collective-permute-done.6.other_ref = bf16[4,144,576]{2,1,0:T(8,128)(2,1)S(1)} collective-permute-done((bf16[4,144,576]{2,1,0:T(8,128)(2,1)S(1)}, bf16[4,144,576]{2,1,0:T(8,128)(2,1)S(1)}, u32[]{:S(2)}, u32[]{:S(2)}) %collective-permute-start.6) | collective-permute-done | bytes 663584 | tf_op jit(solution)/shard_map/ppermute | solution.py:355
  117.2 1.5 %shard_map.61 = (bf16[576,576]{1,0:T(8,128)(2,1)S(1)}, bf16[576,576]{1,0:T(8,128)(2,1)}) custom-call(s32[4]{0:T(128)S(1)} %pad_add_fusion.where_ref, bf16[4,144,576]{2,1,0:T(8,128)(2,1)S(1)} %all-to-all-done.2.mine_ref, bf16[4,144,576]{2,1,0:T(8,128)(2,1)S(1)} %collective-permute-done.6.other_ref), custom_call_target="tpu_custom_call" | custom-call | bytes 2654208 | tf_op jit(solution)/shard_map/pallas_call | solution.py:27
  118.8 0.0 collective-permute-start.7
  118.8 0.0 all-to-all-done.3
  118.8 0.5 collective-permute-start.13
  119.3 2.4 %collective-permute-done.13.far_ref = bf16[576,512]{1,0:T(8,128)(2,1)S(1)} collective-permute-done((bf16[576,512]{1,0:T(8,128)(2,1)S(1)}, bf16[576,512]{1,0:T(8,128)(2,1)S(1)}, u32[]{:S(2)}, u32[]{:S(2)}) %collective-permute-start.13) | collective-permute-done | bytes 589856 | tf_op jit(solution)/shard_map/ppermute | solution.py:355
  121.7 0.3 collective-permute-done.7.far_w
  122.0 1.1 copy-done.4
  123.1 1.0 copy-done.6
  124.1 1.9 %shard_map.65 = bf16[576,512]{1,0:T(8,128)(2,1)} custom-call(bf16[576,576]{1,0:T(8,128)(2,1)S(1)} %get-tuple-element.29.near_w, bf16[576,576]{1,0:T(8,128)(2,1)S(1)} %collective-permute-done.7.far_w, bf16[576,512]{1,0:T(8,128)(2,1)S(1)} %bitcast.22, bf16[576,512]{1,0:T(8,128)(2,1)S(1)} %collective-permute-done.13.far_ref, bf16[576,512]{1,0:T(8,128)(2,1)S(1)} %copy-done.4, ...), custom_call_target="tpu_custom_call" | custom-call | flops 679477248 | bytes 3686400 | tf_op jit(solution)/shard_map/pallas_call | solution.py:27
  (7 shorter events, 0.0 us)
Async XLA Ops:
  0.0 1.3 %copy-start = (bf16[288,8,3,72]{0,3,2,1:T(8,128)(2,1)S(1)}, bf16[288,8,3,72]{0,3,2,1:T(8,128)(2,1)}, u32[]{:S(2)}) copy-start(bf16[288,8,3,72]{0,3,2,1:T(8,128)(2,1)} %param.7) | copy-start | bytes 2985988
  0.0 8.6 %copy-start.2 = (bf16[1,512,1152]{2,1,0:T(8,128)(2,1)S(1)}, bf16[1,512,1152]{2,1,0:T(8,128)(2,1)}, u32[]{:S(2)}) copy-start(bf16[1,512,1152]{2,1,0:T(8,128)(2,1)} %param.5) | copy-start | bytes 3538948
  0.0 8.6 %copy-start.7 = (f32[3,1152]{1,0:T(4,128)S(1)}, f32[3,1152]{1,0:T(4,128)}, u32[]{:S(2)}) copy-start(f32[3,1152]{1,0:T(4,128)} %mod_ref.3) | copy-start | bytes 41476
  2.3 17.0 %all-to-all-start = ((bf16[4,112,288]{1,2,0:T(8,128)(2,1)}), bf16[4,112,288]{1,2,0:T(8,128)(2,1)S(1)}, u32[]{:S(2)}, u32[]{:S(2)}) async-start(bf16[4,112,288]{1,2,0:T(8,128)(2,1)} %bitcast.7), calls=%async_computation | async-start | bytes 589824 | tf_op jit(solution)/shard_map/all_to_all | solution.py:501
  9.1 31.4 %collective-permute-start.2 = (bf16[256,1152]{1,0:T(8,128)(2,1)S(1)}, bf16[256,1152]{1,0:T(8,128)(2,1)}, u32[]{:S(2)}, u32[]{:S(2)}) collective-permute-start(bf16[256,1152]{1,0:T(8,128)(2,1)S(1)} %shard_map.56.mine_ref), channel_id=1, source_target_pairs={{0,4},{4,0},{8,12},{12,8},{1,5},{5,1},{9,13},{13,9},{2,6},{6,2},{1... | collective-permute-start | bytes 1769480 | tf_op jit(solution)/shard_map/ppermute | solution.py:476
  11.2 32.4 %collective-permute-start = (bf16[256,1152]{1,0:T(8,128)(2,1)S(1)}, bf16[256,1152]{1,0:T(8,128)(2,1)}, u32[]{:S(2)}, u32[]{:S(2)}) collective-permute-start(bf16[256,1152]{1,0:T(8,128)(2,1)S(1)} %shard_map.56.mine_ref), channel_id=1, source_target_pairs={{0,8},{4,12},{8,0},{12,4},{1,9},{5,13},{9,1},{13,5},{2,10},{6,14},... | collective-permute-start | bytes 1769480 | tf_op jit(solution)/shard_map/ppermute | solution.py:476
  20.4 25.2 %all-to-all-start.1 = ((bf16[4,4,112,288]{2,3,1,0:T(8,128)(2,1)}), bf16[4,4,112,288]{2,3,1,0:T(8,128)(2,1)}, u32[]{:S(2)}, u32[]{:S(2)}) async-start(bf16[4,4,112,288]{2,3,1,0:T(8,128)(2,1)} %broadcast_in_dim.6), calls=%async_computation.1 | async-start | bytes 2359296 | tf_op jit(solution)/shard_map/all_to_all | solution.py:502
  24.7 25.1 %collective-permute-start.3 = (bf16[256,1152]{1,0:T(8,128)(2,1)S(1)}, bf16[256,1152]{1,0:T(8,128)(2,1)}, u32[]{:S(2)}, u32[]{:S(2)}) collective-permute-start(bf16[256,1152]{1,0:T(8,128)(2,1)S(1)} %shard_map.56.mine_ref), channel_id=1, source_target_pairs={{0,1},{1,0},{2,3},{3,2},{4,5},{5,4},{6,7},{7,6},{8,9},{9,8},{10,11... | collective-permute-start | bytes 1769480 | tf_op jit(solution)/shard_map/ppermute | solution.py:355
  40.5 11.9 %collective-permute-start.4 = (bf16[256,1152]{1,0:T(8,128)(2,1)}, bf16[256,1152]{1,0:T(8,128)(2,1)}, u32[]{:S(2)}, u32[]{:S(2)}) collective-permute-start(bf16[256,1152]{1,0:T(8,128)(2,1)} %collective-permute-done.2.mine_ref), channel_id=1, source_target_pairs={{0,1},{1,0},{2,3},{3,2},{4,5},{5,4},{6,7},{7,6},{8,9},{9,8},{10,11... | collective-permute-start | bytes 1769480 | tf_op jit(solution)/shard_map/ppermute | solution.py:355
  43.6 13.0 %collective-permute-start.1 = (bf16[256,1152]{1,0:T(8,128)(2,1)}, bf16[256,1152]{1,0:T(8,128)(2,1)}, u32[]{:S(2)}, u32[]{:S(2)}) collective-permute-start(bf16[256,1152]{1,0:T(8,128)(2,1)} %collective-permute-done.mine_ref), channel_id=1, source_target_pairs={{0,4},{4,0},{8,12},{12,8},{1,5},{5,1},{9,13},{13,9},{2,6},{6,2},{1... | collective-permute-start | bytes 1769480 | tf_op jit(solution)/shard_map/ppermute | solution.py:476
  43.6 15.0 %collective-permute-start.8 = (bf16[256,1152]{1,0:T(8,128)(2,1)}, bf16[256,1152]{1,0:T(8,128)(2,1)}, u32[]{:S(2)}, u32[]{:S(2)}) collective-permute-start(bf16[256,1152]{1,0:T(8,128)(2,1)} %collective-permute-done.mine_ref), channel_id=1, source_target_pairs={{0,1},{1,0},{2,3},{3,2},{4,5},{5,4},{6,7},{7,6},{8,9},{9,8},{10,11... | collective-permute-start | bytes 1769480 | tf_op jit(solution)/shard_map/ppermute | solution.py:355
  44.1 0.8 copy-start.3
  44.9 0.7 copy-start.5
  48.2 1.3 %copy-start.1 = (bf16[4,4,112,288]{3,2,1,0:T(8,128)(2,1)S(1)}, bf16[4,4,112,288]{3,2,1,0:T(8,128)(2,1)}, u32[]{:S(2)}) copy-start(bf16[4,4,112,288]{3,2,1,0:T(8,128)(2,1)} %copy.7.parts_ref) | copy-start | bytes 3096580
  56.5 7.9 %collective-permute-start.5 = (bf16[256,1152]{1,0:T(8,128)(2,1)}, bf16[256,1152]{1,0:T(8,128)(2,1)S(1)}, u32[]{:S(2)}, u32[]{:S(2)}) collective-permute-start(bf16[256,1152]{1,0:T(8,128)(2,1)} %collective-permute-done.1.mine_ref), channel_id=1, source_target_pairs={{0,1},{1,0},{2,3},{3,2},{4,5},{5,4},{6,7},{7,6},{8,9},{9,8},{10,11... | collective-permute-start | bytes 1769480 | tf_op jit(solution)/shard_map/ppermute | solution.py:355
  56.5 16.5 %collective-permute-start.10 = (bf16[288,512]{1,0:T(8,128)(2,1)}, bf16[288,512]{1,0:T(8,128)(2,1)}, u32[]{:S(2)}, u32[]{:S(2)}) collective-permute-start(bf16[288,512]{1,0:T(8,128)(2,1)} %get-tuple-element.24.refs_5_), channel_id=1, source_target_pairs={{0,2},{2,0},{1,3},{3,1},{4,6},{6,4},{5,7},{7,5},{8,10},{10,8},{9,1... | collective-permute-start | bytes 884744 | tf_op jit(solution)/shard_map/ppermute | solution.py:355
  58.0 15.0 %collective-permute-start.11 = (bf16[288,512]{1,0:T(8,128)(2,1)}, bf16[288,512]{1,0:T(8,128)(2,1)}, u32[]{:S(2)}, u32[]{:S(2)}) collective-permute-start(bf16[288,512]{1,0:T(8,128)(2,1)} %get-tuple-element.25.refs_6_), channel_id=1, source_target_pairs={{0,2},{2,0},{1,3},{3,1},{4,6},{6,4},{5,7},{7,5},{8,10},{10,8},{9,1... | collective-permute-start | bytes 884744 | tf_op jit(solution)/shard_map/ppermute | solution.py:355
  61.3 18.0 %collective-permute-start.12 = (bf16[288,512]{1,0:T(8,128)(2,1)}, bf16[288,512]{1,0:T(8,128)(2,1)}, u32[]{:S(2)}, u32[]{:S(2)}) collective-permute-start(bf16[288,512]{1,0:T(8,128)(2,1)} %get-tuple-element.35.refs_7_), channel_id=1, source_target_pairs={{0,2},{2,0},{1,3},{3,1},{4,6},{6,4},{5,7},{7,5},{8,10},{10,8},{9,1... | collective-permute-start | bytes 884744 | tf_op jit(solution)/shard_map/ppermute | solution.py:355
  67.0 24.1 %collective-permute-start.9 = (bf16[288,512]{1,0:T(8,128)(2,1)}, bf16[288,512]{1,0:T(8,128)(2,1)S(1)}, u32[]{:S(2)}, u32[]{:S(2)}) collective-permute-start(bf16[288,512]{1,0:T(8,128)(2,1)} %get-tuple-element.27.refs_8_), channel_id=1, source_target_pairs={{0,2},{2,0},{1,3},{3,1},{4,6},{6,4},{5,7},{7,5},{8,10},{10,8},{9,1... | collective-permute-start | bytes 884744 | tf_op jit(solution)/shard_map/ppermute | solution.py:355
  68.5 27.3 %all-to-all-start.2 = ((bf16[4,144,576]{2,1,0:T(8,128)(2,1)}), bf16[4,144,576]{2,1,0:T(8,128)(2,1)S(1)}, u32[]{:S(2)}, u32[]{:S(2)}) async-start(bf16[4,144,576]{2,1,0:T(8,128)(2,1)} %broadcast_in_dim.7), calls=%async_computation.2 | async-start | bytes 1474560 | tf_op jit(solution)/shard_map/all_to_all | solution.py:527
  95.8 23.0 %all-to-all-start.3 = ((bf16[4,144,512]{2,1,0:T(8,128)(2,1)}), bf16[4,144,512]{2,1,0:T(8,128)(2,1)S(1)}, u32[]{:S(2)}, u32[]{:S(2)}) async-start(bf16[4,144,512]{2,1,0:T(8,128)(2,1)} %shard_map.64), calls=%async_computation.3 | async-start | bytes 1179648 | tf_op jit(solution)/shard_map/all_to_all | solution.py:521
  99.8 17.5 %collective-permute-start.6 = (bf16[4,144,576]{2,1,0:T(8,128)(2,1)S(1)}, bf16[4,144,576]{2,1,0:T(8,128)(2,1)S(1)}, u32[]{:S(2)}, u32[]{:S(2)}) collective-permute-start(bf16[4,144,576]{2,1,0:T(8,128)(2,1)S(1)} %all-to-all-done.2.mine_ref), channel_id=1, source_target_pairs={{0,16},{16,0},{1,17},{17,1},{2,18},{18,2},{3,19},{19,3},{4,20},{20... | collective-permute-start | bytes 1990664 | tf_op jit(solution)/shard_map/ppermute | solution.py:355
  118.8 3.3 %collective-permute-start.7 = (bf16[576,576]{1,0:T(8,128)(2,1)}, bf16[576,576]{1,0:T(8,128)(2,1)S(1)}, u32[]{:S(2)}, u32[]{:S(2)}) collective-permute-start(bf16[576,576]{1,0:T(8,128)(2,1)} %get-tuple-element.30), channel_id=1, source_target_pairs={{0,1},{1,0},{2,3},{3,2},{4,5},{5,4},{6,7},{7,6},{8,9},{9,8},{10,11... | collective-permute-start | bytes 1990664 | tf_op jit(solution)/shard_map/ppermute | solution.py:355
  118.8 2.9 %collective-permute-start.13 = (bf16[576,512]{1,0:T(8,128)(2,1)S(1)}, bf16[576,512]{1,0:T(8,128)(2,1)S(1)}, u32[]{:S(2)}, u32[]{:S(2)}) collective-permute-start(bf16[576,512]{1,0:T(8,128)(2,1)S(1)} %bitcast.21), channel_id=1, source_target_pairs={{0,1},{1,0},{2,3},{3,2},{4,5},{5,4},{6,7},{7,6},{8,9},{9,8},{10,11... | collective-permute-start | bytes 1769480 | tf_op jit(solution)/shard_map/ppermute | solution.py:355
  122.0 1.1 copy-start.4
  123.1 1.0 copy-start.6

commit v4 on v3

--- a/solution.py
+++ b/solution.py
@@ -63,12 +63,12 @@
 
 
 def weight_kernel(heads, head_dim, parts_ref, out_ref):
-    _, count, part_rows, share = parts_ref.shape
+    _, count, share, part_rows = parts_ref.shape
     head_rows = 3 * head_dim
     per_head = []
     for head in range(heads):
         low, high = [
-            jnp.concatenate([parts_ref[head * 2 + i, source].astype(jnp.float32) for source in range(count)], 1)
+            jnp.concatenate([parts_ref[head * 2 + i, source] for source in range(count)], 0).astype(jnp.float32).T
             for i in range(2)
         ]
         per_head.append(jnp.concatenate([low, high[2 * part_rows - head_rows :]], 0))
@@ -77,28 +77,26 @@
 
 
 def join_weight(parts, heads, head_dim):
-    _, count, _, share = parts.shape
-    out = (heads * 3 * head_dim, count * share)
+    _, count, share, _ = parts.shape
     return call(
         functools.partial(weight_kernel, heads, head_dim),
-        jax.ShapeDtypeStruct(out, jnp.bfloat16),
+        jax.ShapeDtypeStruct((heads * 3 * head_dim, count * share), jnp.bfloat16),
         (parts,),
-        flops=4 * out[0] * out[1],
-        moved=4 * out[0] * out[1],
         grant=16,
     )
 
 
-def project_kernel(kv_width, place_ref, weight_ref, mine_ref, other_ref, kv_ref, q_ref):
+def project_kernel(kv_width, place_ref, weight_ref, mine_ref, other_ref, kv_ref, *q_refs):
     half = mine_ref.shape[0]
     for part, ref in ((place_ref[0], mine_ref), (1 - place_ref[0], other_ref)):
         span = pl.ds(pl.multiple_of(part * half, half), half)
-        mixed = dot_nt(weight_ref[...], ref[...]).astype(jnp.bfloat16)
+        mixed = dot_nt(weight_ref[...] if q_refs else weight_ref[:kv_width], ref[...]).astype(jnp.bfloat16)
         kv_ref[:, span] = mixed[:kv_width]
-        q_ref[:, span] = mixed[kv_width:]
-
-
-def project(place, weight, mine, other, kv_width):
+        for q_ref in q_refs:
+            q_ref[:, span] = mixed[kv_width:]
+
+
+def project(place, weight, mine, other, kv_width, with_queries=True):
     half, width = mine.shape
     rows = 2 * half
     out_width = weight.shape[0]
@@ -107,7 +105,7 @@
         (
             jax.ShapeDtypeStruct((kv_width, rows), jnp.bfloat16),
             jax.ShapeDtypeStruct((out_width - kv_width, rows), jnp.bfloat16),
-        ),
+        )[: 2 if with_queries else 1],
         (place, weight, mine, other),
         flops=2 * rows * width * out_width,
         moved=2 * (rows * width + width * out_width + rows * out_width),
@@ -334,21 +332,24 @@
     return call(order_kernel, (out, out), (where, mine, other), moved=8 * mine.size, grant=8)
 
 
-def finish_kernel(near_w, far_w, near_ref, far_ref, frame_ref, gate_ref, out_ref):
-    projected = dot_nn(near_w[...], near_ref[...]) + dot_nn(far_w[...], far_ref[...])
-    updated = frame_ref[...].astype(jnp.float32) + gate_ref[:, 0:1] * projected
-    out_ref[...] = updated.astype(jnp.bfloat16)
-
-
-def finish(near_w, far_w, near, far, frame_part, gate_part):
-    return call(
-        finish_kernel,
-        jax.ShapeDtypeStruct(frame_part.shape, jnp.bfloat16),
-        (near_w, far_w, near, far, frame_part, gate_part),
-        flops=4 * near_w.shape[0] * near_w.shape[1] * near.shape[1],
-        moved=4 * (near_w.size + near.size + frame_part.size),
-        grant=16,
-    )
+def near_kernel(weight_ref, near_ref, frame_ref, gate_ref, out_ref):
+    projected = dot_nn(weight_ref[...], near_ref[...])
+    out_ref[...] = frame_ref[...].astype(jnp.float32) + gate_ref[:, 0:1] * projected
+
+
+def far_kernel(weight_ref, far_ref, near_sum_ref, gate_ref, out_ref):
+    projected = dot_nn(weight_ref[...], far_ref[...])
+    out_ref[...] = (near_sum_ref[...] + gate_ref[:, 0:1] * projected).astype(jnp.bfloat16)
+
+
+def finish_near(weight, near, frame_part, gate_part):
+    out = jax.ShapeDtypeStruct(frame_part.shape, jnp.float32)
+    return call(near_kernel, out, (weight, near, frame_part, gate_part), grant=16)
+
+
+def finish_far(weight, far, near_sum, gate_part):
+    out = jax.ShapeDtypeStruct(near_sum.shape, jnp.bfloat16)
+    return call(far_kernel, out, (weight, far, near_sum, gate_part), grant=16)
 
 
 def swapped(block, axis):
@@ -498,6 +499,7 @@
     part_rows = -(-3 * head_dim // 32) * 16
     start = tok * (3 * head_dim - part_rows)
     part = lax.dynamic_slice(blocks, (0, group, start, 0), (count, 1, part_rows, share))[:, 0]
+    part = jnp.transpose(part, (0, 2, 1))
     part = lax.all_to_all(part, "frame", 0, 0)
     plane = lax.all_to_all(jnp.broadcast_to(part[None], (4, *part.shape)), ("groups", "tok"), 0, 0)
     weight = join_weight(plane, heads, head_dim)
@@ -511,11 +513,15 @@
     queries, near, far = [], [], []
     for distance, block in enumerate(arrivals):
         if distance == 3:
-            block = after(block, (frame_part, near[0], near[1]))
+            block = after(block, (frame_part, near[0], near[1], near[2]))
         kv, q = project(place, weight, block, swapped(block, "head"), kv_width)
         queries.append(q)
         near.append(kv)
-        far.append(swapped(kv, "tok"))
+        if distance == 0:
+            across = swapped(block, "tok")
+            far += project(place, weight, across, swapped(across, "head"), kv_width, False)
+        else:
+            far.append(swapped(kv, "tok"))
     ids = jnp.stack([me ^ distance for distance in range(count)] + [anchor_offsets[0]]).astype(jnp.int32)
     attended = attend_all(ids, queries, near, far, heads, head_dim)
     arrived = lax.all_to_all(attended, "frame", 0, 0).reshape(count * heads * head_dim, rows)
@@ -527,7 +533,8 @@
     w_part = lax.all_to_all(jnp.broadcast_to(w_part[None], (count, *w_part.shape)), "frame", 0, 0)
     near_w, send_w = order_columns(where, w_part, swapped(w_part, "groups"))
     far_w = swapped(send_w, "head")
-    updated = finish(near_w, far_w, arrived, arrived_far, frame_part, gate_part)
+    near_sum = finish_near(near_w, arrived, frame_part, gate_part)
+    updated = finish_far(far_w, arrived_far, near_sum, gate_part)
     return updated.T[None]
 
 

time: 126 us -> 123 us (0.976)
  waiting for transfers between devices: 51.9 us -> 47.1 us
    ppermute x3, waiting for transfers between devices: 20.2 us -> 16.9 us  [flipped(): lax.ppermute(block, axis, [(i, i ^ distance) for i in range(lax.axis_size...]
    all_to_all x1 -> x0, local copies, waits for them, and re-layouts: 2.49 us -> none  [by_heads(): lax.all_to_all(jnp.broadcast_to(part[None], (4, *part.shape)), ('groups',...]
    unnamed x17 -> x30, local copies, waits for them, and re-layouts: 7.12 us -> 9.12 us
    ppermute x11 -> x12, waiting for transfers between devices: 26 us -> 24.5 us  [swapped(): return lax.ppermute(block, axis, [(0, 1), (1, 0)])]
    ppermute x11 -> x12, starting transfers between devices: 5.1 us -> 6.12 us  [swapped(): return lax.ppermute(block, axis, [(0, 1), (1, 0)])]
    pallas_call x11 -> x13, Pallas kernels: 31.8 us -> 32.4 us  [call(): pl.pallas_call(kernel, out_shape=out_shape, in_specs=[where if i in left...]
  transfers between devices with their start and end apart: 18 -> 19, of which waited for: 8 -> 6; matrix products, arithmetic and copies ran while one was open for 5% -> 3% of each run, Pallas kernels for 24% -> 25%
where the time goes in v4:
time: 123 us
  waiting for transfers between devices  47.1 us (38%)
  Pallas kernels  32.4 us (26%)
  starting transfers between devices  29.2 us (24%)
  local copies, waits for them, and re-layouts  13.2 us (11%)
    pallas_call x13, Pallas kernels, call(): pl.pallas_call(kernel, out_shape=out_shape, in_specs=[where if i in left...  32.4 us
    ppermute x12, waiting for transfers between devices, swapped(): return lax.ppermute(block, axis, [(0, 1), (1, 0)])  24.5 us
    ppermute x3, waiting for transfers between devices, flipped(): lax.ppermute(block, axis, [(i, i ^ distance) for i in range(lax.axis_size...  16.9 us
    unnamed x30, local copies, waits for them, and re-layouts  9.12 us
    all_to_all x1, starting transfers between devices, by_heads(): part = lax.all_to_all(part, 'frame', 0, 0)  6.32 us
    ppermute x12, starting transfers between devices, swapped(): return lax.ppermute(block, axis, [(0, 1), (1, 0)])  6.12 us
    all_to_all x1, waiting for transfers between devices, by_heads(): part = lax.all_to_all(part, 'frame', 0, 0)  5.71 us
    ppermute x3, starting transfers between devices, flipped(): lax.ppermute(block, axis, [(i, i ^ distance) for i in range(lax.axis_size...  4.45 us
  transfers between devices with their start and end apart: 19, of which 6 were waited for; matrix products, arithmetic and copies ran while one was open for 3% of the time, Pallas kernels for 25%

profile of v4, /device:TPU:0, one launch (start us, length us, event | category | flops | bytes accessed | tf_op | source)
XLA Modules:
  0.0 122.7 jit_solution(8323262219805518222)
XLA Ops:
  0.0 1.3 %copy-done = bf16[288,8,3,72]{0,3,2,1:T(8,128)(2,1)S(1)} copy-done((bf16[288,8,3,72]{0,3,2,1:T(8,128)(2,1)S(1)}, bf16[288,8,3,72]{0,3,2,1:T(8,128)(2,1)}, u32[]{:S(2)}) %copy-start) | copy-done | bytes 995352
  1.4 0.9 copy.6
  2.3 6.3 %all-to-all-start = ((bf16[4,288,112]{2,1,0:T(8,128)(2,1)}), bf16[4,288,112]{2,1,0:T(8,128)(2,1)S(1)}, u32[]{:S(2)}, u32[]{:S(2)}) async-start(bf16[4,288,112]{2,1,0:T(8,128)(2,1)} %bitcast.8), calls=%async_computation | async-start | bytes 589824 | tf_op jit(solution)/shard_map/all_to_all | solution.py:503
  8.6 0.5 shard_map.56.mine_ref
  9.1 2.1 %collective-permute-start.2 = (bf16[256,1152]{1,0:T(8,128)(2,1)S(1)}, bf16[256,1152]{1,0:T(8,128)(2,1)}, u32[]{:S(2)}, u32[]{:S(2)}) collective-permute-start(bf16[256,1152]{1,0:T(8,128)(2,1)S(1)} %shard_map.56.mine_ref), channel_id=1, source_target_pairs={{0,4},{4,0},{8,12},{12,8},{1,5},{5,1},{9,13},{13,9},{2,6},{6,2},{1... | collective-permute-start | bytes 1769480 | tf_op jit(solution)/shard_map/ppermute | solution.py:477
  11.2 2.4 %collective-permute-start = (bf16[256,1152]{1,0:T(8,128)(2,1)S(1)}, bf16[256,1152]{1,0:T(8,128)(2,1)}, u32[]{:S(2)}, u32[]{:S(2)}) collective-permute-start(bf16[256,1152]{1,0:T(8,128)(2,1)S(1)} %shard_map.56.mine_ref), channel_id=1, source_target_pairs={{0,8},{4,12},{8,0},{12,4},{1,9},{5,13},{9,1},{13,5},{2,10},{6,14},... | collective-permute-start | bytes 1769480 | tf_op jit(solution)/shard_map/ppermute | solution.py:477
  13.6 5.7 %all-to-all-done = bf16[4,288,112]{2,1,0:T(8,128)(2,1)S(1)} async-done(((bf16[4,288,112]{2,1,0:T(8,128)(2,1)}), bf16[4,288,112]{2,1,0:T(8,128)(2,1)S(1)}, u32[]{:S(2)}, u32[]{:S(2)}) %all-to-all-start) | async-done | bytes 258080 | tf_op jit(solution)/shard_map/all_to_all | solution.py:503
  19.3 1.2 broadcast_in_dim.6
  20.4 4.3 %all-to-all-start.1 = ((bf16[4,4,288,112]{3,2,1,0:T(8,128)(2,1)}), bf16[4,4,288,112]{3,2,1,0:T(8,128)(2,1)}, u32[]{:S(2)}, u32[]{:S(2)}) async-start(bf16[4,4,288,112]{3,2,1,0:T(8,128)(2,1)} %broadcast_in_dim.6), calls=%async_computation.1 | async-start | bytes 2359296 | tf_op jit(solution)/shard_map/all_to_all | solution.py:504
  24.7 2.0 %collective-permute-start.10 = (bf16[256,1152]{1,0:T(8,128)(2,1)S(1)}, bf16[256,1152]{1,0:T(8,128)(2,1)}, u32[]{:S(2)}, u32[]{:S(2)}) collective-permute-start(bf16[256,1152]{1,0:T(8,128)(2,1)S(1)} %shard_map.56.mine_ref), channel_id=1, source_target_pairs={{0,2},{2,0},{1,3},{3,1},{4,6},{6,4},{5,7},{7,5},{8,10},{10,8},{9,1... | collective-permute-start | bytes 1769480 | tf_op jit(solution)/shard_map/ppermute | solution.py:356
  26.7 0.0 collective-permute-start.3
  26.7 13.8 %collective-permute-done.2.mine_ref = bf16[256,1152]{1,0:T(8,128)(2,1)} collective-permute-done((bf16[256,1152]{1,0:T(8,128)(2,1)S(1)}, bf16[256,1152]{1,0:T(8,128)(2,1)}, u32[]{:S(2)}, u32[]{:S(2)}) %collective-permute-start.2) | collective-permute-done | bytes 589856 | tf_op jit(solution)/shard_map/ppermute | solution.py:477
  40.5 0.0 collective-permute-start.4
  40.5 3.1 %collective-permute-done.mine_ref = bf16[256,1152]{1,0:T(8,128)(2,1)} collective-permute-done((bf16[256,1152]{1,0:T(8,128)(2,1)S(1)}, bf16[256,1152]{1,0:T(8,128)(2,1)}, u32[]{:S(2)}, u32[]{:S(2)}) %collective-permute-start) | collective-permute-done | bytes 589856 | tf_op jit(solution)/shard_map/ppermute | solution.py:477
  43.6 0.0 collective-permute-start.5
  43.6 0.0 collective-permute-start.1
  43.6 6.2 %collective-permute-done.10.mine_ref = bf16[256,1152]{1,0:T(8,128)(2,1)} collective-permute-done((bf16[256,1152]{1,0:T(8,128)(2,1)S(1)}, bf16[256,1152]{1,0:T(8,128)(2,1)}, u32[]{:S(2)}, u32[]{:S(2)}) %collective-permute-start.10) | collective-permute-done | bytes 589856 | tf_op jit(solution)/shard_map/ppermute | solution.py:356
  49.8 0.0 collective-permute-start.11
  49.8 0.5 shard_map.57
  50.4 0.8 copy-done.4
  51.2 0.0 all-to-all-done.1.parts_ref
  51.2 1.6 %shard_map.55.weight_ref = bf16[432,1152]{1,0:T(8,128)(2,1)S(1)} custom-call(bf16[4,4,288,112]{3,2,1,0:T(8,128)(2,1)} %all-to-all-done.1.parts_ref), custom_call_target="tpu_custom_call" | custom-call | tf_op jit(solution)/shard_map/pallas_call | solution.py:27
  52.9 0.0 collective-permute-done.3.other_ref
  52.9 1.8 %shard_map.58 = (bf16[288,512]{1,0:T(8,128)(2,1)S(1)}, bf16[144,512]{1,0:T(8,128)(2,1)S(1)}) custom-call(s32[1]{0:T(128)} %bitcast.3.place_ref.core_ref, bf16[432,1152]{1,0:T(8,128)(2,1)S(1)} %shard_map.55.weight_ref, bf16[256,1152]{1,0:T(8,128)(2,1)S(1)} %shard_map.56.mine_ref, bf16[256,1152]{1,0:T(8,128)(2,1)} %collective-permute-done.3.other_ref), custom_call_target="tpu_custom_call" | custom-call | flops 509607936 | bytes 2617344 | tf_op jit(solution)/shard_map/pallas_call | solution.py:27
  54.7 0.7 copy-done.13
  55.4 0.0 collective-permute-done.4.other_ref
  55.4 2.7 %shard_map.59 = (bf16[288,512]{1,0:T(8,128)(2,1)}, bf16[144,512]{1,0:T(8,128)(2,1)S(1)}) custom-call(s32[1]{0:T(128)} %bitcast.3.place_ref.core_ref, bf16[432,1152]{1,0:T(8,128)(2,1)S(1)} %shard_map.55.weight_ref, bf16[256,1152]{1,0:T(8,128)(2,1)} %collective-permute-done.2.mine_ref, bf16[256,1152]{1,0:T(8,128)(2,1)} %collective-permute-done.4.other_ref), custom_call_target="tpu_custom_call" | custom-call | flops 509607936 | bytes 2617344 | tf_op jit(solution)/shard_map/pallas_call | solution.py:27
  58.1 0.0 collective-permute-done.5.other_ref
  58.1 2.7 %shard_map.60 = (bf16[288,512]{1,0:T(8,128)(2,1)}, bf16[144,512]{1,0:T(8,128)(2,1)S(1)}) custom-call(s32[1]{0:T(128)} %bitcast.3.place_ref.core_ref, bf16[432,1152]{1,0:T(8,128)(2,1)S(1)} %shard_map.55.weight_ref, bf16[256,1152]{1,0:T(8,128)(2,1)} %collective-permute-done.mine_ref, bf16[256,1152]{1,0:T(8,128)(2,1)} %collective-permute-done.5.other_ref), custom_call_target="tpu_custom_call" | custom-call | flops 509607936 | bytes 2617344 | tf_op jit(solution)/shard_map/pallas_call | solution.py:27
  60.8 0.7 copy-done.8
  61.5 0.0 collective-permute-done.1.mine_ref
  61.5 0.5 collective-permute-start.6
  62.0 0.3 collective-permute-start.12
  62.3 1.8 %collective-permute-start.13 = (bf16[288,512]{1,0:T(8,128)(2,1)}, bf16[288,512]{1,0:T(8,128)(2,1)}, u32[]{:S(2)}, u32[]{:S(2)}) collective-permute-start(bf16[288,512]{1,0:T(8,128)(2,1)} %get-tuple-element.26.refs_7_), channel_id=1, source_target_pairs={{0,2},{2,0},{1,3},{3,1},{4,6},{6,4},{5,7},{7,5},{8,10},{10,8},{9,1... | collective-permute-start | bytes 884744 | tf_op jit(solution)/shard_map/ppermute | solution.py:356
  64.7 0.1 stack.36.refs_0_
  64.8 0.9 dynamic-slice_bitcast_fusion
  65.7 0.0 collective-permute-done.11.other_ref
  65.7 1.8 %shard_map.63.refs_9_ = bf16[288,512]{1,0:T(8,128)(2,1)S(1)} custom-call(s32[1]{0:T(128)} %bitcast.3.place_ref.core_ref, bf16[432,1152]{1,0:T(8,128)(2,1)S(1)} %shard_map.55.weight_ref, bf16[256,1152]{1,0:T(8,128)(2,1)} %collective-permute-done.10.mine_ref, bf16[256,1152]{1,0:T(8,128)(2,1)} %collective-permute-done.11.other_ref), custom_call_target="tpu_custom_call" | custom-call | flops 509607936 | bytes 2617344 | tf_op jit(solution)/shard_map/pallas_call | solution.py:27
  67.6 0.0 collective-permute-done.6.other_ref
  67.6 2.6 %shard_map.61 = (bf16[288,512]{1,0:T(8,128)(2,1)}, bf16[144,512]{1,0:T(8,128)(2,1)S(1)}) custom-call(s32[1]{0:T(128)} %bitcast.3.place_ref.core_ref, bf16[432,1152]{1,0:T(8,128)(2,1)S(1)} %shard_map.55.weight_ref, bf16[256,1152]{1,0:T(8,128)(2,1)} %collective-permute-done.1.mine_ref, bf16[256,1152]{1,0:T(8,128)(2,1)S(1)} %collective-permute-done.6.other_ref), custom_call_target="tpu_custom_call" | custom-call | flops 509607936 | bytes 2617344 | tf_op jit(solution)/shard_map/pallas_call | solution.py:27
  70.2 0.7 copy-done.10
  70.9 0.3 collective-permute-start.9
  71.1 0.9 broadcast_in_dim.7
  72.1 3.5 %all-to-all-start.2 = ((bf16[4,144,576]{2,1,0:T(8,128)(2,1)}), bf16[4,144,576]{2,1,0:T(8,128)(2,1)S(1)}, u32[]{:S(2)}, u32[]{:S(2)}) async-start(bf16[4,144,576]{2,1,0:T(8,128)(2,1)} %broadcast_in_dim.7), calls=%async_computation.2 | async-start | bytes 1474560 | tf_op jit(solution)/shard_map/all_to_all | solution.py:533
  75.6 0.0 collective-permute-done.12.refs_10_
  75.6 2.9 %collective-permute-done.13.refs_11_ = bf16[288,512]{1,0:T(8,128)(2,1)} collective-permute-done((bf16[288,512]{1,0:T(8,128)(2,1)}, bf16[288,512]{1,0:T(8,128)(2,1)}, u32[]{:S(2)}, u32[]{:S(2)}) %collective-permute-start.13) | collective-permute-done | bytes 294944 | tf_op jit(solution)/shard_map/ppermute | solution.py:356
  78.5 0.9 copy-done.11
  79.4 1.0 copy-done.14
  80.4 11.8 %shard_map.64 = (f32[8,1,512]{2,1,0:T(1,128)S(1)}, f32[8,80,512]{2,1,0:T(8,128)S(1)}) custom-call(s32[5]{0:T(128)S(1)} %stack.36.refs_0_, bf16[144,512]{1,0:T(8,128)(2,1)S(1)} %get-tuple-element.31.refs_1_, bf16[144,512]{1,0:T(8,128)(2,1)S(1)} %get-tuple-element.32.refs_2_, bf16[144,512]{1,0:T(8,128)(2,1)S(1)} %copy-done.9, bf16[144,512]{1,0:T(8,128)(2,1)S(1)} %copy-done.11, ...), custom_call_target="tpu_custom_call" | custom-call | flops 14495514624 | bytes 3538944 | tf_op jit(solution)/shard_map/pallas_call | solution.py:27
  92.2 2.6 %shard_map.65 = bf16[4,144,512]{2,1,0:T(8,128)(2,1)} custom-call(s32[5]{0:T(128)S(1)} %stack.36.refs_0_, bf16[144,512]{1,0:T(8,128)(2,1)S(1)} %get-tuple-element.31.refs_1_, bf16[144,512]{1,0:T(8,128)(2,1)S(1)} %get-tuple-element.32.refs_2_, bf16[144,512]{1,0:T(8,128)(2,1)S(1)} %copy-done.9, bf16[144,512]{1,0:T(8,128)(2,1)S(1)} %copy-done.11, ...), custom_call_target="tpu_custom_call" | custom-call | flops 603979776 | bytes 3538944 | tf_op jit(solution)/shard_map/pallas_call | solution.py:27
  94.8 4.4 %all-to-all-start.3 = ((bf16[4,144,512]{2,1,0:T(8,128)(2,1)}), bf16[4,144,512]{2,1,0:T(8,128)(2,1)S(1)}, u32[]{:S(2)}, u32[]{:S(2)}) async-start(bf16[4,144,512]{2,1,0:T(8,128)(2,1)} %shard_map.65), calls=%async_computation.3 | async-start | bytes 1179648 | tf_op jit(solution)/shard_map/all_to_all | solution.py:527
  99.2 0.8 collective-permute-start.7
  100.0 0.1 pad_add_fusion.where_ref
  100.1 15.4 %collective-permute-done.7.other_ref = bf16[4,144,576]{2,1,0:T(8,128)(2,1)S(1)} collective-permute-done((bf16[4,144,576]{2,1,0:T(8,128)(2,1)S(1)}, bf16[4,144,576]{2,1,0:T(8,128)(2,1)S(1)}, u32[]{:S(2)}, u32[]{:S(2)}) %collective-permute-start.7) | collective-permute-done | bytes 663584 | tf_op jit(solution)/shard_map/ppermute | solution.py:356
  115.5 1.5 %shard_map.62 = (bf16[576,576]{1,0:T(8,128)(2,1)S(1)}, bf16[576,576]{1,0:T(8,128)(2,1)}) custom-call(s32[4]{0:T(128)S(1)} %pad_add_fusion.where_ref, bf16[4,144,576]{2,1,0:T(8,128)(2,1)S(1)} %all-to-all-done.2.mine_ref, bf16[4,144,576]{2,1,0:T(8,128)(2,1)S(1)} %collective-permute-done.7.other_ref), custom_call_target="tpu_custom_call" | custom-call | bytes 2654208 | tf_op jit(solution)/shard_map/pallas_call | solution.py:27
  117.0 0.9 copy-done.2
  117.9 0.0 collective-permute-start.8
  117.9 0.0 all-to-all-done.3
  117.9 0.5 collective-permute-start.14
  118.4 1.1 copy-done.3
  119.5 1.1 copy-done.5
  120.6 0.6 shard_map.66.near_sum_ref
  121.2 0.0 collective-permute-done.14.far_ref
  121.3 1.4 %shard_map.67 = bf16[576,512]{1,0:T(8,128)(2,1)} custom-call(bf16[576,576]{1,0:T(8,128)(2,1)S(1)} %collective-permute-done.8.weight_ref, bf16[576,512]{1,0:T(8,128)(2,1)S(1)} %collective-permute-done.14.far_ref, f32[576,512]{1,0:T(8,128)S(1)} %shard_map.66.near_sum_ref, f32[576,8]{1,0:T(8,128)S(1)} %get-tuple-element.38.gate_ref), custom_call_target="tpu_custom_call" | custom-call | tf_op jit(solution)/shard_map/pallas_call | solution.py:27
  (24 shorter events, 0.1 us)
Async XLA Ops:
  0.0 1.3 %copy-start = (bf16[288,8,3,72]{0,3,2,1:T(8,128)(2,1)S(1)}, bf16[288,8,3,72]{0,3,2,1:T(8,128)(2,1)}, u32[]{:S(2)}) copy-start(bf16[288,8,3,72]{0,3,2,1:T(8,128)(2,1)} %param.7) | copy-start | bytes 2985988
  0.0 8.6 %copy-start.1 = (bf16[1,512,1152]{2,1,0:T(8,128)(2,1)S(1)}, bf16[1,512,1152]{2,1,0:T(8,128)(2,1)}, u32[]{:S(2)}) copy-start(bf16[1,512,1152]{2,1,0:T(8,128)(2,1)} %param.5) | copy-start | bytes 3538948
  0.0 8.6 %copy-start.12 = (f32[3,1152]{1,0:T(4,128)S(1)}, f32[3,1152]{1,0:T(4,128)}, u32[]{:S(2)}) copy-start(f32[3,1152]{1,0:T(4,128)} %mod_ref.3) | copy-start | bytes 41476
  2.3 17.0 %all-to-all-start = ((bf16[4,288,112]{2,1,0:T(8,128)(2,1)}), bf16[4,288,112]{2,1,0:T(8,128)(2,1)S(1)}, u32[]{:S(2)}, u32[]{:S(2)}) async-start(bf16[4,288,112]{2,1,0:T(8,128)(2,1)} %bitcast.8), calls=%async_computation | async-start | bytes 589824 | tf_op jit(solution)/shard_map/all_to_all | solution.py:503
  9.1 31.4 %collective-permute-start.2 = (bf16[256,1152]{1,0:T(8,128)(2,1)S(1)}, bf16[256,1152]{1,0:T(8,128)(2,1)}, u32[]{:S(2)}, u32[]{:S(2)}) collective-permute-start(bf16[256,1152]{1,0:T(8,128)(2,1)S(1)} %shard_map.56.mine_ref), channel_id=1, source_target_pairs={{0,4},{4,0},{8,12},{12,8},{1,5},{5,1},{9,13},{13,9},{2,6},{6,2},{1... | collective-permute-start | bytes 1769480 | tf_op jit(solution)/shard_map/ppermute | solution.py:477
  11.2 32.4 %collective-permute-start = (bf16[256,1152]{1,0:T(8,128)(2,1)S(1)}, bf16[256,1152]{1,0:T(8,128)(2,1)}, u32[]{:S(2)}, u32[]{:S(2)}) collective-permute-start(bf16[256,1152]{1,0:T(8,128)(2,1)S(1)} %shard_map.56.mine_ref), channel_id=1, source_target_pairs={{0,8},{4,12},{8,0},{12,4},{1,9},{5,13},{9,1},{13,5},{2,10},{6,14},... | collective-permute-start | bytes 1769480 | tf_op jit(solution)/shard_map/ppermute | solution.py:477
  20.4 30.8 %all-to-all-start.1 = ((bf16[4,4,288,112]{3,2,1,0:T(8,128)(2,1)}), bf16[4,4,288,112]{3,2,1,0:T(8,128)(2,1)}, u32[]{:S(2)}, u32[]{:S(2)}) async-start(bf16[4,4,288,112]{3,2,1,0:T(8,128)(2,1)} %broadcast_in_dim.6), calls=%async_computation.1 | async-start | bytes 2359296 | tf_op jit(solution)/shard_map/all_to_all | solution.py:504
  24.7 25.1 %collective-permute-start.10 = (bf16[256,1152]{1,0:T(8,128)(2,1)S(1)}, bf16[256,1152]{1,0:T(8,128)(2,1)}, u32[]{:S(2)}, u32[]{:S(2)}) collective-permute-start(bf16[256,1152]{1,0:T(8,128)(2,1)S(1)} %shard_map.56.mine_ref), channel_id=1, source_target_pairs={{0,2},{2,0},{1,3},{3,1},{4,6},{6,4},{5,7},{7,5},{8,10},{10,8},{9,1... | collective-permute-start | bytes 1769480 | tf_op jit(solution)/shard_map/ppermute | solution.py:356
  26.7 26.1 %collective-permute-start.3 = (bf16[256,1152]{1,0:T(8,128)(2,1)S(1)}, bf16[256,1152]{1,0:T(8,128)(2,1)}, u32[]{:S(2)}, u32[]{:S(2)}) collective-permute-start(bf16[256,1152]{1,0:T(8,128)(2,1)S(1)} %shard_map.56.mine_ref), channel_id=1, source_target_pairs={{0,1},{1,0},{2,3},{3,2},{4,5},{5,4},{6,7},{7,6},{8,9},{9,8},{10,11... | collective-permute-start | bytes 1769480 | tf_op jit(solution)/shard_map/ppermute | solution.py:356
  40.5 14.9 %collective-permute-start.4 = (bf16[256,1152]{1,0:T(8,128)(2,1)}, bf16[256,1152]{1,0:T(8,128)(2,1)}, u32[]{:S(2)}, u32[]{:S(2)}) collective-permute-start(bf16[256,1152]{1,0:T(8,128)(2,1)} %collective-permute-done.2.mine_ref), channel_id=1, source_target_pairs={{0,1},{1,0},{2,3},{3,2},{4,5},{5,4},{6,7},{7,6},{8,9},{9,8},{10,11... | collective-permute-start | bytes 1769480 | tf_op jit(solution)/shard_map/ppermute | solution.py:356
  43.6 14.5 %collective-permute-start.5 = (bf16[256,1152]{1,0:T(8,128)(2,1)}, bf16[256,1152]{1,0:T(8,128)(2,1)}, u32[]{:S(2)}, u32[]{:S(2)}) collective-permute-start(bf16[256,1152]{1,0:T(8,128)(2,1)} %collective-permute-done.mine_ref), channel_id=1, source_target_pairs={{0,1},{1,0},{2,3},{3,2},{4,5},{5,4},{6,7},{7,6},{8,9},{9,8},{10,11... | collective-permute-start | bytes 1769480 | tf_op jit(solution)/shard_map/ppermute | solution.py:356
  43.6 17.9 %collective-permute-start.1 = (bf16[256,1152]{1,0:T(8,128)(2,1)}, bf16[256,1152]{1,0:T(8,128)(2,1)}, u32[]{:S(2)}, u32[]{:S(2)}) collective-permute-start(bf16[256,1152]{1,0:T(8,128)(2,1)} %collective-permute-done.mine_ref), channel_id=1, source_target_pairs={{0,4},{4,0},{8,12},{12,8},{1,5},{5,1},{9,13},{13,9},{2,6},{6,2},{1... | collective-permute-start | bytes 1769480 | tf_op jit(solution)/shard_map/ppermute | solution.py:477
  49.8 15.9 %collective-permute-start.11 = (bf16[256,1152]{1,0:T(8,128)(2,1)}, bf16[256,1152]{1,0:T(8,128)(2,1)}, u32[]{:S(2)}, u32[]{:S(2)}) collective-permute-start(bf16[256,1152]{1,0:T(8,128)(2,1)} %collective-permute-done.10.mine_ref), channel_id=1, source_target_pairs={{0,1},{1,0},{2,3},{3,2},{4,5},{5,4},{6,7},{7,6},{8,9},{9,8},{10,11... | collective-permute-start | bytes 1769480 | tf_op jit(solution)/shard_map/ppermute | solution.py:356
  50.4 0.8 copy-start.4
  54.7 0.7 copy-start.13
  60.8 0.7 copy-start.8
  61.5 6.1 %collective-permute-start.6 = (bf16[256,1152]{1,0:T(8,128)(2,1)}, bf16[256,1152]{1,0:T(8,128)(2,1)S(1)}, u32[]{:S(2)}, u32[]{:S(2)}) collective-permute-start(bf16[256,1152]{1,0:T(8,128)(2,1)} %collective-permute-done.1.mine_ref), channel_id=1, source_target_pairs={{0,1},{1,0},{2,3},{3,2},{4,5},{5,4},{6,7},{7,6},{8,9},{9,8},{10,11... | collective-permute-start | bytes 1769480 | tf_op jit(solution)/shard_map/ppermute | solution.py:356
  62.0 13.6 %collective-permute-start.12 = (bf16[288,512]{1,0:T(8,128)(2,1)}, bf16[288,512]{1,0:T(8,128)(2,1)}, u32[]{:S(2)}, u32[]{:S(2)}) collective-permute-start(bf16[288,512]{1,0:T(8,128)(2,1)} %get-tuple-element.25.refs_6_), channel_id=1, source_target_pairs={{0,2},{2,0},{1,3},{3,1},{4,6},{6,4},{5,7},{7,5},{8,10},{10,8},{9,1... | collective-permute-start | bytes 884744 | tf_op jit(solution)/shard_map/ppermute | solution.py:356
  62.3 16.2 %collective-permute-start.13 = (bf16[288,512]{1,0:T(8,128)(2,1)}, bf16[288,512]{1,0:T(8,128)(2,1)}, u32[]{:S(2)}, u32[]{:S(2)}) collective-permute-start(bf16[288,512]{1,0:T(8,128)(2,1)} %get-tuple-element.26.refs_7_), channel_id=1, source_target_pairs={{0,2},{2,0},{1,3},{3,1},{4,6},{6,4},{5,7},{7,5},{8,10},{10,8},{9,1... | collective-permute-start | bytes 884744 | tf_op jit(solution)/shard_map/ppermute | solution.py:356
  67.5 2.7 %copy-start.6 = (bf16[288,512]{1,0:T(8,128)(2,1)}, bf16[288,512]{1,0:T(8,128)(2,1)S(1)}, u32[]{:S(2)}) copy-start(bf16[288,512]{1,0:T(8,128)(2,1)S(1)} %shard_map.63.refs_9_) | copy-start | bytes 884740
  70.2 0.7 copy-start.10
  70.9 7.6 %copy-start.7 = (bf16[288,512]{1,0:T(8,128)(2,1)S(1)}, bf16[288,512]{1,0:T(8,128)(2,1)}, u32[]{:S(2)}) copy-start(bf16[288,512]{1,0:T(8,128)(2,1)} %copy-done.6) | copy-start | bytes 884740
  70.9 7.6 %copy-start.9 = (bf16[144,512]{1,0:T(8,128)(2,1)S(1)}, bf16[144,512]{1,0:T(8,128)(2,1)}, u32[]{:S(2)}) copy-start(bf16[144,512]{1,0:T(8,128)(2,1)} %copy-done.8) | copy-start | bytes 442372
  70.9 21.3 %collective-permute-start.9 = (bf16[288,512]{1,0:T(8,128)(2,1)}, bf16[288,512]{1,0:T(8,128)(2,1)S(1)}, u32[]{:S(2)}, u32[]{:S(2)}) collective-permute-start(bf16[288,512]{1,0:T(8,128)(2,1)} %get-tuple-element.28.refs_8_), channel_id=1, source_target_pairs={{0,2},{2,0},{1,3},{3,1},{4,6},{6,4},{5,7},{7,5},{8,10},{10,8},{9,1... | collective-permute-start | bytes 884744 | tf_op jit(solution)/shard_map/ppermute | solution.py:356
  72.1 22.7 %all-to-all-start.2 = ((bf16[4,144,576]{2,1,0:T(8,128)(2,1)}), bf16[4,144,576]{2,1,0:T(8,128)(2,1)S(1)}, u32[]{:S(2)}, u32[]{:S(2)}) async-start(bf16[4,144,576]{2,1,0:T(8,128)(2,1)} %broadcast_in_dim.7), calls=%async_computation.2 | async-start | bytes 1474560 | tf_op jit(solution)/shard_map/all_to_all | solution.py:533
  78.5 0.9 copy-start.11
  79.4 1.0 copy-start.14
  94.8 23.2 %all-to-all-start.3 = ((bf16[4,144,512]{2,1,0:T(8,128)(2,1)}), bf16[4,144,512]{2,1,0:T(8,128)(2,1)S(1)}, u32[]{:S(2)}, u32[]{:S(2)}) async-start(bf16[4,144,512]{2,1,0:T(8,128)(2,1)} %shard_map.65), calls=%async_computation.3 | async-start | bytes 1179648 | tf_op jit(solution)/shard_map/all_to_all | solution.py:527
  99.2 16.3 %collective-permute-start.7 = (bf16[4,144,576]{2,1,0:T(8,128)(2,1)S(1)}, bf16[4,144,576]{2,1,0:T(8,128)(2,1)S(1)}, u32[]{:S(2)}, u32[]{:S(2)}) collective-permute-start(bf16[4,144,576]{2,1,0:T(8,128)(2,1)S(1)} %all-to-all-done.2.mine_ref), channel_id=1, source_target_pairs={{0,16},{16,0},{1,17},{17,1},{2,18},{18,2},{3,19},{19,3},{4,20},{20... | collective-permute-start | bytes 1990664 | tf_op jit(solution)/shard_map/ppermute | solution.py:356
  117.0 0.9 copy-start.2
  117.9 3.3 %collective-permute-start.8 = (bf16[576,576]{1,0:T(8,128)(2,1)}, bf16[576,576]{1,0:T(8,128)(2,1)S(1)}, u32[]{:S(2)}, u32[]{:S(2)}) collective-permute-start(bf16[576,576]{1,0:T(8,128)(2,1)} %get-tuple-element.30), channel_id=1, source_target_pairs={{0,1},{1,0},{2,3},{3,2},{4,5},{5,4},{6,7},{7,6},{8,9},{9,8},{10,11... | collective-permute-start | bytes 1990664 | tf_op jit(solution)/shard_map/ppermute | solution.py:356
  117.9 3.3 %collective-permute-start.14 = (bf16[576,512]{1,0:T(8,128)(2,1)S(1)}, bf16[576,512]{1,0:T(8,128)(2,1)S(1)}, u32[]{:S(2)}, u32[]{:S(2)}) collective-permute-start(bf16[576,512]{1,0:T(8,128)(2,1)S(1)} %bitcast.23), channel_id=1, source_target_pairs={{0,1},{1,0},{2,3},{3,2},{4,5},{5,4},{6,7},{7,6},{8,9},{9,8},{10,11... | collective-permute-start | bytes 1769480 | tf_op jit(solution)/shard_map/ppermute | solution.py:356
  118.4 1.1 copy-start.3
  119.5 1.1 copy-start.5

commit v5 on v4

--- a/solution.py
+++ b/solution.py
@@ -314,7 +314,7 @@
     )
 
 
-def order_kernel(where_ref, mine_ref, other_ref, near_ref, send_ref):
+def part_kernel(where_ref, mine_ref, other_ref, heads_ref, start_ref, gate_ref, out_ref, weight):
     group, core = where_ref[1], where_ref[3]
     block = mine_ref.shape[1]
     per_core = mine_ref.shape[0] // 2
@@ -322,34 +322,19 @@
         half = group if same else 1 - group
         for index in range(per_core):
             start = pl.multiple_of((index * 2 + half) * block, block)
-            near_ref[pl.ds(start, block), :] = ref[core * per_core + index]
-            send_ref[pl.ds(start, block), :] = ref[(1 - core) * per_core + index]
-
-
-def order_columns(where, mine, other):
-    count, block, depth = mine.shape
-    out = jax.ShapeDtypeStruct((count * block, depth), mine.dtype)
-    return call(order_kernel, (out, out), (where, mine, other), moved=8 * mine.size, grant=8)
-
-
-def near_kernel(weight_ref, near_ref, frame_ref, gate_ref, out_ref):
-    projected = dot_nn(weight_ref[...], near_ref[...])
-    out_ref[...] = frame_ref[...].astype(jnp.float32) + gate_ref[:, 0:1] * projected
-
-
-def far_kernel(weight_ref, far_ref, near_sum_ref, gate_ref, out_ref):
-    projected = dot_nn(weight_ref[...], far_ref[...])
-    out_ref[...] = (near_sum_ref[...] + gate_ref[:, 0:1] * projected).astype(jnp.bfloat16)
-
-
-def finish_near(weight, near, frame_part, gate_part):
-    out = jax.ShapeDtypeStruct(frame_part.shape, jnp.float32)
-    return call(near_kernel, out, (weight, near, frame_part, gate_part), grant=16)
-
-
-def finish_far(weight, far, near_sum, gate_part):
-    out = jax.ShapeDtypeStruct(near_sum.shape, jnp.bfloat16)
-    return call(far_kernel, out, (weight, far, near_sum, gate_part), grant=16)
+            weight[pl.ds(start, block), :] = ref[core * per_core + index]
+    projected = dot_nn(weight[...], heads_ref[...])
+    out_ref[...] = (start_ref[...].astype(jnp.float32) + gate_ref[:, 0:1] * projected).astype(out_ref.dtype)
+
+
+def add_part(where, mine, other, heads, start, gate, dtype):
+    return call(
+        part_kernel,
+        jax.ShapeDtypeStruct(start.shape, dtype),
+        (where, mine, other, heads, start, gate),
+        [pltpu.VMEM((start.shape[0], mine.shape[2]), jnp.bfloat16)],
+        grant=16,
+    )
 
 
 def swapped(block, axis):
@@ -518,7 +503,7 @@
         queries.append(q)
         near.append(kv)
         if distance == 0:
-            across = swapped(block, "tok")
+            across = after(swapped(block, "tok"), kv)
             far += project(place, weight, across, swapped(across, "head"), kv_width, False)
         else:
             far.append(swapped(kv, "tok"))
@@ -531,10 +516,10 @@
     w_part = lax.dynamic_slice_in_dim(w_out.T, group * columns, columns, 0)
     w_part = after(w_part, near[-1])
     w_part = lax.all_to_all(jnp.broadcast_to(w_part[None], (count, *w_part.shape)), "frame", 0, 0)
-    near_w, send_w = order_columns(where, w_part, swapped(w_part, "groups"))
-    far_w = swapped(send_w, "head")
-    near_sum = finish_near(near_w, arrived, frame_part, gate_part)
-    updated = finish_far(far_w, arrived_far, near_sum, gate_part)
+    w_other = swapped(w_part, "groups")
+    near_sum = add_part(where, w_part, w_other, arrived, frame_part, gate_part, jnp.float32)
+    w_far = [swapped(w, "head") for w in (w_part, w_other)]
+    updated = add_part(where, *w_far, arrived_far, near_sum, gate_part, jnp.bfloat16)
     return updated.T[None]
 
 

time: 123 us -> 122 us (level)
  Pallas kernels: 32.4 us -> 35.3 us
  local copies, waits for them, and re-layouts: 13.2 us -> 11.1 us
  waiting for transfers between devices: 47.1 us -> 45.7 us
    ppermute x12 -> x13, waiting for transfers between devices: 24.5 us -> 19.3 us  [swapped(): return lax.ppermute(block, axis, [(0, 1), (1, 0)])]
    ppermute x3, waiting for transfers between devices: 16.9 us -> 20.7 us  [flipped(): lax.ppermute(block, axis, [(i, i ^ distance) for i in range(lax.axis_size...]
    pallas_call x13 -> x12, Pallas kernels: 32.4 us -> 35.3 us  [call(): pl.pallas_call(kernel, out_shape=out_shape, in_specs=[where if i in left...]
    unnamed x30 -> x26, local copies, waits for them, and re-layouts: 9.12 us -> 7.09 us
    ppermute x12 -> x13, starting transfers between devices: 6.12 us -> 6.89 us  [swapped(): return lax.ppermute(block, axis, [(0, 1), (1, 0)])]
  transfers between devices with their start and end apart: 19 -> 20, of which waited for: 6 -> 7; matrix products, arithmetic and copies ran while one was open for 3% -> 3% of each run, Pallas kernels for 25% -> 27%
where the time goes in v5:
time: 122 us
  waiting for transfers between devices  45.7 us (37%)
  Pallas kernels  35.3 us (29%)
  starting transfers between devices  28.9 us (24%)
  local copies, waits for them, and re-layouts  11.1 us (9%)
    pallas_call x12, Pallas kernels, call(): pl.pallas_call(kernel, out_shape=out_shape, in_specs=[where if i in left...  35.3 us
    ppermute x3, waiting for transfers between devices, flipped(): lax.ppermute(block, axis, [(i, i ^ distance) for i in range(lax.axis_size...  20.7 us
    ppermute x13, waiting for transfers between devices, swapped(): return lax.ppermute(block, axis, [(0, 1), (1, 0)])  19.3 us
    unnamed x26, local copies, waits for them, and re-layouts  7.09 us
    ppermute x13, starting transfers between devices, swapped(): return lax.ppermute(block, axis, [(0, 1), (1, 0)])  6.89 us
    all_to_all x1, starting transfers between devices, by_heads(): part = lax.all_to_all(part, 'frame', 0, 0)  6.32 us
    all_to_all x1, waiting for transfers between devices, by_heads(): part = lax.all_to_all(part, 'frame', 0, 0)  5.71 us
    ppermute x3, starting transfers between devices, flipped(): lax.ppermute(block, axis, [(i, i ^ distance) for i in range(lax.axis_size...  4.45 us
  transfers between devices with their start and end apart: 20, of which 7 were waited for; matrix products, arithmetic and copies ran while one was open for 3% of the time, Pallas kernels for 27%

profile of v5, /device:TPU:0, one launch (start us, length us, event | category | flops | bytes accessed | tf_op | source)
XLA Modules:
  0.0 122.0 jit_solution(15043431470445603783)
XLA Ops:
  0.0 1.3 %copy-done = bf16[288,8,3,72]{0,3,2,1:T(8,128)(2,1)S(1)} copy-done((bf16[288,8,3,72]{0,3,2,1:T(8,128)(2,1)S(1)}, bf16[288,8,3,72]{0,3,2,1:T(8,128)(2,1)}, u32[]{:S(2)}) %copy-start) | copy-done | bytes 995352
  1.4 0.9 copy.6
  2.3 6.3 %all-to-all-start = ((bf16[4,288,112]{2,1,0:T(8,128)(2,1)}), bf16[4,288,112]{2,1,0:T(8,128)(2,1)S(1)}, u32[]{:S(2)}, u32[]{:S(2)}) async-start(bf16[4,288,112]{2,1,0:T(8,128)(2,1)} %bitcast.8), calls=%async_computation | async-start | bytes 589824 | tf_op jit(solution)/shard_map/all_to_all | solution.py:488
  8.6 0.5 shard_map.56.mine_ref
  9.1 2.1 %collective-permute-start.2 = (bf16[256,1152]{1,0:T(8,128)(2,1)S(1)}, bf16[256,1152]{1,0:T(8,128)(2,1)}, u32[]{:S(2)}, u32[]{:S(2)}) collective-permute-start(bf16[256,1152]{1,0:T(8,128)(2,1)S(1)} %shard_map.56.mine_ref), channel_id=1, source_target_pairs={{0,4},{4,0},{8,12},{12,8},{1,5},{5,1},{9,13},{13,9},{2,6},{6,2},{1... | collective-permute-start | bytes 1769480 | tf_op jit(solution)/shard_map/ppermute | solution.py:462
  11.2 2.4 %collective-permute-start = (bf16[256,1152]{1,0:T(8,128)(2,1)S(1)}, bf16[256,1152]{1,0:T(8,128)(2,1)}, u32[]{:S(2)}, u32[]{:S(2)}) collective-permute-start(bf16[256,1152]{1,0:T(8,128)(2,1)S(1)} %shard_map.56.mine_ref), channel_id=1, source_target_pairs={{0,8},{4,12},{8,0},{12,4},{1,9},{5,13},{9,1},{13,5},{2,10},{6,14},... | collective-permute-start | bytes 1769480 | tf_op jit(solution)/shard_map/ppermute | solution.py:462
  13.6 5.7 %all-to-all-done = bf16[4,288,112]{2,1,0:T(8,128)(2,1)S(1)} async-done(((bf16[4,288,112]{2,1,0:T(8,128)(2,1)}), bf16[4,288,112]{2,1,0:T(8,128)(2,1)S(1)}, u32[]{:S(2)}, u32[]{:S(2)}) %all-to-all-start) | async-done | bytes 258080 | tf_op jit(solution)/shard_map/all_to_all | solution.py:488
  19.3 1.2 broadcast_in_dim.6
  20.4 4.3 %all-to-all-start.1 = ((bf16[4,4,288,112]{3,2,1,0:T(8,128)(2,1)}), bf16[4,4,288,112]{3,2,1,0:T(8,128)(2,1)}, u32[]{:S(2)}, u32[]{:S(2)}) async-start(bf16[4,4,288,112]{3,2,1,0:T(8,128)(2,1)} %broadcast_in_dim.6), calls=%async_computation.1 | async-start | bytes 2359296 | tf_op jit(solution)/shard_map/all_to_all | solution.py:489
  24.7 0.1 collective-permute-start.3
  24.8 1.9 %collective-permute-start.11 = (bf16[256,1152]{1,0:T(8,128)(2,1)S(1)}, bf16[256,1152]{1,0:T(8,128)(2,1)}, u32[]{:S(2)}, u32[]{:S(2)}) collective-permute-start(bf16[256,1152]{1,0:T(8,128)(2,1)S(1)} %shard_map.56.mine_ref), channel_id=1, source_target_pairs={{0,2},{2,0},{1,3},{3,1},{4,6},{6,4},{5,7},{7,5},{8,10},{10,8},{9,1... | collective-permute-start | bytes 1769480 | tf_op jit(solution)/shard_map/ppermute | solution.py:341
  26.7 13.8 %collective-permute-done.2.mine_ref = bf16[256,1152]{1,0:T(8,128)(2,1)} collective-permute-done((bf16[256,1152]{1,0:T(8,128)(2,1)S(1)}, bf16[256,1152]{1,0:T(8,128)(2,1)}, u32[]{:S(2)}, u32[]{:S(2)}) %collective-permute-start.2) | collective-permute-done | bytes 589856 | tf_op jit(solution)/shard_map/ppermute | solution.py:462
  40.5 0.0 collective-permute-start.4
  40.5 3.1 %collective-permute-done.mine_ref = bf16[256,1152]{1,0:T(8,128)(2,1)} collective-permute-done((bf16[256,1152]{1,0:T(8,128)(2,1)S(1)}, bf16[256,1152]{1,0:T(8,128)(2,1)}, u32[]{:S(2)}, u32[]{:S(2)}) %collective-permute-start) | collective-permute-done | bytes 589856 | tf_op jit(solution)/shard_map/ppermute | solution.py:462
  43.6 0.0 collective-permute-start.5
  43.6 0.0 collective-permute-start.1
  43.6 0.5 shard_map.57
  44.1 0.8 copy-done.2
  45.0 0.0 all-to-all-done.1.parts_ref
  45.0 1.6 %shard_map.55.weight_ref = bf16[432,1152]{1,0:T(8,128)(2,1)S(1)} custom-call(bf16[4,4,288,112]{3,2,1,0:T(8,128)(2,1)} %all-to-all-done.1.parts_ref), custom_call_target="tpu_custom_call" | custom-call | tf_op jit(solution)/shard_map/pallas_call | solution.py:27
  46.6 0.0 collective-permute-done.3.other_ref
  46.6 1.8 %shard_map.58 = (bf16[288,512]{1,0:T(8,128)(2,1)S(1)}, bf16[144,512]{1,0:T(8,128)(2,1)S(1)}) custom-call(s32[1]{0:T(128)} %bitcast.3.place_ref.core_ref, bf16[432,1152]{1,0:T(8,128)(2,1)S(1)} %shard_map.55.weight_ref, bf16[256,1152]{1,0:T(8,128)(2,1)S(1)} %shard_map.56.mine_ref, bf16[256,1152]{1,0:T(8,128)(2,1)} %collective-permute-done.3.other_ref), custom_call_target="tpu_custom_call" | custom-call | flops 509607936 | bytes 2617344 | tf_op jit(solution)/shard_map/pallas_call | solution.py:27
  48.5 0.7 copy-done.11
  49.2 0.6 collective-permute-done.11.mine_ref
  49.8 0.0 collective-permute-start.12
  49.8 0.0 collective-permute-done.4.other_ref
  49.8 2.7 %shard_map.59 = (bf16[288,512]{1,0:T(8,128)(2,1)}, bf16[144,512]{1,0:T(8,128)(2,1)S(1)}) custom-call(s32[1]{0:T(128)} %bitcast.3.place_ref.core_ref, bf16[432,1152]{1,0:T(8,128)(2,1)S(1)} %shard_map.55.weight_ref, bf16[256,1152]{1,0:T(8,128)(2,1)} %collective-permute-done.2.mine_ref, bf16[256,1152]{1,0:T(8,128)(2,1)} %collective-permute-done.4.other_ref), custom_call_target="tpu_custom_call" | custom-call | flops 509607936 | bytes 2617344 | tf_op jit(solution)/shard_map/pallas_call | solution.py:27
  52.5 0.0 collective-permute-done.5.other_ref
  52.5 2.7 %shard_map.60 = (bf16[288,512]{1,0:T(8,128)(2,1)}, bf16[144,512]{1,0:T(8,128)(2,1)S(1)}) custom-call(s32[1]{0:T(128)} %bitcast.3.place_ref.core_ref, bf16[432,1152]{1,0:T(8,128)(2,1)S(1)} %shard_map.55.weight_ref, bf16[256,1152]{1,0:T(8,128)(2,1)} %collective-permute-done.mine_ref, bf16[256,1152]{1,0:T(8,128)(2,1)} %collective-permute-done.5.other_ref), custom_call_target="tpu_custom_call" | custom-call | flops 509607936 | bytes 2617344 | tf_op jit(solution)/shard_map/pallas_call | solution.py:27
  55.2 0.7 copy-done.6
  55.9 3.8 %collective-permute-done.1.mine_ref = bf16[256,1152]{1,0:T(8,128)(2,1)} collective-permute-done((bf16[256,1152]{1,0:T(8,128)(2,1)}, bf16[256,1152]{1,0:T(8,128)(2,1)}, u32[]{:S(2)}, u32[]{:S(2)}) %collective-permute-start.1) | collective-permute-done | bytes 589856 | tf_op jit(solution)/shard_map/ppermute | solution.py:462
  59.6 0.0 collective-permute-start.6
  59.6 1.5 %collective-permute-start.13 = (bf16[288,512]{1,0:T(8,128)(2,1)}, bf16[288,512]{1,0:T(8,128)(2,1)}, u32[]{:S(2)}, u32[]{:S(2)}) collective-permute-start(bf16[288,512]{1,0:T(8,128)(2,1)} %get-tuple-element.24.refs_6_), channel_id=1, source_target_pairs={{0,2},{2,0},{1,3},{3,1},{4,6},{6,4},{5,7},{7,5},{8,10},{10,8},{9,1... | collective-permute-start | bytes 884744 | tf_op jit(solution)/shard_map/ppermute | solution.py:341
  61.1 0.5 collective-permute-start.14
  62.3 0.1 stack.36.refs_0_
  62.4 0.9 dynamic-slice_bitcast_fusion
  63.4 1.8 %shard_map.62.refs_9_ = bf16[288,512]{1,0:T(8,128)(2,1)S(1)} custom-call(s32[1]{0:T(128)} %bitcast.3.place_ref.core_ref, bf16[432,1152]{1,0:T(8,128)(2,1)S(1)} %shard_map.55.weight_ref, bf16[256,1152]{1,0:T(8,128)(2,1)} %collective-permute-done.11.mine_ref, bf16[256,1152]{1,0:T(8,128)(2,1)} %collective-permute-done.12.other_ref), custom_call_target="tpu_custom_call" | custom-call | flops 509607936 | bytes 2617344 | tf_op jit(solution)/shard_map/pallas_call | solution.py:27
  65.2 0.0 collective-permute-done.6.other_ref
  65.2 2.6 %shard_map.61 = (bf16[288,512]{1,0:T(8,128)(2,1)}, bf16[144,512]{1,0:T(8,128)(2,1)S(1)}) custom-call(s32[1]{0:T(128)} %bitcast.3.place_ref.core_ref, bf16[432,1152]{1,0:T(8,128)(2,1)S(1)} %shard_map.55.weight_ref, bf16[256,1152]{1,0:T(8,128)(2,1)} %collective-permute-done.1.mine_ref, bf16[256,1152]{1,0:T(8,128)(2,1)S(1)} %collective-permute-done.6.other_ref), custom_call_target="tpu_custom_call" | custom-call | flops 509607936 | bytes 2617344 | tf_op jit(solution)/shard_map/pallas_call | solution.py:27
  67.8 0.6 copy-done.8
  68.5 1.5 %collective-permute-start.10 = (bf16[288,512]{1,0:T(8,128)(2,1)}, bf16[288,512]{1,0:T(8,128)(2,1)S(1)}, u32[]{:S(2)}, u32[]{:S(2)}) collective-permute-start(bf16[288,512]{1,0:T(8,128)(2,1)} %get-tuple-element.27.refs_8_), channel_id=1, source_target_pairs={{0,2},{2,0},{1,3},{3,1},{4,6},{6,4},{5,7},{7,5},{8,10},{10,8},{9,1... | collective-permute-start | bytes 884744 | tf_op jit(solution)/shard_map/ppermute | solution.py:341
  70.0 0.9 broadcast_in_dim.7
  70.9 3.5 %all-to-all-start.2 = ((bf16[4,144,576]{2,1,0:T(8,128)(2,1)}), bf16[4,144,576]{2,1,0:T(8,128)(2,1)S(1)}, u32[]{:S(2)}, u32[]{:S(2)}) async-start(bf16[4,144,576]{2,1,0:T(8,128)(2,1)} %broadcast_in_dim.7), calls=%async_computation.2 | async-start | bytes 1474560 | tf_op jit(solution)/shard_map/all_to_all | solution.py:518
  74.4 0.0 collective-permute-done.13.refs_10_
  74.4 1.7 %collective-permute-done.14.refs_11_ = bf16[288,512]{1,0:T(8,128)(2,1)} collective-permute-done((bf16[288,512]{1,0:T(8,128)(2,1)}, bf16[288,512]{1,0:T(8,128)(2,1)}, u32[]{:S(2)}, u32[]{:S(2)}) %collective-permute-start.14) | collective-permute-done | bytes 294944 | tf_op jit(solution)/shard_map/ppermute | solution.py:341
  76.1 0.9 copy-done.9
  77.0 1.0 copy-done.12
  78.0 11.6 %shard_map.63 = (f32[8,1,512]{2,1,0:T(1,128)S(1)}, f32[8,80,512]{2,1,0:T(8,128)S(1)}) custom-call(s32[5]{0:T(128)S(1)} %stack.36.refs_0_, bf16[144,512]{1,0:T(8,128)(2,1)S(1)} %get-tuple-element.29.refs_1_, bf16[144,512]{1,0:T(8,128)(2,1)S(1)} %get-tuple-element.30.refs_2_, bf16[144,512]{1,0:T(8,128)(2,1)S(1)} %copy-done.7, bf16[144,512]{1,0:T(8,128)(2,1)S(1)} %copy-done.9, ...), custom_call_target="tpu_custom_call" | custom-call | flops 14495514624 | bytes 3538944 | tf_op jit(solution)/shard_map/pallas_call | solution.py:27
  89.6 0.0 collective-permute-done.10.refs_5_
  89.6 4.7 %shard_map.64 = bf16[4,144,512]{2,1,0:T(8,128)(2,1)} custom-call(s32[5]{0:T(128)S(1)} %stack.36.refs_0_, bf16[144,512]{1,0:T(8,128)(2,1)S(1)} %get-tuple-element.29.refs_1_, bf16[144,512]{1,0:T(8,128)(2,1)S(1)} %get-tuple-element.30.refs_2_, bf16[144,512]{1,0:T(8,128)(2,1)S(1)} %copy-done.7, bf16[144,512]{1,0:T(8,128)(2,1)S(1)} %copy-done.9, ...), custom_call_target="tpu_custom_call" | custom-call | flops 603979776 | bytes 3538944 | tf_op jit(solution)/shard_map/pallas_call | solution.py:27
  94.3 0.0 all-to-all-done.2.mine_ref
  94.3 3.5 %all-to-all-start.3 = ((bf16[4,144,512]{2,1,0:T(8,128)(2,1)}), bf16[4,144,512]{2,1,0:T(8,128)(2,1)S(1)}, u32[]{:S(2)}, u32[]{:S(2)}) async-start(bf16[4,144,512]{2,1,0:T(8,128)(2,1)} %shard_map.64), calls=%async_computation.3 | async-start | bytes 1179648 | tf_op jit(solution)/shard_map/all_to_all | solution.py:512
  97.8 0.9 collective-permute-start.8
  98.6 0.0 collective-permute-start.7
  98.6 17.0 %collective-permute-done.8.other_ref = bf16[4,144,576]{2,1,0:T(8,128)(2,1)} collective-permute-done((bf16[4,144,576]{2,1,0:T(8,128)(2,1)S(1)}, bf16[4,144,576]{2,1,0:T(8,128)(2,1)}, u32[]{:S(2)}, u32[]{:S(2)}) %collective-permute-start.8) | collective-permute-done | bytes 663584 | tf_op jit(solution)/shard_map/ppermute | solution.py:341
  115.7 0.0 collective-permute-start.9
  115.7 0.0 all-to-all-done.3
  115.7 0.5 collective-permute-start.15
  116.2 0.1 pad_add_fusion.where_ref
  116.3 1.1 copy-done.3
  117.3 1.8 %shard_map.65.start_ref = f32[576,512]{1,0:T(8,128)S(1)} custom-call(s32[4]{0:T(128)S(1)} %pad_add_fusion.where_ref, bf16[4,144,576]{2,1,0:T(8,128)(2,1)S(1)} %all-to-all-done.2.mine_ref, bf16[4,144,576]{2,1,0:T(8,128)(2,1)} %collective-permute-done.8.other_ref, bf16[576,512]{1,0:T(8,128)(2,1)S(1)} %bitcast.24, bf16[576,512]{1,0:T(8,128)(2,1)S(1)} %copy-done.3, ...), custom_call_target="tpu_custom_call" | custom-call | tf_op jit(solution)/shard_map/pallas_call | solution.py:27
  119.1 0.0 collective-permute-done.7.mine_ref
  119.1 0.0 collective-permute-done.9.other_ref
  119.2 2.8 %shard_map.66 = bf16[576,512]{1,0:T(8,128)(2,1)} custom-call(s32[4]{0:T(128)S(1)} %pad_add_fusion.where_ref, bf16[4,144,576]{2,1,0:T(8,128)(2,1)} %collective-permute-done.7.mine_ref, bf16[4,144,576]{2,1,0:T(8,128)(2,1)} %collective-permute-done.9.other_ref, bf16[576,512]{1,0:T(8,128)(2,1)S(1)} %collective-permute-done.15.heads_ref, ...), custom_call_target="tpu_custom_call" | custom-call | tf_op jit(solution)/shard_map/pallas_call | solution.py:27
  (21 shorter events, 0.1 us)
Async XLA Ops:
  0.0 1.3 %copy-start = (bf16[288,8,3,72]{0,3,2,1:T(8,128)(2,1)S(1)}, bf16[288,8,3,72]{0,3,2,1:T(8,128)(2,1)}, u32[]{:S(2)}) copy-start(bf16[288,8,3,72]{0,3,2,1:T(8,128)(2,1)} %param.7) | copy-start | bytes 2985988
  0.0 8.6 %copy-start.1 = (bf16[1,512,1152]{2,1,0:T(8,128)(2,1)S(1)}, bf16[1,512,1152]{2,1,0:T(8,128)(2,1)}, u32[]{:S(2)}) copy-start(bf16[1,512,1152]{2,1,0:T(8,128)(2,1)} %param.5) | copy-start | bytes 3538948
  0.0 8.6 %copy-start.10 = (f32[3,1152]{1,0:T(4,128)S(1)}, f32[3,1152]{1,0:T(4,128)}, u32[]{:S(2)}) copy-start(f32[3,1152]{1,0:T(4,128)} %mod_ref.3) | copy-start | bytes 41476
  2.3 17.0 %all-to-all-start = ((bf16[4,288,112]{2,1,0:T(8,128)(2,1)}), bf16[4,288,112]{2,1,0:T(8,128)(2,1)S(1)}, u32[]{:S(2)}, u32[]{:S(2)}) async-start(bf16[4,288,112]{2,1,0:T(8,128)(2,1)} %bitcast.8), calls=%async_computation | async-start | bytes 589824 | tf_op jit(solution)/shard_map/all_to_all | solution.py:488
  9.1 31.4 %collective-permute-start.2 = (bf16[256,1152]{1,0:T(8,128)(2,1)S(1)}, bf16[256,1152]{1,0:T(8,128)(2,1)}, u32[]{:S(2)}, u32[]{:S(2)}) collective-permute-start(bf16[256,1152]{1,0:T(8,128)(2,1)S(1)} %shard_map.56.mine_ref), channel_id=1, source_target_pairs={{0,4},{4,0},{8,12},{12,8},{1,5},{5,1},{9,13},{13,9},{2,6},{6,2},{1... | collective-permute-start | bytes 1769480 | tf_op jit(solution)/shard_map/ppermute | solution.py:462
  11.2 32.4 %collective-permute-start = (bf16[256,1152]{1,0:T(8,128)(2,1)S(1)}, bf16[256,1152]{1,0:T(8,128)(2,1)}, u32[]{:S(2)}, u32[]{:S(2)}) collective-permute-start(bf16[256,1152]{1,0:T(8,128)(2,1)S(1)} %shard_map.56.mine_ref), channel_id=1, source_target_pairs={{0,8},{4,12},{8,0},{12,4},{1,9},{5,13},{9,1},{13,5},{2,10},{6,14},... | collective-permute-start | bytes 1769480 | tf_op jit(solution)/shard_map/ppermute | solution.py:462
  20.4 24.5 %all-to-all-start.1 = ((bf16[4,4,288,112]{3,2,1,0:T(8,128)(2,1)}), bf16[4,4,288,112]{3,2,1,0:T(8,128)(2,1)}, u32[]{:S(2)}, u32[]{:S(2)}) async-start(bf16[4,4,288,112]{3,2,1,0:T(8,128)(2,1)} %broadcast_in_dim.6), calls=%async_computation.1 | async-start | bytes 2359296 | tf_op jit(solution)/shard_map/all_to_all | solution.py:489
  24.7 21.9 %collective-permute-start.3 = (bf16[256,1152]{1,0:T(8,128)(2,1)S(1)}, bf16[256,1152]{1,0:T(8,128)(2,1)}, u32[]{:S(2)}, u32[]{:S(2)}) collective-permute-start(bf16[256,1152]{1,0:T(8,128)(2,1)S(1)} %shard_map.56.mine_ref), channel_id=1, source_target_pairs={{0,1},{1,0},{2,3},{3,2},{4,5},{5,4},{6,7},{7,6},{8,9},{9,8},{10,11... | collective-permute-start | bytes 1769480 | tf_op jit(solution)/shard_map/ppermute | solution.py:341
  24.8 25.0 %collective-permute-start.11 = (bf16[256,1152]{1,0:T(8,128)(2,1)S(1)}, bf16[256,1152]{1,0:T(8,128)(2,1)}, u32[]{:S(2)}, u32[]{:S(2)}) collective-permute-start(bf16[256,1152]{1,0:T(8,128)(2,1)S(1)} %shard_map.56.mine_ref), channel_id=1, source_target_pairs={{0,2},{2,0},{1,3},{3,1},{4,6},{6,4},{5,7},{7,5},{8,10},{10,8},{9,1... | collective-permute-start | bytes 1769480 | tf_op jit(solution)/shard_map/ppermute | solution.py:341
  40.5 9.3 %collective-permute-start.4 = (bf16[256,1152]{1,0:T(8,128)(2,1)}, bf16[256,1152]{1,0:T(8,128)(2,1)}, u32[]{:S(2)}, u32[]{:S(2)}) collective-permute-start(bf16[256,1152]{1,0:T(8,128)(2,1)} %collective-permute-done.2.mine_ref), channel_id=1, source_target_pairs={{0,1},{1,0},{2,3},{3,2},{4,5},{5,4},{6,7},{7,6},{8,9},{9,8},{10,11... | collective-permute-start | bytes 1769480 | tf_op jit(solution)/shard_map/ppermute | solution.py:341
  43.6 8.9 %collective-permute-start.5 = (bf16[256,1152]{1,0:T(8,128)(2,1)}, bf16[256,1152]{1,0:T(8,128)(2,1)}, u32[]{:S(2)}, u32[]{:S(2)}) collective-permute-start(bf16[256,1152]{1,0:T(8,128)(2,1)} %collective-permute-done.mine_ref), channel_id=1, source_target_pairs={{0,1},{1,0},{2,3},{3,2},{4,5},{5,4},{6,7},{7,6},{8,9},{9,8},{10,11... | collective-permute-start | bytes 1769480 | tf_op jit(solution)/shard_map/ppermute | solution.py:341
  43.6 16.1 %collective-permute-start.1 = (bf16[256,1152]{1,0:T(8,128)(2,1)}, bf16[256,1152]{1,0:T(8,128)(2,1)}, u32[]{:S(2)}, u32[]{:S(2)}) collective-permute-start(bf16[256,1152]{1,0:T(8,128)(2,1)} %collective-permute-done.mine_ref), channel_id=1, source_target_pairs={{0,4},{4,0},{8,12},{12,8},{1,5},{5,1},{9,13},{13,9},{2,6},{6,2},{1... | collective-permute-start | bytes 1769480 | tf_op jit(solution)/shard_map/ppermute | solution.py:462
  44.1 0.8 copy-start.2
  48.5 0.7 copy-start.11
  49.8 13.6 %collective-permute-start.12 = (bf16[256,1152]{1,0:T(8,128)(2,1)}, bf16[256,1152]{1,0:T(8,128)(2,1)}, u32[]{:S(2)}, u32[]{:S(2)}) collective-permute-start(bf16[256,1152]{1,0:T(8,128)(2,1)} %collective-permute-done.11.mine_ref), channel_id=1, source_target_pairs={{0,1},{1,0},{2,3},{3,2},{4,5},{5,4},{6,7},{7,6},{8,9},{9,8},{10,11... | collective-permute-start | bytes 1769480 | tf_op jit(solution)/shard_map/ppermute | solution.py:341
  55.2 0.7 copy-start.6
  59.6 5.6 %collective-permute-start.6 = (bf16[256,1152]{1,0:T(8,128)(2,1)}, bf16[256,1152]{1,0:T(8,128)(2,1)S(1)}, u32[]{:S(2)}, u32[]{:S(2)}) collective-permute-start(bf16[256,1152]{1,0:T(8,128)(2,1)} %collective-permute-done.1.mine_ref), channel_id=1, source_target_pairs={{0,1},{1,0},{2,3},{3,2},{4,5},{5,4},{6,7},{7,6},{8,9},{9,8},{10,11... | collective-permute-start | bytes 1769480 | tf_op jit(solution)/shard_map/ppermute | solution.py:341
  59.6 14.8 %collective-permute-start.13 = (bf16[288,512]{1,0:T(8,128)(2,1)}, bf16[288,512]{1,0:T(8,128)(2,1)}, u32[]{:S(2)}, u32[]{:S(2)}) collective-permute-start(bf16[288,512]{1,0:T(8,128)(2,1)} %get-tuple-element.24.refs_6_), channel_id=1, source_target_pairs={{0,2},{2,0},{1,3},{3,1},{4,6},{6,4},{5,7},{7,5},{8,10},{10,8},{9,1... | collective-permute-start | bytes 884744 | tf_op jit(solution)/shard_map/ppermute | solution.py:341
  61.1 14.9 %collective-permute-start.14 = (bf16[288,512]{1,0:T(8,128)(2,1)}, bf16[288,512]{1,0:T(8,128)(2,1)}, u32[]{:S(2)}, u32[]{:S(2)}) collective-permute-start(bf16[288,512]{1,0:T(8,128)(2,1)} %get-tuple-element.25.refs_7_), channel_id=1, source_target_pairs={{0,2},{2,0},{1,3},{3,1},{4,6},{6,4},{5,7},{7,5},{8,10},{10,8},{9,1... | collective-permute-start | bytes 884744 | tf_op jit(solution)/shard_map/ppermute | solution.py:341
  65.2 2.6 %copy-start.4 = (bf16[288,512]{1,0:T(8,128)(2,1)}, bf16[288,512]{1,0:T(8,128)(2,1)S(1)}, u32[]{:S(2)}) copy-start(bf16[288,512]{1,0:T(8,128)(2,1)S(1)} %shard_map.62.refs_9_) | copy-start | bytes 884740
  67.8 0.6 copy-start.8
  68.5 7.6 %copy-start.5 = (bf16[288,512]{1,0:T(8,128)(2,1)S(1)}, bf16[288,512]{1,0:T(8,128)(2,1)}, u32[]{:S(2)}) copy-start(bf16[288,512]{1,0:T(8,128)(2,1)} %copy-done.4) | copy-start | bytes 884740
  68.5 7.6 %copy-start.7 = (bf16[144,512]{1,0:T(8,128)(2,1)S(1)}, bf16[144,512]{1,0:T(8,128)(2,1)}, u32[]{:S(2)}) copy-start(bf16[144,512]{1,0:T(8,128)(2,1)} %copy-done.6) | copy-start | bytes 442372
  68.5 21.1 %collective-permute-start.10 = (bf16[288,512]{1,0:T(8,128)(2,1)}, bf16[288,512]{1,0:T(8,128)(2,1)S(1)}, u32[]{:S(2)}, u32[]{:S(2)}) collective-permute-start(bf16[288,512]{1,0:T(8,128)(2,1)} %get-tuple-element.27.refs_8_), channel_id=1, source_target_pairs={{0,2},{2,0},{1,3},{3,1},{4,6},{6,4},{5,7},{7,5},{8,10},{10,8},{9,1... | collective-permute-start | bytes 884744 | tf_op jit(solution)/shard_map/ppermute | solution.py:341
  70.9 23.3 %all-to-all-start.2 = ((bf16[4,144,576]{2,1,0:T(8,128)(2,1)}), bf16[4,144,576]{2,1,0:T(8,128)(2,1)S(1)}, u32[]{:S(2)}, u32[]{:S(2)}) async-start(bf16[4,144,576]{2,1,0:T(8,128)(2,1)} %broadcast_in_dim.7), calls=%async_computation.2 | async-start | bytes 1474560 | tf_op jit(solution)/shard_map/all_to_all | solution.py:518
  76.1 0.9 copy-start.9
  77.0 1.0 copy-start.12
  94.3 21.4 %all-to-all-start.3 = ((bf16[4,144,512]{2,1,0:T(8,128)(2,1)}), bf16[4,144,512]{2,1,0:T(8,128)(2,1)S(1)}, u32[]{:S(2)}, u32[]{:S(2)}) async-start(bf16[4,144,512]{2,1,0:T(8,128)(2,1)} %shard_map.64), calls=%async_computation.3 | async-start | bytes 1179648 | tf_op jit(solution)/shard_map/all_to_all | solution.py:512
  97.8 17.9 %collective-permute-start.8 = (bf16[4,144,576]{2,1,0:T(8,128)(2,1)S(1)}, bf16[4,144,576]{2,1,0:T(8,128)(2,1)}, u32[]{:S(2)}, u32[]{:S(2)}) collective-permute-start(bf16[4,144,576]{2,1,0:T(8,128)(2,1)S(1)} %all-to-all-done.2.mine_ref), channel_id=1, source_target_pairs={{0,16},{16,0},{1,17},{17,1},{2,18},{18,2},{3,19},{19,3},{4,20},{20... | collective-permute-start | bytes 1990664 | tf_op jit(solution)/shard_map/ppermute | solution.py:341
  98.6 20.5 %collective-permute-start.7 = (bf16[4,144,576]{2,1,0:T(8,128)(2,1)S(1)}, bf16[4,144,576]{2,1,0:T(8,128)(2,1)}, u32[]{:S(2)}, u32[]{:S(2)}) collective-permute-start(bf16[4,144,576]{2,1,0:T(8,128)(2,1)S(1)} %all-to-all-done.2.mine_ref), channel_id=1, source_target_pairs={{0,1},{1,0},{2,3},{3,2},{4,5},{5,4},{6,7},{7,6},{8,9},{9,8},{10,11... | collective-permute-start | bytes 1990664 | tf_op jit(solution)/shard_map/ppermute | solution.py:341
  115.7 3.5 %collective-permute-start.9 = (bf16[4,144,576]{2,1,0:T(8,128)(2,1)}, bf16[4,144,576]{2,1,0:T(8,128)(2,1)}, u32[]{:S(2)}, u32[]{:S(2)}) collective-permute-start(bf16[4,144,576]{2,1,0:T(8,128)(2,1)} %collective-permute-done.8.other_ref), channel_id=1, source_target_pairs={{0,1},{1,0},{2,3},{3,2},{4,5},{5,4},{6,7},{7,6},{8,9},{9,8},{10,11... | collective-permute-start | bytes 1990664 | tf_op jit(solution)/shard_map/ppermute | solution.py:341
  115.7 3.5 %collective-permute-start.15 = (bf16[576,512]{1,0:T(8,128)(2,1)S(1)}, bf16[576,512]{1,0:T(8,128)(2,1)S(1)}, u32[]{:S(2)}, u32[]{:S(2)}) collective-permute-start(bf16[576,512]{1,0:T(8,128)(2,1)S(1)} %bitcast.23), channel_id=1, source_target_pairs={{0,1},{1,0},{2,3},{3,2},{4,5},{5,4},{6,7},{7,6},{8,9},{9,8},{10,11... | collective-permute-start | bytes 1769480 | tf_op jit(solution)/shard_map/ppermute | solution.py:341
  116.3 1.1 copy-start.3

commit v6 on v5

--- a/solution.py
+++ b/solution.py
@@ -314,17 +314,17 @@
     )
 
 
-def part_kernel(where_ref, mine_ref, other_ref, heads_ref, start_ref, gate_ref, out_ref, weight):
+def part_kernel(where_ref, mine_ref, other_ref, heads_ref, start_ref, gate_ref, out_ref):
     group, core = where_ref[1], where_ref[3]
     block = mine_ref.shape[1]
     per_core = mine_ref.shape[0] // 2
     for same, ref in ((True, mine_ref), (False, other_ref)):
         half = group if same else 1 - group
         for index in range(per_core):
-            start = pl.multiple_of((index * 2 + half) * block, block)
-            weight[pl.ds(start, block), :] = ref[core * per_core + index]
-    projected = dot_nn(weight[...], heads_ref[...])
-    out_ref[...] = (start_ref[...].astype(jnp.float32) + gate_ref[:, 0:1] * projected).astype(out_ref.dtype)
+            rows = pl.ds(pl.multiple_of((index * 2 + half) * block, block), block)
+            projected = dot_nn(ref[core * per_core + index], heads_ref[...])
+            updated = start_ref[rows, :].astype(jnp.float32) + gate_ref[rows, 0:1] * projected
+            out_ref[rows, :] = updated.astype(out_ref.dtype)
 
 
 def add_part(where, mine, other, heads, start, gate, dtype):
@@ -332,7 +332,6 @@
         part_kernel,
         jax.ShapeDtypeStruct(start.shape, dtype),
         (where, mine, other, heads, start, gate),
-        [pltpu.VMEM((start.shape[0], mine.shape[2]), jnp.bfloat16)],
         grant=16,
     )
 

time: 122 us -> 123 us (level)
  no operation moved by 1% of the time
where the time goes in v6:
time: 123 us; the launch traced here: 122 us
  waiting for transfers between devices  45.7 us (37%)
  Pallas kernels  35.3 us (29%)
  starting transfers between devices  28.9 us (23%)
  local copies, waits for them, and re-layouts  11.1 us (9%)
    pallas_call x12, Pallas kernels, call(): pl.pallas_call(kernel, out_shape=out_shape, in_specs=[where if i in left...  35.3 us
    ppermute x3, waiting for transfers between devices, flipped(): lax.ppermute(block, axis, [(i, i ^ distance) for i in range(lax.axis_size...  20.7 us
    ppermute x13, waiting for transfers between devices, swapped(): return lax.ppermute(block, axis, [(0, 1), (1, 0)])  19.3 us
    unnamed x26, local copies, waits for them, and re-layouts  7.09 us
    ppermute x13, starting transfers between devices, swapped(): return lax.ppermute(block, axis, [(0, 1), (1, 0)])  6.89 us
    all_to_all x1, starting transfers between devices, by_heads(): part = lax.all_to_all(part, 'frame', 0, 0)  6.32 us
    all_to_all x1, waiting for transfers between devices, by_heads(): part = lax.all_to_all(part, 'frame', 0, 0)  5.71 us
    ppermute x3, starting transfers between devices, flipped(): lax.ppermute(block, axis, [(i, i ^ distance) for i in range(lax.axis_size...  4.45 us
  transfers between devices with their start and end apart: 20, of which 7 were waited for; matrix products, arithmetic and copies ran while one was open for 3% of the time, Pallas kernels for 27%

profile of v6, /device:TPU:0, one launch (start us, length us, event | category | flops | bytes accessed | tf_op | source)
XLA Modules:
  0.0 122.0 jit_solution(7420613814259658335)
XLA Ops:
  0.0 1.3 %copy-done = bf16[288,8,3,72]{0,3,2,1:T(8,128)(2,1)S(1)} copy-done((bf16[288,8,3,72]{0,3,2,1:T(8,128)(2,1)S(1)}, bf16[288,8,3,72]{0,3,2,1:T(8,128)(2,1)}, u32[]{:S(2)}) %copy-start) | copy-done | bytes 995352
  1.4 0.9 copy.6
  2.3 6.3 %all-to-all-start = ((bf16[4,288,112]{2,1,0:T(8,128)(2,1)}), bf16[4,288,112]{2,1,0:T(8,128)(2,1)S(1)}, u32[]{:S(2)}, u32[]{:S(2)}) async-start(bf16[4,288,112]{2,1,0:T(8,128)(2,1)} %bitcast.8), calls=%async_computation | async-start | bytes 589824 | tf_op jit(solution)/shard_map/all_to_all | solution.py:487
  8.6 0.5 shard_map.56.mine_ref
  9.1 2.1 %collective-permute-start.2 = (bf16[256,1152]{1,0:T(8,128)(2,1)S(1)}, bf16[256,1152]{1,0:T(8,128)(2,1)}, u32[]{:S(2)}, u32[]{:S(2)}) collective-permute-start(bf16[256,1152]{1,0:T(8,128)(2,1)S(1)} %shard_map.56.mine_ref), channel_id=1, source_target_pairs={{0,4},{4,0},{8,12},{12,8},{1,5},{5,1},{9,13},{13,9},{2,6},{6,2},{1... | collective-permute-start | bytes 1769480 | tf_op jit(solution)/shard_map/ppermute | solution.py:461
  11.2 2.4 %collective-permute-start = (bf16[256,1152]{1,0:T(8,128)(2,1)S(1)}, bf16[256,1152]{1,0:T(8,128)(2,1)}, u32[]{:S(2)}, u32[]{:S(2)}) collective-permute-start(bf16[256,1152]{1,0:T(8,128)(2,1)S(1)} %shard_map.56.mine_ref), channel_id=1, source_target_pairs={{0,8},{4,12},{8,0},{12,4},{1,9},{5,13},{9,1},{13,5},{2,10},{6,14},... | collective-permute-start | bytes 1769480 | tf_op jit(solution)/shard_map/ppermute | solution.py:461
  13.6 5.7 %all-to-all-done = bf16[4,288,112]{2,1,0:T(8,128)(2,1)S(1)} async-done(((bf16[4,288,112]{2,1,0:T(8,128)(2,1)}), bf16[4,288,112]{2,1,0:T(8,128)(2,1)S(1)}, u32[]{:S(2)}, u32[]{:S(2)}) %all-to-all-start) | async-done | bytes 258080 | tf_op jit(solution)/shard_map/all_to_all | solution.py:487
  19.3 1.2 broadcast_in_dim.6
  20.4 4.3 %all-to-all-start.1 = ((bf16[4,4,288,112]{3,2,1,0:T(8,128)(2,1)}), bf16[4,4,288,112]{3,2,1,0:T(8,128)(2,1)}, u32[]{:S(2)}, u32[]{:S(2)}) async-start(bf16[4,4,288,112]{3,2,1,0:T(8,128)(2,1)} %broadcast_in_dim.6), calls=%async_computation.1 | async-start | bytes 2359296 | tf_op jit(solution)/shard_map/all_to_all | solution.py:488
  24.7 0.1 collective-permute-start.3
  24.8 1.9 %collective-permute-start.11 = (bf16[256,1152]{1,0:T(8,128)(2,1)S(1)}, bf16[256,1152]{1,0:T(8,128)(2,1)}, u32[]{:S(2)}, u32[]{:S(2)}) collective-permute-start(bf16[256,1152]{1,0:T(8,128)(2,1)S(1)} %shard_map.56.mine_ref), channel_id=1, source_target_pairs={{0,2},{2,0},{1,3},{3,1},{4,6},{6,4},{5,7},{7,5},{8,10},{10,8},{9,1... | collective-permute-start | bytes 1769480 | tf_op jit(solution)/shard_map/ppermute | solution.py:340
  26.7 13.8 %collective-permute-done.2.mine_ref = bf16[256,1152]{1,0:T(8,128)(2,1)} collective-permute-done((bf16[256,1152]{1,0:T(8,128)(2,1)S(1)}, bf16[256,1152]{1,0:T(8,128)(2,1)}, u32[]{:S(2)}, u32[]{:S(2)}) %collective-permute-start.2) | collective-permute-done | bytes 589856 | tf_op jit(solution)/shard_map/ppermute | solution.py:461
  40.5 0.0 collective-permute-start.4
  40.5 3.1 %collective-permute-done.mine_ref = bf16[256,1152]{1,0:T(8,128)(2,1)} collective-permute-done((bf16[256,1152]{1,0:T(8,128)(2,1)S(1)}, bf16[256,1152]{1,0:T(8,128)(2,1)}, u32[]{:S(2)}, u32[]{:S(2)}) %collective-permute-start) | collective-permute-done | bytes 589856 | tf_op jit(solution)/shard_map/ppermute | solution.py:461
  43.6 0.0 collective-permute-start.5
  43.6 0.0 collective-permute-start.1
  43.6 0.5 shard_map.57
  44.1 0.8 copy-done.2
  45.0 0.0 all-to-all-done.1.parts_ref
  45.0 1.6 %shard_map.55.weight_ref = bf16[432,1152]{1,0:T(8,128)(2,1)S(1)} custom-call(bf16[4,4,288,112]{3,2,1,0:T(8,128)(2,1)} %all-to-all-done.1.parts_ref), custom_call_target="tpu_custom_call" | custom-call | tf_op jit(solution)/shard_map/pallas_call | solution.py:27
  46.6 0.0 collective-permute-done.3.other_ref
  46.6 1.8 %shard_map.58 = (bf16[288,512]{1,0:T(8,128)(2,1)S(1)}, bf16[144,512]{1,0:T(8,128)(2,1)S(1)}) custom-call(s32[1]{0:T(128)} %bitcast.3.place_ref.core_ref, bf16[432,1152]{1,0:T(8,128)(2,1)S(1)} %shard_map.55.weight_ref, bf16[256,1152]{1,0:T(8,128)(2,1)S(1)} %shard_map.56.mine_ref, bf16[256,1152]{1,0:T(8,128)(2,1)} %collective-permute-done.3.other_ref), custom_call_target="tpu_custom_call" | custom-call | flops 509607936 | bytes 2617344 | tf_op jit(solution)/shard_map/pallas_call | solution.py:27
  48.5 0.7 copy-done.11
  49.2 0.6 collective-permute-done.11.mine_ref
  49.8 0.0 collective-permute-start.12
  49.8 0.0 collective-permute-done.4.other_ref
  49.8 2.7 %shard_map.59 = (bf16[288,512]{1,0:T(8,128)(2,1)}, bf16[144,512]{1,0:T(8,128)(2,1)S(1)}) custom-call(s32[1]{0:T(128)} %bitcast.3.place_ref.core_ref, bf16[432,1152]{1,0:T(8,128)(2,1)S(1)} %shard_map.55.weight_ref, bf16[256,1152]{1,0:T(8,128)(2,1)} %collective-permute-done.2.mine_ref, bf16[256,1152]{1,0:T(8,128)(2,1)} %collective-permute-done.4.other_ref), custom_call_target="tpu_custom_call" | custom-call | flops 509607936 | bytes 2617344 | tf_op jit(solution)/shard_map/pallas_call | solution.py:27
  52.5 0.0 collective-permute-done.5.other_ref
  52.5 2.7 %shard_map.60 = (bf16[288,512]{1,0:T(8,128)(2,1)}, bf16[144,512]{1,0:T(8,128)(2,1)S(1)}) custom-call(s32[1]{0:T(128)} %bitcast.3.place_ref.core_ref, bf16[432,1152]{1,0:T(8,128)(2,1)S(1)} %shard_map.55.weight_ref, bf16[256,1152]{1,0:T(8,128)(2,1)} %collective-permute-done.mine_ref, bf16[256,1152]{1,0:T(8,128)(2,1)} %collective-permute-done.5.other_ref), custom_call_target="tpu_custom_call" | custom-call | flops 509607936 | bytes 2617344 | tf_op jit(solution)/shard_map/pallas_call | solution.py:27
  55.2 0.7 copy-done.6
  55.9 3.8 %collective-permute-done.1.mine_ref = bf16[256,1152]{1,0:T(8,128)(2,1)} collective-permute-done((bf16[256,1152]{1,0:T(8,128)(2,1)}, bf16[256,1152]{1,0:T(8,128)(2,1)}, u32[]{:S(2)}, u32[]{:S(2)}) %collective-permute-start.1) | collective-permute-done | bytes 589856 | tf_op jit(solution)/shard_map/ppermute | solution.py:461
  59.6 0.0 collective-permute-start.6
  59.6 1.5 %collective-permute-start.13 = (bf16[288,512]{1,0:T(8,128)(2,1)}, bf16[288,512]{1,0:T(8,128)(2,1)}, u32[]{:S(2)}, u32[]{:S(2)}) collective-permute-start(bf16[288,512]{1,0:T(8,128)(2,1)} %get-tuple-element.24.refs_6_), channel_id=1, source_target_pairs={{0,2},{2,0},{1,3},{3,1},{4,6},{6,4},{5,7},{7,5},{8,10},{10,8},{9,1... | collective-permute-start | bytes 884744 | tf_op jit(solution)/shard_map/ppermute | solution.py:340
  61.1 0.5 collective-permute-start.14
  62.3 0.1 stack.36.refs_0_
  62.4 0.9 dynamic-slice_bitcast_fusion
  63.4 0.0 collective-permute-done.12.other_ref
  63.4 1.8 %shard_map.62.refs_9_ = bf16[288,512]{1,0:T(8,128)(2,1)S(1)} custom-call(s32[1]{0:T(128)} %bitcast.3.place_ref.core_ref, bf16[432,1152]{1,0:T(8,128)(2,1)S(1)} %shard_map.55.weight_ref, bf16[256,1152]{1,0:T(8,128)(2,1)} %collective-permute-done.11.mine_ref, bf16[256,1152]{1,0:T(8,128)(2,1)} %collective-permute-done.12.other_ref), custom_call_target="tpu_custom_call" | custom-call | flops 509607936 | bytes 2617344 | tf_op jit(solution)/shard_map/pallas_call | solution.py:27
  65.2 0.0 collective-permute-done.6.other_ref
  65.2 2.6 %shard_map.61 = (bf16[288,512]{1,0:T(8,128)(2,1)}, bf16[144,512]{1,0:T(8,128)(2,1)S(1)}) custom-call(s32[1]{0:T(128)} %bitcast.3.place_ref.core_ref, bf16[432,1152]{1,0:T(8,128)(2,1)S(1)} %shard_map.55.weight_ref, bf16[256,1152]{1,0:T(8,128)(2,1)} %collective-permute-done.1.mine_ref, bf16[256,1152]{1,0:T(8,128)(2,1)S(1)} %collective-permute-done.6.other_ref), custom_call_target="tpu_custom_call" | custom-call | flops 509607936 | bytes 2617344 | tf_op jit(solution)/shard_map/pallas_call | solution.py:27
  67.8 0.6 copy-done.8
  68.5 1.5 %collective-permute-start.10 = (bf16[288,512]{1,0:T(8,128)(2,1)}, bf16[288,512]{1,0:T(8,128)(2,1)S(1)}, u32[]{:S(2)}, u32[]{:S(2)}) collective-permute-start(bf16[288,512]{1,0:T(8,128)(2,1)} %get-tuple-element.27.refs_8_), channel_id=1, source_target_pairs={{0,2},{2,0},{1,3},{3,1},{4,6},{6,4},{5,7},{7,5},{8,10},{10,8},{9,1... | collective-permute-start | bytes 884744 | tf_op jit(solution)/shard_map/ppermute | solution.py:340
  70.0 0.9 broadcast_in_dim.7
  70.9 3.5 %all-to-all-start.2 = ((bf16[4,144,576]{2,1,0:T(8,128)(2,1)}), bf16[4,144,576]{2,1,0:T(8,128)(2,1)S(1)}, u32[]{:S(2)}, u32[]{:S(2)}) async-start(bf16[4,144,576]{2,1,0:T(8,128)(2,1)} %broadcast_in_dim.7), calls=%async_computation.2 | async-start | bytes 1474560 | tf_op jit(solution)/shard_map/all_to_all | solution.py:517
  74.4 0.0 collective-permute-done.13.refs_10_
  74.4 1.7 %collective-permute-done.14.refs_11_ = bf16[288,512]{1,0:T(8,128)(2,1)} collective-permute-done((bf16[288,512]{1,0:T(8,128)(2,1)}, bf16[288,512]{1,0:T(8,128)(2,1)}, u32[]{:S(2)}, u32[]{:S(2)}) %collective-permute-start.14) | collective-permute-done | bytes 294944 | tf_op jit(solution)/shard_map/ppermute | solution.py:340
  76.1 0.9 copy-done.9
  77.0 1.0 copy-done.12
  78.0 11.6 %shard_map.63 = (f32[8,1,512]{2,1,0:T(1,128)S(1)}, f32[8,80,512]{2,1,0:T(8,128)S(1)}) custom-call(s32[5]{0:T(128)S(1)} %stack.36.refs_0_, bf16[144,512]{1,0:T(8,128)(2,1)S(1)} %get-tuple-element.29.refs_1_, bf16[144,512]{1,0:T(8,128)(2,1)S(1)} %get-tuple-element.30.refs_2_, bf16[144,512]{1,0:T(8,128)(2,1)S(1)} %copy-done.7, bf16[144,512]{1,0:T(8,128)(2,1)S(1)} %copy-done.9, ...), custom_call_target="tpu_custom_call" | custom-call | flops 14495514624 | bytes 3538944 | tf_op jit(solution)/shard_map/pallas_call | solution.py:27
  89.6 0.0 collective-permute-done.10.refs_5_
  89.6 4.7 %shard_map.64 = bf16[4,144,512]{2,1,0:T(8,128)(2,1)} custom-call(s32[5]{0:T(128)S(1)} %stack.36.refs_0_, bf16[144,512]{1,0:T(8,128)(2,1)S(1)} %get-tuple-element.29.refs_1_, bf16[144,512]{1,0:T(8,128)(2,1)S(1)} %get-tuple-element.30.refs_2_, bf16[144,512]{1,0:T(8,128)(2,1)S(1)} %copy-done.7, bf16[144,512]{1,0:T(8,128)(2,1)S(1)} %copy-done.9, ...), custom_call_target="tpu_custom_call" | custom-call | flops 603979776 | bytes 3538944 | tf_op jit(solution)/shard_map/pallas_call | solution.py:27
  94.3 0.0 all-to-all-done.2.mine_ref
  94.3 3.5 %all-to-all-start.3 = ((bf16[4,144,512]{2,1,0:T(8,128)(2,1)}), bf16[4,144,512]{2,1,0:T(8,128)(2,1)S(1)}, u32[]{:S(2)}, u32[]{:S(2)}) async-start(bf16[4,144,512]{2,1,0:T(8,128)(2,1)} %shard_map.64), calls=%async_computation.3 | async-start | bytes 1179648 | tf_op jit(solution)/shard_map/all_to_all | solution.py:511
  97.8 0.9 collective-permute-start.8
  98.6 0.0 collective-permute-start.7
  98.6 17.0 %collective-permute-done.8.other_ref = bf16[4,144,576]{2,1,0:T(8,128)(2,1)} collective-permute-done((bf16[4,144,576]{2,1,0:T(8,128)(2,1)S(1)}, bf16[4,144,576]{2,1,0:T(8,128)(2,1)}, u32[]{:S(2)}, u32[]{:S(2)}) %collective-permute-start.8) | collective-permute-done | bytes 663584 | tf_op jit(solution)/shard_map/ppermute | solution.py:340
  115.7 0.0 collective-permute-start.9
  115.7 0.0 all-to-all-done.3
  115.7 0.5 collective-permute-start.15
  116.2 0.1 pad_add_fusion.where_ref
  116.3 1.1 copy-done.3
  117.3 1.8 %shard_map.65.start_ref = f32[576,512]{1,0:T(8,128)S(1)} custom-call(s32[4]{0:T(128)S(1)} %pad_add_fusion.where_ref, bf16[4,144,576]{2,1,0:T(8,128)(2,1)S(1)} %all-to-all-done.2.mine_ref, bf16[4,144,576]{2,1,0:T(8,128)(2,1)} %collective-permute-done.8.other_ref, bf16[576,512]{1,0:T(8,128)(2,1)S(1)} %bitcast.24, bf16[576,512]{1,0:T(8,128)(2,1)S(1)} %copy-done.3, ...), custom_call_target="tpu_custom_call" | custom-call | tf_op jit(solution)/shard_map/pallas_call | solution.py:27
  119.1 0.0 collective-permute-done.15.heads_ref
  119.1 2.8 %shard_map.66 = bf16[576,512]{1,0:T(8,128)(2,1)} custom-call(s32[4]{0:T(128)S(1)} %pad_add_fusion.where_ref, bf16[4,144,576]{2,1,0:T(8,128)(2,1)} %collective-permute-done.7.mine_ref, bf16[4,144,576]{2,1,0:T(8,128)(2,1)} %collective-permute-done.9.other_ref, bf16[576,512]{1,0:T(8,128)(2,1)S(1)} %collective-permute-done.15.heads_ref, ...), custom_call_target="tpu_custom_call" | custom-call | tf_op jit(solution)/shard_map/pallas_call | solution.py:27
  (21 shorter events, 0.1 us)
Async XLA Ops:
  0.0 1.3 %copy-start = (bf16[288,8,3,72]{0,3,2,1:T(8,128)(2,1)S(1)}, bf16[288,8,3,72]{0,3,2,1:T(8,128)(2,1)}, u32[]{:S(2)}) copy-start(bf16[288,8,3,72]{0,3,2,1:T(8,128)(2,1)} %param.7) | copy-start | bytes 2985988
  0.0 8.6 %copy-start.1 = (bf16[1,512,1152]{2,1,0:T(8,128)(2,1)S(1)}, bf16[1,512,1152]{2,1,0:T(8,128)(2,1)}, u32[]{:S(2)}) copy-start(bf16[1,512,1152]{2,1,0:T(8,128)(2,1)} %param.5) | copy-start | bytes 3538948
  0.0 8.6 %copy-start.10 = (f32[3,1152]{1,0:T(4,128)S(1)}, f32[3,1152]{1,0:T(4,128)}, u32[]{:S(2)}) copy-start(f32[3,1152]{1,0:T(4,128)} %mod_ref.3) | copy-start | bytes 41476
  2.3 17.0 %all-to-all-start = ((bf16[4,288,112]{2,1,0:T(8,128)(2,1)}), bf16[4,288,112]{2,1,0:T(8,128)(2,1)S(1)}, u32[]{:S(2)}, u32[]{:S(2)}) async-start(bf16[4,288,112]{2,1,0:T(8,128)(2,1)} %bitcast.8), calls=%async_computation | async-start | bytes 589824 | tf_op jit(solution)/shard_map/all_to_all | solution.py:487
  9.1 31.4 %collective-permute-start.2 = (bf16[256,1152]{1,0:T(8,128)(2,1)S(1)}, bf16[256,1152]{1,0:T(8,128)(2,1)}, u32[]{:S(2)}, u32[]{:S(2)}) collective-permute-start(bf16[256,1152]{1,0:T(8,128)(2,1)S(1)} %shard_map.56.mine_ref), channel_id=1, source_target_pairs={{0,4},{4,0},{8,12},{12,8},{1,5},{5,1},{9,13},{13,9},{2,6},{6,2},{1... | collective-permute-start | bytes 1769480 | tf_op jit(solution)/shard_map/ppermute | solution.py:461
  11.2 32.4 %collective-permute-start = (bf16[256,1152]{1,0:T(8,128)(2,1)S(1)}, bf16[256,1152]{1,0:T(8,128)(2,1)}, u32[]{:S(2)}, u32[]{:S(2)}) collective-permute-start(bf16[256,1152]{1,0:T(8,128)(2,1)S(1)} %shard_map.56.mine_ref), channel_id=1, source_target_pairs={{0,8},{4,12},{8,0},{12,4},{1,9},{5,13},{9,1},{13,5},{2,10},{6,14},... | collective-permute-start | bytes 1769480 | tf_op jit(solution)/shard_map/ppermute | solution.py:461
  20.4 24.5 %all-to-all-start.1 = ((bf16[4,4,288,112]{3,2,1,0:T(8,128)(2,1)}), bf16[4,4,288,112]{3,2,1,0:T(8,128)(2,1)}, u32[]{:S(2)}, u32[]{:S(2)}) async-start(bf16[4,4,288,112]{3,2,1,0:T(8,128)(2,1)} %broadcast_in_dim.6), calls=%async_computation.1 | async-start | bytes 2359296 | tf_op jit(solution)/shard_map/all_to_all | solution.py:488
  24.7 21.9 %collective-permute-start.3 = (bf16[256,1152]{1,0:T(8,128)(2,1)S(1)}, bf16[256,1152]{1,0:T(8,128)(2,1)}, u32[]{:S(2)}, u32[]{:S(2)}) collective-permute-start(bf16[256,1152]{1,0:T(8,128)(2,1)S(1)} %shard_map.56.mine_ref), channel_id=1, source_target_pairs={{0,1},{1,0},{2,3},{3,2},{4,5},{5,4},{6,7},{7,6},{8,9},{9,8},{10,11... | collective-permute-start | bytes 1769480 | tf_op jit(solution)/shard_map/ppermute | solution.py:340
  24.8 25.0 %collective-permute-start.11 = (bf16[256,1152]{1,0:T(8,128)(2,1)S(1)}, bf16[256,1152]{1,0:T(8,128)(2,1)}, u32[]{:S(2)}, u32[]{:S(2)}) collective-permute-start(bf16[256,1152]{1,0:T(8,128)(2,1)S(1)} %shard_map.56.mine_ref), channel_id=1, source_target_pairs={{0,2},{2,0},{1,3},{3,1},{4,6},{6,4},{5,7},{7,5},{8,10},{10,8},{9,1... | collective-permute-start | bytes 1769480 | tf_op jit(solution)/shard_map/ppermute | solution.py:340
  40.5 9.3 %collective-permute-start.4 = (bf16[256,1152]{1,0:T(8,128)(2,1)}, bf16[256,1152]{1,0:T(8,128)(2,1)}, u32[]{:S(2)}, u32[]{:S(2)}) collective-permute-start(bf16[256,1152]{1,0:T(8,128)(2,1)} %collective-permute-done.2.mine_ref), channel_id=1, source_target_pairs={{0,1},{1,0},{2,3},{3,2},{4,5},{5,4},{6,7},{7,6},{8,9},{9,8},{10,11... | collective-permute-start | bytes 1769480 | tf_op jit(solution)/shard_map/ppermute | solution.py:340
  43.6 8.9 %collective-permute-start.5 = (bf16[256,1152]{1,0:T(8,128)(2,1)}, bf16[256,1152]{1,0:T(8,128)(2,1)}, u32[]{:S(2)}, u32[]{:S(2)}) collective-permute-start(bf16[256,1152]{1,0:T(8,128)(2,1)} %collective-permute-done.mine_ref), channel_id=1, source_target_pairs={{0,1},{1,0},{2,3},{3,2},{4,5},{5,4},{6,7},{7,6},{8,9},{9,8},{10,11... | collective-permute-start | bytes 1769480 | tf_op jit(solution)/shard_map/ppermute | solution.py:340
  43.6 16.1 %collective-permute-start.1 = (bf16[256,1152]{1,0:T(8,128)(2,1)}, bf16[256,1152]{1,0:T(8,128)(2,1)}, u32[]{:S(2)}, u32[]{:S(2)}) collective-permute-start(bf16[256,1152]{1,0:T(8,128)(2,1)} %collective-permute-done.mine_ref), channel_id=1, source_target_pairs={{0,4},{4,0},{8,12},{12,8},{1,5},{5,1},{9,13},{13,9},{2,6},{6,2},{1... | collective-permute-start | bytes 1769480 | tf_op jit(solution)/shard_map/ppermute | solution.py:461
  44.1 0.8 copy-start.2
  48.5 0.7 copy-start.11
  49.8 13.6 %collective-permute-start.12 = (bf16[256,1152]{1,0:T(8,128)(2,1)}, bf16[256,1152]{1,0:T(8,128)(2,1)}, u32[]{:S(2)}, u32[]{:S(2)}) collective-permute-start(bf16[256,1152]{1,0:T(8,128)(2,1)} %collective-permute-done.11.mine_ref), channel_id=1, source_target_pairs={{0,1},{1,0},{2,3},{3,2},{4,5},{5,4},{6,7},{7,6},{8,9},{9,8},{10,11... | collective-permute-start | bytes 1769480 | tf_op jit(solution)/shard_map/ppermute | solution.py:340
  55.2 0.7 copy-start.6
  59.6 5.6 %collective-permute-start.6 = (bf16[256,1152]{1,0:T(8,128)(2,1)}, bf16[256,1152]{1,0:T(8,128)(2,1)S(1)}, u32[]{:S(2)}, u32[]{:S(2)}) collective-permute-start(bf16[256,1152]{1,0:T(8,128)(2,1)} %collective-permute-done.1.mine_ref), channel_id=1, source_target_pairs={{0,1},{1,0},{2,3},{3,2},{4,5},{5,4},{6,7},{7,6},{8,9},{9,8},{10,11... | collective-permute-start | bytes 1769480 | tf_op jit(solution)/shard_map/ppermute | solution.py:340
  59.6 14.8 %collective-permute-start.13 = (bf16[288,512]{1,0:T(8,128)(2,1)}, bf16[288,512]{1,0:T(8,128)(2,1)}, u32[]{:S(2)}, u32[]{:S(2)}) collective-permute-start(bf16[288,512]{1,0:T(8,128)(2,1)} %get-tuple-element.24.refs_6_), channel_id=1, source_target_pairs={{0,2},{2,0},{1,3},{3,1},{4,6},{6,4},{5,7},{7,5},{8,10},{10,8},{9,1... | collective-permute-start | bytes 884744 | tf_op jit(solution)/shard_map/ppermute | solution.py:340
  61.1 14.9 %collective-permute-start.14 = (bf16[288,512]{1,0:T(8,128)(2,1)}, bf16[288,512]{1,0:T(8,128)(2,1)}, u32[]{:S(2)}, u32[]{:S(2)}) collective-permute-start(bf16[288,512]{1,0:T(8,128)(2,1)} %get-tuple-element.25.refs_7_), channel_id=1, source_target_pairs={{0,2},{2,0},{1,3},{3,1},{4,6},{6,4},{5,7},{7,5},{8,10},{10,8},{9,1... | collective-permute-start | bytes 884744 | tf_op jit(solution)/shard_map/ppermute | solution.py:340
  65.2 2.6 %copy-start.4 = (bf16[288,512]{1,0:T(8,128)(2,1)}, bf16[288,512]{1,0:T(8,128)(2,1)S(1)}, u32[]{:S(2)}) copy-start(bf16[288,512]{1,0:T(8,128)(2,1)S(1)} %shard_map.62.refs_9_) | copy-start | bytes 884740
  67.8 0.6 copy-start.8
  68.5 7.6 %copy-start.5 = (bf16[288,512]{1,0:T(8,128)(2,1)S(1)}, bf16[288,512]{1,0:T(8,128)(2,1)}, u32[]{:S(2)}) copy-start(bf16[288,512]{1,0:T(8,128)(2,1)} %copy-done.4) | copy-start | bytes 884740
  68.5 7.6 %copy-start.7 = (bf16[144,512]{1,0:T(8,128)(2,1)S(1)}, bf16[144,512]{1,0:T(8,128)(2,1)}, u32[]{:S(2)}) copy-start(bf16[144,512]{1,0:T(8,128)(2,1)} %copy-done.6) | copy-start | bytes 442372
  68.5 21.1 %collective-permute-start.10 = (bf16[288,512]{1,0:T(8,128)(2,1)}, bf16[288,512]{1,0:T(8,128)(2,1)S(1)}, u32[]{:S(2)}, u32[]{:S(2)}) collective-permute-start(bf16[288,512]{1,0:T(8,128)(2,1)} %get-tuple-element.27.refs_8_), channel_id=1, source_target_pairs={{0,2},{2,0},{1,3},{3,1},{4,6},{6,4},{5,7},{7,5},{8,10},{10,8},{9,1... | collective-permute-start | bytes 884744 | tf_op jit(solution)/shard_map/ppermute | solution.py:340
  70.9 23.3 %all-to-all-start.2 = ((bf16[4,144,576]{2,1,0:T(8,128)(2,1)}), bf16[4,144,576]{2,1,0:T(8,128)(2,1)S(1)}, u32[]{:S(2)}, u32[]{:S(2)}) async-start(bf16[4,144,576]{2,1,0:T(8,128)(2,1)} %broadcast_in_dim.7), calls=%async_computation.2 | async-start | bytes 1474560 | tf_op jit(solution)/shard_map/all_to_all | solution.py:517
  76.1 0.9 copy-start.9
  77.0 1.0 copy-start.12
  94.3 21.4 %all-to-all-start.3 = ((bf16[4,144,512]{2,1,0:T(8,128)(2,1)}), bf16[4,144,512]{2,1,0:T(8,128)(2,1)S(1)}, u32[]{:S(2)}, u32[]{:S(2)}) async-start(bf16[4,144,512]{2,1,0:T(8,128)(2,1)} %shard_map.64), calls=%async_computation.3 | async-start | bytes 1179648 | tf_op jit(solution)/shard_map/all_to_all | solution.py:511
  97.8 17.9 %collective-permute-start.8 = (bf16[4,144,576]{2,1,0:T(8,128)(2,1)S(1)}, bf16[4,144,576]{2,1,0:T(8,128)(2,1)}, u32[]{:S(2)}, u32[]{:S(2)}) collective-permute-start(bf16[4,144,576]{2,1,0:T(8,128)(2,1)S(1)} %all-to-all-done.2.mine_ref), channel_id=1, source_target_pairs={{0,16},{16,0},{1,17},{17,1},{2,18},{18,2},{3,19},{19,3},{4,20},{20... | collective-permute-start | bytes 1990664 | tf_op jit(solution)/shard_map/ppermute | solution.py:340
  98.6 20.5 %collective-permute-start.7 = (bf16[4,144,576]{2,1,0:T(8,128)(2,1)S(1)}, bf16[4,144,576]{2,1,0:T(8,128)(2,1)}, u32[]{:S(2)}, u32[]{:S(2)}) collective-permute-start(bf16[4,144,576]{2,1,0:T(8,128)(2,1)S(1)} %all-to-all-done.2.mine_ref), channel_id=1, source_target_pairs={{0,1},{1,0},{2,3},{3,2},{4,5},{5,4},{6,7},{7,6},{8,9},{9,8},{10,11... | collective-permute-start | bytes 1990664 | tf_op jit(solution)/shard_map/ppermute | solution.py:340
  115.7 3.5 %collective-permute-start.9 = (bf16[4,144,576]{2,1,0:T(8,128)(2,1)}, bf16[4,144,576]{2,1,0:T(8,128)(2,1)}, u32[]{:S(2)}, u32[]{:S(2)}) collective-permute-start(bf16[4,144,576]{2,1,0:T(8,128)(2,1)} %collective-permute-done.8.other_ref), channel_id=1, source_target_pairs={{0,1},{1,0},{2,3},{3,2},{4,5},{5,4},{6,7},{7,6},{8,9},{9,8},{10,11... | collective-permute-start | bytes 1990664 | tf_op jit(solution)/shard_map/ppermute | solution.py:340
  115.7 3.4 %collective-permute-start.15 = (bf16[576,512]{1,0:T(8,128)(2,1)S(1)}, bf16[576,512]{1,0:T(8,128)(2,1)S(1)}, u32[]{:S(2)}, u32[]{:S(2)}) collective-permute-start(bf16[576,512]{1,0:T(8,128)(2,1)S(1)} %bitcast.23), channel_id=1, source_target_pairs={{0,1},{1,0},{2,3},{3,2},{4,5},{5,4},{6,7},{7,6},{8,9},{9,8},{10,11... | collective-permute-start | bytes 1769480 | tf_op jit(solution)/shard_map/ppermute | solution.py:340
  116.3 1.1 copy-start.3

commit v7 on v5

--- a/solution.py
+++ b/solution.py
@@ -133,7 +133,7 @@
 
 def run_items(items, q_list, k_list, key_rows, heads, head_dim, q_all, k_all, v_all, scores_of, block_high, scale_old, high, total):
     factor = math.log2(math.e) / math.sqrt(head_dim)
-    step = math.gcd(key_rows, 256)
+    step = math.gcd(key_rows, 512)
 
     def stage(now, before):
         if now is not None:

time: 122 us -> 123 us (level)
  starting transfers between devices: 28.9 us -> 30.5 us
  Pallas kernels: 35.3 us -> 33.7 us
    ppermute x13, starting transfers between devices: 6.89 us -> 8.52 us  [swapped(): return lax.ppermute(block, axis, [(0, 1), (1, 0)])]
    pallas_call x12, Pallas kernels: 35.3 us -> 33.7 us  [call(): pl.pallas_call(kernel, out_shape=out_shape, in_specs=[where if i in left...]
  transfers between devices with their start and end apart: 20 -> 20, of which waited for: 7 -> 8; matrix products, arithmetic and copies ran while one was open for 3% -> 3% of each run, Pallas kernels for 27% -> 25%
where the time goes in v7:
time: 123 us; the launch traced here: 122 us
  waiting for transfers between devices  45.6 us (37%)
  Pallas kernels  33.7 us (27%)
  starting transfers between devices  30.5 us (25%)
  local copies, waits for them, and re-layouts  11.1 us (9%)
    pallas_call x12, Pallas kernels, call(): pl.pallas_call(kernel, out_shape=out_shape, in_specs=[where if i in left...  33.7 us
    ppermute x3, waiting for transfers between devices, flipped(): lax.ppermute(block, axis, [(i, i ^ distance) for i in range(lax.axis_size...  20.7 us
    ppermute x13, waiting for transfers between devices, swapped(): return lax.ppermute(block, axis, [(0, 1), (1, 0)])  18.4 us
    ppermute x13, starting transfers between devices, swapped(): return lax.ppermute(block, axis, [(0, 1), (1, 0)])  8.52 us
    unnamed x26, local copies, waits for them, and re-layouts  7.09 us
    all_to_all x1, starting transfers between devices, by_heads(): part = lax.all_to_all(part, 'frame', 0, 0)  6.32 us
    all_to_all x1, waiting for transfers between devices, by_heads(): part = lax.all_to_all(part, 'frame', 0, 0)  5.71 us
    ppermute x3, starting transfers between devices, flipped(): lax.ppermute(block, axis, [(i, i ^ distance) for i in range(lax.axis_size...  4.45 us
  transfers between devices with their start and end apart: 20, of which 8 were waited for; matrix products, arithmetic and copies ran while one was open for 3% of the time, Pallas kernels for 25%

profile of v7, /device:TPU:0, one launch (start us, length us, event | category | flops | bytes accessed | tf_op | source)
XLA Modules:
  0.0 121.9 jit_solution(17548035704198922354)
XLA Ops:
  0.0 1.3 %copy-done = bf16[288,8,3,72]{0,3,2,1:T(8,128)(2,1)S(1)} copy-done((bf16[288,8,3,72]{0,3,2,1:T(8,128)(2,1)S(1)}, bf16[288,8,3,72]{0,3,2,1:T(8,128)(2,1)}, u32[]{:S(2)}) %copy-start) | copy-done | bytes 995352
  1.4 0.9 copy.6
  2.3 6.3 %all-to-all-start = ((bf16[4,288,112]{2,1,0:T(8,128)(2,1)}), bf16[4,288,112]{2,1,0:T(8,128)(2,1)S(1)}, u32[]{:S(2)}, u32[]{:S(2)}) async-start(bf16[4,288,112]{2,1,0:T(8,128)(2,1)} %bitcast.8), calls=%async_computation | async-start | bytes 589824 | tf_op jit(solution)/shard_map/all_to_all | solution.py:488
  8.6 0.5 shard_map.56.mine_ref
  9.1 2.1 %collective-permute-start.2 = (bf16[256,1152]{1,0:T(8,128)(2,1)S(1)}, bf16[256,1152]{1,0:T(8,128)(2,1)}, u32[]{:S(2)}, u32[]{:S(2)}) collective-permute-start(bf16[256,1152]{1,0:T(8,128)(2,1)S(1)} %shard_map.56.mine_ref), channel_id=1, source_target_pairs={{0,4},{4,0},{8,12},{12,8},{1,5},{5,1},{9,13},{13,9},{2,6},{6,2},{1... | collective-permute-start | bytes 1769480 | tf_op jit(solution)/shard_map/ppermute | solution.py:462
  11.2 2.4 %collective-permute-start = (bf16[256,1152]{1,0:T(8,128)(2,1)S(1)}, bf16[256,1152]{1,0:T(8,128)(2,1)}, u32[]{:S(2)}, u32[]{:S(2)}) collective-permute-start(bf16[256,1152]{1,0:T(8,128)(2,1)S(1)} %shard_map.56.mine_ref), channel_id=1, source_target_pairs={{0,8},{4,12},{8,0},{12,4},{1,9},{5,13},{9,1},{13,5},{2,10},{6,14},... | collective-permute-start | bytes 1769480 | tf_op jit(solution)/shard_map/ppermute | solution.py:462
  13.6 5.7 %all-to-all-done = bf16[4,288,112]{2,1,0:T(8,128)(2,1)S(1)} async-done(((bf16[4,288,112]{2,1,0:T(8,128)(2,1)}), bf16[4,288,112]{2,1,0:T(8,128)(2,1)S(1)}, u32[]{:S(2)}, u32[]{:S(2)}) %all-to-all-start) | async-done | bytes 258080 | tf_op jit(solution)/shard_map/all_to_all | solution.py:488
  19.3 1.2 broadcast_in_dim.6
  20.4 4.3 %all-to-all-start.1 = ((bf16[4,4,288,112]{3,2,1,0:T(8,128)(2,1)}), bf16[4,4,288,112]{3,2,1,0:T(8,128)(2,1)}, u32[]{:S(2)}, u32[]{:S(2)}) async-start(bf16[4,4,288,112]{3,2,1,0:T(8,128)(2,1)} %broadcast_in_dim.6), calls=%async_computation.1 | async-start | bytes 2359296 | tf_op jit(solution)/shard_map/all_to_all | solution.py:489
  24.7 0.1 collective-permute-start.3
  24.8 1.9 %collective-permute-start.11 = (bf16[256,1152]{1,0:T(8,128)(2,1)S(1)}, bf16[256,1152]{1,0:T(8,128)(2,1)}, u32[]{:S(2)}, u32[]{:S(2)}) collective-permute-start(bf16[256,1152]{1,0:T(8,128)(2,1)S(1)} %shard_map.56.mine_ref), channel_id=1, source_target_pairs={{0,2},{2,0},{1,3},{3,1},{4,6},{6,4},{5,7},{7,5},{8,10},{10,8},{9,1... | collective-permute-start | bytes 1769480 | tf_op jit(solution)/shard_map/ppermute | solution.py:341
  26.7 13.8 %collective-permute-done.2.mine_ref = bf16[256,1152]{1,0:T(8,128)(2,1)} collective-permute-done((bf16[256,1152]{1,0:T(8,128)(2,1)S(1)}, bf16[256,1152]{1,0:T(8,128)(2,1)}, u32[]{:S(2)}, u32[]{:S(2)}) %collective-permute-start.2) | collective-permute-done | bytes 589856 | tf_op jit(solution)/shard_map/ppermute | solution.py:462
  40.5 0.0 collective-permute-start.4
  40.5 3.1 %collective-permute-done.mine_ref = bf16[256,1152]{1,0:T(8,128)(2,1)} collective-permute-done((bf16[256,1152]{1,0:T(8,128)(2,1)S(1)}, bf16[256,1152]{1,0:T(8,128)(2,1)}, u32[]{:S(2)}, u32[]{:S(2)}) %collective-permute-start) | collective-permute-done | bytes 589856 | tf_op jit(solution)/shard_map/ppermute | solution.py:462
  43.6 0.0 collective-permute-start.5
  43.6 0.0 collective-permute-start.1
  43.6 0.5 shard_map.57
  44.1 0.8 copy-done.2
  45.0 0.0 all-to-all-done.1.parts_ref
  45.0 1.6 %shard_map.55.weight_ref = bf16[432,1152]{1,0:T(8,128)(2,1)S(1)} custom-call(bf16[4,4,288,112]{3,2,1,0:T(8,128)(2,1)} %all-to-all-done.1.parts_ref), custom_call_target="tpu_custom_call" | custom-call | tf_op jit(solution)/shard_map/pallas_call | solution.py:27
  46.6 0.0 collective-permute-done.3.other_ref
  46.6 1.8 %shard_map.58 = (bf16[288,512]{1,0:T(8,128)(2,1)S(1)}, bf16[144,512]{1,0:T(8,128)(2,1)S(1)}) custom-call(s32[1]{0:T(128)} %bitcast.3.place_ref.core_ref, bf16[432,1152]{1,0:T(8,128)(2,1)S(1)} %shard_map.55.weight_ref, bf16[256,1152]{1,0:T(8,128)(2,1)S(1)} %shard_map.56.mine_ref, bf16[256,1152]{1,0:T(8,128)(2,1)} %collective-permute-done.3.other_ref), custom_call_target="tpu_custom_call" | custom-call | flops 509607936 | bytes 2617344 | tf_op jit(solution)/shard_map/pallas_call | solution.py:27
  48.5 0.7 copy-done.11
  49.2 0.6 collective-permute-done.11.mine_ref
  49.8 0.0 collective-permute-start.12
  49.8 0.0 collective-permute-done.4.other_ref
  49.8 2.7 %shard_map.59 = (bf16[288,512]{1,0:T(8,128)(2,1)}, bf16[144,512]{1,0:T(8,128)(2,1)S(1)}) custom-call(s32[1]{0:T(128)} %bitcast.3.place_ref.core_ref, bf16[432,1152]{1,0:T(8,128)(2,1)S(1)} %shard_map.55.weight_ref, bf16[256,1152]{1,0:T(8,128)(2,1)} %collective-permute-done.2.mine_ref, bf16[256,1152]{1,0:T(8,128)(2,1)} %collective-permute-done.4.other_ref), custom_call_target="tpu_custom_call" | custom-call | flops 509607936 | bytes 2617344 | tf_op jit(solution)/shard_map/pallas_call | solution.py:27
  52.5 0.0 collective-permute-done.5.other_ref
  52.5 2.7 %shard_map.60 = (bf16[288,512]{1,0:T(8,128)(2,1)}, bf16[144,512]{1,0:T(8,128)(2,1)S(1)}) custom-call(s32[1]{0:T(128)} %bitcast.3.place_ref.core_ref, bf16[432,1152]{1,0:T(8,128)(2,1)S(1)} %shard_map.55.weight_ref, bf16[256,1152]{1,0:T(8,128)(2,1)} %collective-permute-done.mine_ref, bf16[256,1152]{1,0:T(8,128)(2,1)} %collective-permute-done.5.other_ref), custom_call_target="tpu_custom_call" | custom-call | flops 509607936 | bytes 2617344 | tf_op jit(solution)/shard_map/pallas_call | solution.py:27
  55.2 0.7 copy-done.6
  55.9 3.8 %collective-permute-done.1.mine_ref = bf16[256,1152]{1,0:T(8,128)(2,1)} collective-permute-done((bf16[256,1152]{1,0:T(8,128)(2,1)}, bf16[256,1152]{1,0:T(8,128)(2,1)}, u32[]{:S(2)}, u32[]{:S(2)}) %collective-permute-start.1) | collective-permute-done | bytes 589856 | tf_op jit(solution)/shard_map/ppermute | solution.py:462
  59.6 0.0 collective-permute-start.6
  59.6 1.5 %collective-permute-start.13 = (bf16[288,512]{1,0:T(8,128)(2,1)}, bf16[288,512]{1,0:T(8,128)(2,1)}, u32[]{:S(2)}, u32[]{:S(2)}) collective-permute-start(bf16[288,512]{1,0:T(8,128)(2,1)} %get-tuple-element.24.refs_6_), channel_id=1, source_target_pairs={{0,2},{2,0},{1,3},{3,1},{4,6},{6,4},{5,7},{7,5},{8,10},{10,8},{9,1... | collective-permute-start | bytes 884744 | tf_op jit(solution)/shard_map/ppermute | solution.py:341
  61.1 0.5 collective-permute-start.14
  62.3 0.1 stack.36.refs_0_
  62.4 0.9 dynamic-slice_bitcast_fusion
  63.4 0.0 collective-permute-done.12.other_ref
  63.4 1.8 %shard_map.62.refs_9_ = bf16[288,512]{1,0:T(8,128)(2,1)S(1)} custom-call(s32[1]{0:T(128)} %bitcast.3.place_ref.core_ref, bf16[432,1152]{1,0:T(8,128)(2,1)S(1)} %shard_map.55.weight_ref, bf16[256,1152]{1,0:T(8,128)(2,1)} %collective-permute-done.11.mine_ref, bf16[256,1152]{1,0:T(8,128)(2,1)} %collective-permute-done.12.other_ref), custom_call_target="tpu_custom_call" | custom-call | flops 509607936 | bytes 2617344 | tf_op jit(solution)/shard_map/pallas_call | solution.py:27
  65.2 0.0 collective-permute-done.6.other_ref
  65.2 2.6 %shard_map.61 = (bf16[288,512]{1,0:T(8,128)(2,1)}, bf16[144,512]{1,0:T(8,128)(2,1)S(1)}) custom-call(s32[1]{0:T(128)} %bitcast.3.place_ref.core_ref, bf16[432,1152]{1,0:T(8,128)(2,1)S(1)} %shard_map.55.weight_ref, bf16[256,1152]{1,0:T(8,128)(2,1)} %collective-permute-done.1.mine_ref, bf16[256,1152]{1,0:T(8,128)(2,1)S(1)} %collective-permute-done.6.other_ref), custom_call_target="tpu_custom_call" | custom-call | flops 509607936 | bytes 2617344 | tf_op jit(solution)/shard_map/pallas_call | solution.py:27
  67.8 0.6 copy-done.8
  68.5 1.5 %collective-permute-start.10 = (bf16[288,512]{1,0:T(8,128)(2,1)}, bf16[288,512]{1,0:T(8,128)(2,1)S(1)}, u32[]{:S(2)}, u32[]{:S(2)}) collective-permute-start(bf16[288,512]{1,0:T(8,128)(2,1)} %get-tuple-element.27.refs_8_), channel_id=1, source_target_pairs={{0,2},{2,0},{1,3},{3,1},{4,6},{6,4},{5,7},{7,5},{8,10},{10,8},{9,1... | collective-permute-start | bytes 884744 | tf_op jit(solution)/shard_map/ppermute | solution.py:341
  70.0 0.9 broadcast_in_dim.7
  70.9 3.5 %all-to-all-start.2 = ((bf16[4,144,576]{2,1,0:T(8,128)(2,1)}), bf16[4,144,576]{2,1,0:T(8,128)(2,1)S(1)}, u32[]{:S(2)}, u32[]{:S(2)}) async-start(bf16[4,144,576]{2,1,0:T(8,128)(2,1)} %broadcast_in_dim.7), calls=%async_computation.2 | async-start | bytes 1474560 | tf_op jit(solution)/shard_map/all_to_all | solution.py:518
  74.4 0.0 collective-permute-done.13.refs_10_
  74.4 1.7 %collective-permute-done.14.refs_11_ = bf16[288,512]{1,0:T(8,128)(2,1)} collective-permute-done((bf16[288,512]{1,0:T(8,128)(2,1)}, bf16[288,512]{1,0:T(8,128)(2,1)}, u32[]{:S(2)}, u32[]{:S(2)}) %collective-permute-start.14) | collective-permute-done | bytes 294944 | tf_op jit(solution)/shard_map/ppermute | solution.py:341
  76.1 0.9 copy-done.9
  77.0 1.0 copy-done.12
  78.0 12.1 %shard_map.63 = (f32[8,1,512]{2,1,0:T(1,128)S(1)}, f32[8,80,512]{2,1,0:T(8,128)S(1)}) custom-call(s32[5]{0:T(128)S(1)} %stack.36.refs_0_, bf16[144,512]{1,0:T(8,128)(2,1)S(1)} %get-tuple-element.29.refs_1_, bf16[144,512]{1,0:T(8,128)(2,1)S(1)} %get-tuple-element.30.refs_2_, bf16[144,512]{1,0:T(8,128)(2,1)S(1)} %copy-done.7, bf16[144,512]{1,0:T(8,128)(2,1)S(1)} %copy-done.9, ...), custom_call_target="tpu_custom_call" | custom-call | flops 14495514624 | bytes 3538944 | tf_op jit(solution)/shard_map/pallas_call | solution.py:27
  90.1 0.0 collective-permute-done.10.refs_5_
  90.1 2.6 %shard_map.64 = bf16[4,144,512]{2,1,0:T(8,128)(2,1)} custom-call(s32[5]{0:T(128)S(1)} %stack.36.refs_0_, bf16[144,512]{1,0:T(8,128)(2,1)S(1)} %get-tuple-element.29.refs_1_, bf16[144,512]{1,0:T(8,128)(2,1)S(1)} %get-tuple-element.30.refs_2_, bf16[144,512]{1,0:T(8,128)(2,1)S(1)} %copy-done.7, bf16[144,512]{1,0:T(8,128)(2,1)S(1)} %copy-done.9, ...), custom_call_target="tpu_custom_call" | custom-call | flops 603979776 | bytes 3538944 | tf_op jit(solution)/shard_map/pallas_call | solution.py:27
  92.7 0.9 all-to-all-done.2.mine_ref
  93.6 3.5 %all-to-all-start.3 = ((bf16[4,144,512]{2,1,0:T(8,128)(2,1)}), bf16[4,144,512]{2,1,0:T(8,128)(2,1)S(1)}, u32[]{:S(2)}, u32[]{:S(2)}) async-start(bf16[4,144,512]{2,1,0:T(8,128)(2,1)} %shard_map.64), calls=%async_computation.3 | async-start | bytes 1179648 | tf_op jit(solution)/shard_map/all_to_all | solution.py:512
  97.0 2.5 %collective-permute-start.8 = (bf16[4,144,576]{2,1,0:T(8,128)(2,1)S(1)}, bf16[4,144,576]{2,1,0:T(8,128)(2,1)}, u32[]{:S(2)}, u32[]{:S(2)}) collective-permute-start(bf16[4,144,576]{2,1,0:T(8,128)(2,1)S(1)} %all-to-all-done.2.mine_ref), channel_id=1, source_target_pairs={{0,16},{16,0},{1,17},{17,1},{2,18},{18,2},{3,19},{19,3},{4,20},{20... | collective-permute-start | bytes 1990664 | tf_op jit(solution)/shard_map/ppermute | solution.py:341
  99.5 0.0 collective-permute-start.7
  99.5 16.1 %collective-permute-done.8.other_ref = bf16[4,144,576]{2,1,0:T(8,128)(2,1)} collective-permute-done((bf16[4,144,576]{2,1,0:T(8,128)(2,1)S(1)}, bf16[4,144,576]{2,1,0:T(8,128)(2,1)}, u32[]{:S(2)}, u32[]{:S(2)}) %collective-permute-start.8) | collective-permute-done | bytes 663584 | tf_op jit(solution)/shard_map/ppermute | solution.py:341
  115.6 0.0 collective-permute-start.9
  115.6 0.5 collective-permute-start.15
  116.1 0.1 pad_add_fusion.where_ref
  116.2 1.1 copy-done.3
  117.3 1.8 %shard_map.65.start_ref = f32[576,512]{1,0:T(8,128)S(1)} custom-call(s32[4]{0:T(128)S(1)} %pad_add_fusion.where_ref, bf16[4,144,576]{2,1,0:T(8,128)(2,1)S(1)} %all-to-all-done.2.mine_ref, bf16[4,144,576]{2,1,0:T(8,128)(2,1)} %collective-permute-done.8.other_ref, bf16[576,512]{1,0:T(8,128)(2,1)S(1)} %bitcast.24, bf16[576,512]{1,0:T(8,128)(2,1)S(1)} %copy-done.3, ...), custom_call_target="tpu_custom_call" | custom-call | tf_op jit(solution)/shard_map/pallas_call | solution.py:27
  119.1 0.0 collective-permute-done.15.heads_ref
  119.1 0.0 collective-permute-done.9.other_ref
  119.1 2.8 %shard_map.66 = bf16[576,512]{1,0:T(8,128)(2,1)} custom-call(s32[4]{0:T(128)S(1)} %pad_add_fusion.where_ref, bf16[4,144,576]{2,1,0:T(8,128)(2,1)} %collective-permute-done.7.mine_ref, bf16[4,144,576]{2,1,0:T(8,128)(2,1)} %collective-permute-done.9.other_ref, bf16[576,512]{1,0:T(8,128)(2,1)S(1)} %collective-permute-done.15.heads_ref, ...), custom_call_target="tpu_custom_call" | custom-call | tf_op jit(solution)/shard_map/pallas_call | solution.py:27
  (21 shorter events, 0.1 us)
Async XLA Ops:
  0.0 1.3 %copy-start = (bf16[288,8,3,72]{0,3,2,1:T(8,128)(2,1)S(1)}, bf16[288,8,3,72]{0,3,2,1:T(8,128)(2,1)}, u32[]{:S(2)}) copy-start(bf16[288,8,3,72]{0,3,2,1:T(8,128)(2,1)} %param.7) | copy-start | bytes 2985988
  0.0 8.6 %copy-start.1 = (bf16[1,512,1152]{2,1,0:T(8,128)(2,1)S(1)}, bf16[1,512,1152]{2,1,0:T(8,128)(2,1)}, u32[]{:S(2)}) copy-start(bf16[1,512,1152]{2,1,0:T(8,128)(2,1)} %param.5) | copy-start | bytes 3538948
  0.0 8.6 %copy-start.10 = (f32[3,1152]{1,0:T(4,128)S(1)}, f32[3,1152]{1,0:T(4,128)}, u32[]{:S(2)}) copy-start(f32[3,1152]{1,0:T(4,128)} %mod_ref.3) | copy-start | bytes 41476
  2.3 17.0 %all-to-all-start = ((bf16[4,288,112]{2,1,0:T(8,128)(2,1)}), bf16[4,288,112]{2,1,0:T(8,128)(2,1)S(1)}, u32[]{:S(2)}, u32[]{:S(2)}) async-start(bf16[4,288,112]{2,1,0:T(8,128)(2,1)} %bitcast.8), calls=%async_computation | async-start | bytes 589824 | tf_op jit(solution)/shard_map/all_to_all | solution.py:488
  9.1 31.4 %collective-permute-start.2 = (bf16[256,1152]{1,0:T(8,128)(2,1)S(1)}, bf16[256,1152]{1,0:T(8,128)(2,1)}, u32[]{:S(2)}, u32[]{:S(2)}) collective-permute-start(bf16[256,1152]{1,0:T(8,128)(2,1)S(1)} %shard_map.56.mine_ref), channel_id=1, source_target_pairs={{0,4},{4,0},{8,12},{12,8},{1,5},{5,1},{9,13},{13,9},{2,6},{6,2},{1... | collective-permute-start | bytes 1769480 | tf_op jit(solution)/shard_map/ppermute | solution.py:462
  11.2 32.4 %collective-permute-start = (bf16[256,1152]{1,0:T(8,128)(2,1)S(1)}, bf16[256,1152]{1,0:T(8,128)(2,1)}, u32[]{:S(2)}, u32[]{:S(2)}) collective-permute-start(bf16[256,1152]{1,0:T(8,128)(2,1)S(1)} %shard_map.56.mine_ref), channel_id=1, source_target_pairs={{0,8},{4,12},{8,0},{12,4},{1,9},{5,13},{9,1},{13,5},{2,10},{6,14},... | collective-permute-start | bytes 1769480 | tf_op jit(solution)/shard_map/ppermute | solution.py:462
  20.4 24.5 %all-to-all-start.1 = ((bf16[4,4,288,112]{3,2,1,0:T(8,128)(2,1)}), bf16[4,4,288,112]{3,2,1,0:T(8,128)(2,1)}, u32[]{:S(2)}, u32[]{:S(2)}) async-start(bf16[4,4,288,112]{3,2,1,0:T(8,128)(2,1)} %broadcast_in_dim.6), calls=%async_computation.1 | async-start | bytes 2359296 | tf_op jit(solution)/shard_map/all_to_all | solution.py:489
  24.7 21.9 %collective-permute-start.3 = (bf16[256,1152]{1,0:T(8,128)(2,1)S(1)}, bf16[256,1152]{1,0:T(8,128)(2,1)}, u32[]{:S(2)}, u32[]{:S(2)}) collective-permute-start(bf16[256,1152]{1,0:T(8,128)(2,1)S(1)} %shard_map.56.mine_ref), channel_id=1, source_target_pairs={{0,1},{1,0},{2,3},{3,2},{4,5},{5,4},{6,7},{7,6},{8,9},{9,8},{10,11... | collective-permute-start | bytes 1769480 | tf_op jit(solution)/shard_map/ppermute | solution.py:341
  24.8 25.0 %collective-permute-start.11 = (bf16[256,1152]{1,0:T(8,128)(2,1)S(1)}, bf16[256,1152]{1,0:T(8,128)(2,1)}, u32[]{:S(2)}, u32[]{:S(2)}) collective-permute-start(bf16[256,1152]{1,0:T(8,128)(2,1)S(1)} %shard_map.56.mine_ref), channel_id=1, source_target_pairs={{0,2},{2,0},{1,3},{3,1},{4,6},{6,4},{5,7},{7,5},{8,10},{10,8},{9,1... | collective-permute-start | bytes 1769480 | tf_op jit(solution)/shard_map/ppermute | solution.py:341
  40.5 9.3 %collective-permute-start.4 = (bf16[256,1152]{1,0:T(8,128)(2,1)}, bf16[256,1152]{1,0:T(8,128)(2,1)}, u32[]{:S(2)}, u32[]{:S(2)}) collective-permute-start(bf16[256,1152]{1,0:T(8,128)(2,1)} %collective-permute-done.2.mine_ref), channel_id=1, source_target_pairs={{0,1},{1,0},{2,3},{3,2},{4,5},{5,4},{6,7},{7,6},{8,9},{9,8},{10,11... | collective-permute-start | bytes 1769480 | tf_op jit(solution)/shard_map/ppermute | solution.py:341
  43.6 8.9 %collective-permute-start.5 = (bf16[256,1152]{1,0:T(8,128)(2,1)}, bf16[256,1152]{1,0:T(8,128)(2,1)}, u32[]{:S(2)}, u32[]{:S(2)}) collective-permute-start(bf16[256,1152]{1,0:T(8,128)(2,1)} %collective-permute-done.mine_ref), channel_id=1, source_target_pairs={{0,1},{1,0},{2,3},{3,2},{4,5},{5,4},{6,7},{7,6},{8,9},{9,8},{10,11... | collective-permute-start | bytes 1769480 | tf_op jit(solution)/shard_map/ppermute | solution.py:341
  43.6 16.1 %collective-permute-start.1 = (bf16[256,1152]{1,0:T(8,128)(2,1)}, bf16[256,1152]{1,0:T(8,128)(2,1)}, u32[]{:S(2)}, u32[]{:S(2)}) collective-permute-start(bf16[256,1152]{1,0:T(8,128)(2,1)} %collective-permute-done.mine_ref), channel_id=1, source_target_pairs={{0,4},{4,0},{8,12},{12,8},{1,5},{5,1},{9,13},{13,9},{2,6},{6,2},{1... | collective-permute-start | bytes 1769480 | tf_op jit(solution)/shard_map/ppermute | solution.py:462
  44.1 0.8 copy-start.2
  48.5 0.7 copy-start.11
  49.8 13.6 %collective-permute-start.12 = (bf16[256,1152]{1,0:T(8,128)(2,1)}, bf16[256,1152]{1,0:T(8,128)(2,1)}, u32[]{:S(2)}, u32[]{:S(2)}) collective-permute-start(bf16[256,1152]{1,0:T(8,128)(2,1)} %collective-permute-done.11.mine_ref), channel_id=1, source_target_pairs={{0,1},{1,0},{2,3},{3,2},{4,5},{5,4},{6,7},{7,6},{8,9},{9,8},{10,11... | collective-permute-start | bytes 1769480 | tf_op jit(solution)/shard_map/ppermute | solution.py:341
  55.2 0.7 copy-start.6
  59.6 5.6 %collective-permute-start.6 = (bf16[256,1152]{1,0:T(8,128)(2,1)}, bf16[256,1152]{1,0:T(8,128)(2,1)S(1)}, u32[]{:S(2)}, u32[]{:S(2)}) collective-permute-start(bf16[256,1152]{1,0:T(8,128)(2,1)} %collective-permute-done.1.mine_ref), channel_id=1, source_target_pairs={{0,1},{1,0},{2,3},{3,2},{4,5},{5,4},{6,7},{7,6},{8,9},{9,8},{10,11... | collective-permute-start | bytes 1769480 | tf_op jit(solution)/shard_map/ppermute | solution.py:341
  59.6 14.8 %collective-permute-start.13 = (bf16[288,512]{1,0:T(8,128)(2,1)}, bf16[288,512]{1,0:T(8,128)(2,1)}, u32[]{:S(2)}, u32[]{:S(2)}) collective-permute-start(bf16[288,512]{1,0:T(8,128)(2,1)} %get-tuple-element.24.refs_6_), channel_id=1, source_target_pairs={{0,2},{2,0},{1,3},{3,1},{4,6},{6,4},{5,7},{7,5},{8,10},{10,8},{9,1... | collective-permute-start | bytes 884744 | tf_op jit(solution)/shard_map/ppermute | solution.py:341
  61.1 14.9 %collective-permute-start.14 = (bf16[288,512]{1,0:T(8,128)(2,1)}, bf16[288,512]{1,0:T(8,128)(2,1)}, u32[]{:S(2)}, u32[]{:S(2)}) collective-permute-start(bf16[288,512]{1,0:T(8,128)(2,1)} %get-tuple-element.25.refs_7_), channel_id=1, source_target_pairs={{0,2},{2,0},{1,3},{3,1},{4,6},{6,4},{5,7},{7,5},{8,10},{10,8},{9,1... | collective-permute-start | bytes 884744 | tf_op jit(solution)/shard_map/ppermute | solution.py:341
  65.2 2.6 %copy-start.4 = (bf16[288,512]{1,0:T(8,128)(2,1)}, bf16[288,512]{1,0:T(8,128)(2,1)S(1)}, u32[]{:S(2)}) copy-start(bf16[288,512]{1,0:T(8,128)(2,1)S(1)} %shard_map.62.refs_9_) | copy-start | bytes 884740
  67.8 0.6 copy-start.8
  68.5 7.6 %copy-start.5 = (bf16[288,512]{1,0:T(8,128)(2,1)S(1)}, bf16[288,512]{1,0:T(8,128)(2,1)}, u32[]{:S(2)}) copy-start(bf16[288,512]{1,0:T(8,128)(2,1)} %copy-done.4) | copy-start | bytes 884740
  68.5 7.6 %copy-start.7 = (bf16[144,512]{1,0:T(8,128)(2,1)S(1)}, bf16[144,512]{1,0:T(8,128)(2,1)}, u32[]{:S(2)}) copy-start(bf16[144,512]{1,0:T(8,128)(2,1)} %copy-done.6) | copy-start | bytes 442372
  68.5 21.6 %collective-permute-start.10 = (bf16[288,512]{1,0:T(8,128)(2,1)}, bf16[288,512]{1,0:T(8,128)(2,1)S(1)}, u32[]{:S(2)}, u32[]{:S(2)}) collective-permute-start(bf16[288,512]{1,0:T(8,128)(2,1)} %get-tuple-element.27.refs_8_), channel_id=1, source_target_pairs={{0,2},{2,0},{1,3},{3,1},{4,6},{6,4},{5,7},{7,5},{8,10},{10,8},{9,1... | collective-permute-start | bytes 884744 | tf_op jit(solution)/shard_map/ppermute | solution.py:341
  70.9 22.6 %all-to-all-start.2 = ((bf16[4,144,576]{2,1,0:T(8,128)(2,1)}), bf16[4,144,576]{2,1,0:T(8,128)(2,1)S(1)}, u32[]{:S(2)}, u32[]{:S(2)}) async-start(bf16[4,144,576]{2,1,0:T(8,128)(2,1)} %broadcast_in_dim.7), calls=%async_computation.2 | async-start | bytes 1474560 | tf_op jit(solution)/shard_map/all_to_all | solution.py:518
  76.1 0.9 copy-start.9
  77.0 1.0 copy-start.12
  93.6 22.1 %all-to-all-start.3 = ((bf16[4,144,512]{2,1,0:T(8,128)(2,1)}), bf16[4,144,512]{2,1,0:T(8,128)(2,1)S(1)}, u32[]{:S(2)}, u32[]{:S(2)}) async-start(bf16[4,144,512]{2,1,0:T(8,128)(2,1)} %shard_map.64), calls=%async_computation.3 | async-start | bytes 1179648 | tf_op jit(solution)/shard_map/all_to_all | solution.py:512
  97.0 18.6 %collective-permute-start.8 = (bf16[4,144,576]{2,1,0:T(8,128)(2,1)S(1)}, bf16[4,144,576]{2,1,0:T(8,128)(2,1)}, u32[]{:S(2)}, u32[]{:S(2)}) collective-permute-start(bf16[4,144,576]{2,1,0:T(8,128)(2,1)S(1)} %all-to-all-done.2.mine_ref), channel_id=1, source_target_pairs={{0,16},{16,0},{1,17},{17,1},{2,18},{18,2},{3,19},{19,3},{4,20},{20... | collective-permute-start | bytes 1990664 | tf_op jit(solution)/shard_map/ppermute | solution.py:341
  99.5 19.5 %collective-permute-start.7 = (bf16[4,144,576]{2,1,0:T(8,128)(2,1)S(1)}, bf16[4,144,576]{2,1,0:T(8,128)(2,1)}, u32[]{:S(2)}, u32[]{:S(2)}) collective-permute-start(bf16[4,144,576]{2,1,0:T(8,128)(2,1)S(1)} %all-to-all-done.2.mine_ref), channel_id=1, source_target_pairs={{0,1},{1,0},{2,3},{3,2},{4,5},{5,4},{6,7},{7,6},{8,9},{9,8},{10,11... | collective-permute-start | bytes 1990664 | tf_op jit(solution)/shard_map/ppermute | solution.py:341
  115.6 3.5 %collective-permute-start.9 = (bf16[4,144,576]{2,1,0:T(8,128)(2,1)}, bf16[4,144,576]{2,1,0:T(8,128)(2,1)}, u32[]{:S(2)}, u32[]{:S(2)}) collective-permute-start(bf16[4,144,576]{2,1,0:T(8,128)(2,1)} %collective-permute-done.8.other_ref), channel_id=1, source_target_pairs={{0,1},{1,0},{2,3},{3,2},{4,5},{5,4},{6,7},{7,6},{8,9},{9,8},{10,11... | collective-permute-start | bytes 1990664 | tf_op jit(solution)/shard_map/ppermute | solution.py:341
  115.6 3.5 %collective-permute-start.15 = (bf16[576,512]{1,0:T(8,128)(2,1)S(1)}, bf16[576,512]{1,0:T(8,128)(2,1)S(1)}, u32[]{:S(2)}, u32[]{:S(2)}) collective-permute-start(bf16[576,512]{1,0:T(8,128)(2,1)S(1)} %bitcast.23), channel_id=1, source_target_pairs={{0,1},{1,0},{2,3},{3,2},{4,5},{5,4},{6,7},{7,6},{8,9},{9,8},{10,11... | collective-permute-start | bytes 1769480 | tf_op jit(solution)/shard_map/ppermute | solution.py:341
  116.2 1.1 copy-start.3
